TPU v7x, 32 devices: a whole 2x2x4 slice. The times are simulated.
32 devices in a mesh: rows: 4 (over x, core), state: 8 (over z, y).
Axes of the slice: x: 2, y: 2, z: 4, core: 2. Of those that a mesh axis runs over, the one named last changes fastest.
Arguments:
- hidden_in: bfloat16 [16384, 2048], P('rows'), may hold values from -64 to 64
- starts: int32 [16384], P('rows'), may hold values 0 or 1
- cotangent: bfloat16 [16384, 2048], P('rows', 'state'), may hold values from -6 to 6
- norm_gain: float32 [2048], replicated, may hold values from 0.1 to 1.9
- w_zx: bfloat16 [2048, 2, 4096], P(None, None, 'state'), may hold values from -3 to 3
- w_dt: bfloat16 [2048, 64], P(None, 'state'), may hold values from -0.125 to 0.125
- w_bc: bfloat16 [2048, 2, 128], P(None, None, 'state'), may hold values from -0.125 to 0.125
- conv_x_w: float32 [4, 4096], P(None, 'state'), may hold values from -3 to 3
- conv_x_b: float32 [4096], P('state'), may hold values from -0.5 to 0.5
- conv_bc_w: float32 [4, 2, 128], P(None, None, 'state'), may hold values from -3 to 3
- conv_bc_b: float32 [2, 128], P(None, 'state'), may hold values from -0.5 to 0.5
- dt_bias: float32 [64], P('state'), may hold values from -7 to -1
- a_log: float32 [64], P('state'), may hold values from 0 to 2.7
- d_skip: float32 [64], P('state'), may hold values from 0.5 to 1.5
- gnorm_w: float32 [4096], P('state'), may hold values from 0.1 to 1.9
- w_out: bfloat16 [4096, 2048], P('state'), may hold values from -0.09375 to 0.09375
Outputs:
- output: bfloat16 [16384, 2048], P('rows', 'state')
- grad_input: float32 [16384, 2048], P('rows', 'state')
- grad_norm_gain: float32 [2048], P('state')
- grad_w_zx: float32 [2048, 2, 4096], P(None, None, 'state')
- grad_w_dt: float32 [2048, 64], P(None, 'state')
- grad_w_bc: float32 [2048, 2, 128], P(None, None, 'state')
- grad_conv_x_w: float32 [4, 4096], P(None, 'state')
- grad_conv_x_b: float32 [4096], P('state')
- grad_conv_bc_w: float32 [4, 2, 128], P(None, None, 'state')
- grad_conv_bc_b: float32 [2, 128], P(None, 'state')
- grad_dt_bias: float32 [64], P('state')
- grad_a_log: float32 [64], P('state')
- grad_d_skip: float32 [64], P('state')
- grad_gnorm_w: float32 [4096], P('state')
- grad_w_out: float32 [4096, 2048], P('state')
All inputs are finite; a program needn't handle non-finite values. No bound on the sum of `starts` on one device may be relied on, other than what follows from the above.
Results may differ from a plain program's by a relative error of at most 0.009.
Values may be sent and summed in bfloat16 or wider, within the bound.
No kernel may reach another device: no remote copies, remote signals or barrier semaphores. Data moves between devices by JAX's collectives and lax.ppermute only.
A program may use at most 384 MiB of HBM per device.

v0:
```python
import jax
import jax.numpy as jnp
from jax import lax
from jax.sharding import PartitionSpec as P

BLOCK = 256
LEN = 2048


HIGHEST = lax.Precision.HIGHEST
EPSILON = 1e-05


def causal_conv(values, kernel, offset, doc_ids):
    taps = kernel.shape[0]
    summed = offset + kernel[taps - 1] * values
    ones_tail = (1,) * (values.ndim - 2)
    for lag_steps in range(1, taps):
        lagged = jnp.concatenate(
            [jnp.zeros_like(values[:, :lag_steps]), values[:, :-lag_steps]], axis=1
        )
        lag_ids = jnp.concatenate(
            [jnp.full_like(doc_ids[:, :lag_steps], -1), doc_ids[:, :-lag_steps]], axis=1
        )
        same_doc = (lag_ids == doc_ids).astype(values.dtype).reshape(doc_ids.shape + ones_tail)
        summed = summed + kernel[taps - 1 - lag_steps] * lagged * same_doc
    return summed


def block_step(carry_state, block):
    inflow, log_rate, b_rows, c_rows, doc_ids, start_rows = block
    block_len = log_rate.shape[1]
    running = jnp.cumsum(log_rate, axis=1)
    places = jnp.arange(block_len)
    within = (doc_ids[:, :, None] == doc_ids[:, None, :]) & (places[:, None] >= places[None, :])[
        None
    ]
    within_mask = within.astype(log_rate.dtype)[..., None]
    gaps = running[:, :, None, :] - running[:, None, :, :]
    decays = jnp.exp(jnp.where(within[..., None], gaps, 0.0)) * within_mask
    intersection = jnp.einsum("sin,sjn->sij", c_rows, b_rows, precision=HIGHEST)
    mixing = decays * intersection[..., None]
    inside = jnp.einsum("sijh,sjhp->sihp", mixing, inflow, precision=HIGHEST)
    opened = (jnp.cumsum(start_rows, axis=1) == 0).astype(log_rate.dtype)
    leading = jnp.exp(running) * opened[..., None]
    carried = (
        jnp.einsum("sin,shnp->sihp", c_rows, carry_state, precision=HIGHEST) * leading[..., None]
    )
    trailing = (
        jnp.exp(running[:, -1:, :] - running)
        * (doc_ids == doc_ids[:, -1:]).astype(log_rate.dtype)[..., None]
    )
    gained = jnp.einsum("sjn,sjh,sjhp->shnp", b_rows, trailing, inflow, precision=HIGHEST)
    retain = jnp.exp(running[:, -1, :]) * opened[:, -1:]
    carry_state = carry_state * retain[:, :, None, None] + gained
    return (carry_state, inside + carried)


def state_space(
    xvals, dt_raw, dt_bias, a_log, b_rows, c_rows, d_skip, doc_ids, start_rows, seqs, block_len
):
    tok_count, head_count, head_dim = xvals.shape
    step_size = jax.nn.softplus(dt_raw + dt_bias)
    log_rate = -jnp.exp(a_log) * step_size
    inflow = xvals * step_size[..., None]
    blocks = tok_count // (seqs * block_len)

    def split(values):
        values = values.reshape((seqs, blocks, block_len) + values.shape[1:])
        return jnp.moveaxis(values, 1, 0)

    initial = jnp.zeros((seqs, head_count, b_rows.shape[1], head_dim), jnp.float32)
    final_state, pieces = lax.scan(
        jax.checkpoint(block_step),
        initial,
        (
            split(inflow),
            split(log_rate),
            split(b_rows),
            split(c_rows),
            split(doc_ids),
            split(start_rows),
        ),
    )
    pieces = jnp.moveaxis(pieces, 0, 1).reshape(tok_count, head_count, head_dim)
    return pieces + d_skip[:, None] * xvals


def shards(
    hidden_in,
    starts,
    cotangent,
    norm_gain,
    w_zx,
    w_dt,
    w_bc,
    conv_x_w,
    conv_x_b,
    conv_bc_w,
    conv_bc_b,
    dt_bias,
    a_log,
    d_skip,
    gnorm_w,
    w_out,
):
    tok_count, model_dim = hidden_in.shape
    seq_count = tok_count // LEN
    state_parts = lax.axis_size("state")
    local_dim = cotangent.shape[1]
    column_start = lax.axis_index("state") * local_dim
    inner_local = w_zx.shape[2]
    head_local = w_dt.shape[1]
    head_dim = inner_local // head_local
    inner_dim = inner_local * state_parts
    hidden = hidden_in.astype(jnp.float32)
    scale_rows = lax.rsqrt(jnp.mean(hidden * hidden, axis=-1, keepdims=True) + EPSILON)
    normed = (hidden * scale_rows * norm_gain).astype(jnp.bfloat16)
    gate_value = jnp.einsum("td,dkc->tkc", normed, w_zx, preferred_element_type=jnp.float32)
    dt_raw = jnp.dot(normed, w_dt, preferred_element_type=jnp.float32)
    state_proj = jnp.einsum("td,dkn->tkn", normed, w_bc, preferred_element_type=jnp.float32)
    start_rows = starts.reshape(seq_count, LEN)
    doc_ids = jnp.cumsum(start_rows, axis=1)

    def conv_apply(pre_values, kernel, offset):
        return jax.nn.silu(causal_conv(pre_values, kernel, offset, doc_ids))

    mixer_pre = gate_value[:, 1].reshape(seq_count, LEN, inner_local)
    mixed_x, conv_x_pull = jax.vjp(conv_apply, mixer_pre, conv_x_w, conv_x_b)
    mixed_low = (
        mixed_x.astype(jnp.bfloat16).astype(jnp.float32).reshape(tok_count, head_local, head_dim)
    )
    state_pre = state_proj.reshape(seq_count, LEN, 2, -1)
    state_local, conv_bc_pull = jax.vjp(conv_apply, state_pre, conv_bc_w, conv_bc_b)
    state_all = lax.all_gather(
        state_local.astype(jnp.bfloat16).reshape(tok_count, 2, -1), "state", axis=2, tiled=True
    )
    state_full = state_all.astype(jnp.float32)

    def scan_heads(xvals, raw_steps, bias_steps, log_decay, b_rows, c_rows, skip_weight):
        return state_space(
            xvals,
            raw_steps,
            bias_steps,
            log_decay,
            b_rows,
            c_rows,
            skip_weight,
            doc_ids.reshape(-1),
            starts,
            seq_count,
            BLOCK,
        )

    scanned, scan_pull = jax.vjp(
        scan_heads, mixed_low, dt_raw, dt_bias, a_log, state_full[:, 0], state_full[:, 1], d_skip
    )
    scanned = scanned.reshape(tok_count, inner_local)
    gate_lane = gate_value[:, 0]
    gate_sigmoid = jax.nn.sigmoid(gate_lane)
    gate_act = gate_lane * gate_sigmoid
    gated = scanned * gate_act
    power_sum = lax.psum(jnp.sum(gated * gated, axis=-1), "state")
    gate_scale = lax.rsqrt(power_sum / inner_dim + EPSILON)[:, None]
    normed_out = (gated * gate_scale * gnorm_w).astype(jnp.bfloat16)
    partial_out = jnp.dot(normed_out, w_out, preferred_element_type=jnp.float32)
    mixer_sum = lax.psum_scatter(partial_out, "state", scatter_dimension=1, tiled=True)
    hidden_local = lax.dynamic_slice_in_dim(hidden, column_start, local_dim, 1)
    output = (hidden_local + mixer_sum).astype(jnp.bfloat16)
    cot_full = lax.all_gather(cotangent, "state", axis=1, tiled=True)
    grad_w_out = jnp.einsum("ti,td->id", normed_out, cot_full, preferred_element_type=jnp.float32)
    d_normed_out = jnp.einsum("td,id->ti", cot_full, w_out, preferred_element_type=jnp.float32)
    grad_gnorm = jnp.sum(d_normed_out * gated * gate_scale, axis=0)
    weighted_gate = d_normed_out * gnorm_w
    slope_gate = lax.psum(jnp.sum(weighted_gate * gated, axis=-1), "state")
    grad_gated = gate_scale * (
        weighted_gate - gated * gate_scale * gate_scale * (slope_gate / inner_dim)[:, None]
    )
    grad_scanned = grad_gated * gate_act
    grad_gate = grad_gated * scanned * gate_sigmoid * (1.0 + gate_lane * (1.0 - gate_sigmoid))
    grad_mixed, grad_steps, grad_dt_bias, grad_a_log, grad_bstate, grad_cstate, grad_d_skip = (
        scan_pull(grad_scanned.reshape(tok_count, head_local, head_dim))
    )
    grad_states = lax.psum_scatter(
        jnp.stack([grad_bstate, grad_cstate], axis=1), "state", scatter_dimension=2, tiled=True
    )
    grad_state_pre, grad_conv_bc_w, grad_conv_bc_b = conv_bc_pull(
        grad_states.reshape(seq_count, LEN, 2, -1)
    )
    grad_mixer_pre, grad_conv_x_w, grad_conv_x_b = conv_x_pull(
        grad_mixed.reshape(seq_count, LEN, inner_local)
    )
    grad_proj = jnp.stack(
        [grad_gate, grad_mixer_pre.reshape(tok_count, inner_local)], axis=1
    ).astype(jnp.bfloat16)
    grad_steps_low = grad_steps.astype(jnp.bfloat16)
    grad_state_low = grad_state_pre.reshape(tok_count, 2, -1).astype(jnp.bfloat16)
    grad_w_zx = jnp.einsum("td,tkc->dkc", normed, grad_proj, preferred_element_type=jnp.float32)
    grad_w_dt = jnp.einsum("td,th->dh", normed, grad_steps_low, preferred_element_type=jnp.float32)
    grad_w_bc = jnp.einsum(
        "td,tkn->dkn", normed, grad_state_low, preferred_element_type=jnp.float32
    )
    partial_in = (
        jnp.einsum("tkc,dkc->td", grad_proj, w_zx, preferred_element_type=jnp.float32)
        + jnp.einsum("th,dh->td", grad_steps_low, w_dt, preferred_element_type=jnp.float32)
        + jnp.einsum("tkn,dkn->td", grad_state_low, w_bc, preferred_element_type=jnp.float32)
    )
    cot_local = cotangent.astype(jnp.float32)
    grad_normed = lax.psum(partial_in, "state")
    gain_total = jnp.sum(grad_normed * hidden * scale_rows, axis=0)
    weighted_in = grad_normed * norm_gain
    grad_hidden = scale_rows * (
        weighted_in
        - hidden * scale_rows * scale_rows * jnp.mean(weighted_in * hidden, axis=-1, keepdims=True)
    )
    grad_input = cot_local + lax.dynamic_slice_in_dim(grad_hidden, column_start, local_dim, 1)
    grad_gain = lax.dynamic_slice_in_dim(gain_total, column_start, local_dim, 0)
    (
        grad_gain,
        grad_w_zx,
        grad_w_dt,
        grad_w_bc,
        grad_conv_x_w,
        grad_conv_x_b,
        grad_conv_bc_w,
        grad_conv_bc_b,
        grad_dt_bias,
        grad_a_log,
        grad_d_skip,
        grad_gnorm,
        grad_w_out,
    ) = lax.psum(
        (
            grad_gain,
            grad_w_zx,
            grad_w_dt,
            grad_w_bc,
            grad_conv_x_w,
            grad_conv_x_b,
            grad_conv_bc_w,
            grad_conv_bc_b,
            grad_dt_bias,
            grad_a_log,
            grad_d_skip,
            grad_gnorm,
            grad_w_out,
        ),
        "rows",
    )
    return (
        output,
        grad_input,
        grad_gain,
        grad_w_zx,
        grad_w_dt,
        grad_w_bc,
        grad_conv_x_w,
        grad_conv_x_b,
        grad_conv_bc_w,
        grad_conv_bc_b,
        grad_dt_bias,
        grad_a_log,
        grad_d_skip,
        grad_gnorm,
        grad_w_out,
    )


def solution(mesh):
    placed = (
        P("rows", None),
        P("rows"),
        P("rows", "state"),
        P(),
        P(None, None, "state"),
        P(None, "state"),
        P(None, None, "state"),
        P(None, "state"),
        P("state"),
        P(None, None, "state"),
        P(None, "state"),
        P("state"),
        P("state"),
        P("state"),
        P("state"),
        P("state", None),
    )
    return jax.shard_map(
        shards,
        mesh=mesh,
        in_specs=placed,
        out_specs=(
            P("rows", "state"),
            P("rows", "state"),
            P("state"),
            P(None, None, "state"),
            P(None, "state"),
            P(None, None, "state"),
            P(None, "state"),
            P("state"),
            P(None, None, "state"),
            P(None, "state"),
            P("state"),
            P("state"),
            P("state"),
            P("state"),
            P("state", None),
        ),
        check_vma=False,
    )
```

profile of v0, /device:TPU:0, one launch (start us, length us, event | category | flops | bytes accessed | tf_op | source)
XLA Modules:
  0.0 3278.1 jit_solution(8603749533427608358)
XLA Ops:
  16.4 19.0 convert_multiply_fusion
  46.9 22.3 fusion.104
  89.0 18.3 fusion.121
  116.4 16.0 copy.367
  162.7 12.9 reshape.646
  231.6 150.5 %while.39 = (s32[]{:T(128)}, f32[2,8,128,64]{2,3,1,0:T(8,128)S(1)}, f32[8,2,256,8,64]{2,4,3,1,0:T(8,128)}, f32[8,2,8,128,64]{3,4,2,1,0:T(8,128)}, f32[8,2,256,8]...) while((s32[]{:T(128)}, f32[2,8,128,64]{2,3,1,0:T(8,128)S(1)}, ...), condition=%wide.region_8.9_spmd.clone, body=%wide.region_3.8_spmd.clone.sunk | while | flops 1818376192 | bytes 12181119 | solution.py:73
  382.1 13.7 fusion.118
  395.8 12.7 copy.392
  408.5 14.2 reshape.643
  422.7 38.8 %psum.112 = f32[4096]{0:T(1024)S(1)} all-reduce(f32[4096]{0:T(1024)S(1)} %bitcast.588), channel_id=1, replica_groups=mesh['rows'=4,'state'=8] {'state'}, use_global_device_ids=true, to_apply=%region_10.11 | all-reduce | flops 4096 | bytes 32768 | tf_op jit(solution)/shard_map/psum | solution.py:163
  461.6 26.3 multiply_reduce_fusion.6
  487.9 33.0 %psum.113 = f32[4096]{0:T(1024)S(1)} all-reduce(f32[4096]{0:T(1024)S(1)} %get-tuple-element.745), channel_id=1, replica_groups=mesh['rows'=4,'state'=8] {'state'}, use_global_device_ids=true, to_apply=%region_13.14 | all-reduce | flops 4096 | bytes 32768 | tf_op jit(solution)/shard_map/psum | solution.py:175
  520.9 21.0 fusion.115
  569.5 631.6 %while.40 = (s32[]{:T(128)}, f32[2,8,128,64]{2,3,1,0:T(8,128)}, f32[8,2,256,8,64]{2,4,3,1,0:T(8,128)}, f32[8,2,256,8]{2,3,1,0:T(8,128)}, f32[8,2,256,128]{3,2,0,...) while((s32[]{:T(128)}, f32[2,8,128,64]{2,3,1,0:T(8,128)}, ...), condition=%wide.region_27.28_spmd.clone, body=%wide.region_14.27_spmd.clone.sunk | while | flops 4248233984 | bytes 41395800 | solution.py:73
  1201.1 13.4 copy.363
  1240.8 22.7 multiply_reduce_fusion.10
  1263.5 16.0 multiply_reduce_fusion.9
  1299.7 18.4 fusion.143
  1363.4 22.0 fusion.102
  1385.4 16.6 fusion.141
  1402.1 87.9 %all-reduce.34.cloned.1.call-done = f32[4096,2,128]{0,1,2:T(2,128)} async-done(((f32[4096,2,128]{0,1,2:T(2,128)}), f32[4096,2,128]{0,1,2:T(2,128)}) %all-reduce.34.cloned.1.call-update) | async-done | bytes 4194320
  1511.1 25.4 fusion.120
  1536.5 13.4 fusion.137
  1550.1 35.4 %bitcast_add_fusion = f32[4096,2048]{1,0:T(8,128)} fusion(f32[4096,2048]{1,0:T(8,128)} %fusion.137, f32[4096,2048,1]{1,0,2:T(8,128)} %fusion.120, bf16[4096,2,16]{0,2,1:T(8,128)(2,1)S(1)} %convert_element_type.136, bf16[2048,2,16]{0,2,1:T(8,128)(2,1)S(1)} %copy-done.19), kind=kOutput, calls=%fused_computation.143 | convolution fusion | flops 553648128 | bytes 101056512 | tf_op jit(solution)/shard_map/tkn,dkn->td/dot_general | solution.py:206
  1585.6 19.2 fusion.142
  1604.9 18.8 convert_element_type.122
  1624.0 113.2 %all-reduce.36.cloned.1.call-done = (f32[2048,2,512]{2,0,1:T(8,128)}, f32[2048,8]{0,1:T(8,128)}, f32[2048,2,16]{0,2,1:T(8,128)}, f32[512,2048]{1,0:T(8,128)}) async-done(((f32[2048,2,512]{2,0,1:T(8,128)}, f32[2048,8]{0,1:T(8,128)}, f32[2048,2,16]{0,2,1:T(8,128)}, f32[512,2048]{1,0:T(8,128)}), (f32[2048,2,512]{2,0,1:T(8,128)}, f32[2048,8]{0,1:T(8,128)}, f32[2048,2,16]{0,2,1:T(8,128)}, ...) | async-done | bytes 12910608 | tf_op jit(solution)/shard_map/psum | solution.py:232
  1737.2 15.4 copy.377
  1752.6 963.5 %all-reduce.32.cloned.1.call-done = f32[4096,2048]{1,0:T(8,128)} async-done(((f32[4096,2048]{1,0:T(8,128)}), f32[4096,2048]{1,0:T(8,128)}) %all-reduce.32.cloned.1.call-update) | async-done | bytes 33554448 | tf_op jit(solution)/shard_map/psum | solution.py:209
  2716.2 29.7 multiply_reduce_fusion.3
  2746.0 12.4 all-reduce.26
  2764.9 497.2 %reduce-scatter.2.cloned.1.call-done = f32[4096,256]{1,0:T(8,128)} async-done(((f32[4096,2048]{1,0:T(8,128)}), f32[4096,256]{1,0:T(8,128)}) %reduce-scatter.2.cloned.1.call-update) | async-done | bytes 4194320 | tf_op jit(solution)/shard_map/reduce_scatter | solution.py:167
  (1028 shorter events, 1070.9 us)
Async XLA Ops:
  7.2 454.4 %copy-start = (bf16[512,2048]{1,0:T(8,128)(2,1)S(1)}, bf16[512,2048]{1,0:T(8,128)(2,1)}, u32[]{:S(2)}) copy-start(bf16[512,2048]{1,0:T(8,128)(2,1)} %param.35) | copy-start | bytes 6291460
  7.2 208.9 %all-gather.3.cloned.1.call-start = ((), (), s32[]{:S(2)}) async-start(), calls=%async_computation.1 | async-start | bytes 2359296 | tf_op jit(solution)/shard_map/all_gather | solution.py:135
  41.5 27.8 copy-start.5
  41.7 47.3 %copy-start.21 = (f32[2,2048]{1,0:T(2,128)}, f32[2,2048]{1,0:T(2,128)S(1)}, u32[]{:S(2)}) copy-start(f32[2,2048]{1,0:T(2,128)S(1)} %get-tuple-element.873) | copy-start | bytes 49156
  41.7 47.3 %copy-start.23 = (f32[2,2048]{1,0:T(2,128)}, f32[2,2048]{1,0:T(2,128)S(1)}, u32[]{:S(2)}) copy-start(f32[2,2048]{1,0:T(2,128)S(1)} %get-tuple-element.874) | copy-start | bytes 49156
  41.7 47.3 %copy-start.25 = (f32[2,2048]{1,0:T(2,128)}, f32[2,2048]{1,0:T(2,128)S(1)}, u32[]{:S(2)}) copy-start(f32[2,2048]{1,0:T(2,128)S(1)} %get-tuple-element.875) | copy-start | bytes 49156
  45.8 415.7 %all-gather.5.cloned.1.call-start = ((), (), s32[]{:S(2)}) async-start(), calls=%async_computation.3 | async-start | bytes 18874368 | tf_op jit(solution)/shard_map/all_gather | solution.py:170
  46.6 1443.5 %all-reduce.34.cloned.1.call-start = ((), (), s32[]{:S(2)}) async-start(), calls=%async_computation.5 | async-start | bytes 8388608
  116.4 27.1 slice-start
  116.4 27.1 slice-start.1
  186.8 334.1 %copy-start.38 = (f32[512]{0:T(512)}, f32[512]{0:T(512)S(1)}, u32[]{:S(2)}) copy-start(f32[512]{0:T(512)S(1)} %mul.927) | copy-start | bytes 6148
  408.5 53.1 %copy-start.70 = (f32[512]{0:T(512)S(1)}, f32[512]{0:T(512)}, u32[]{:S(2)}) copy-start(f32[512]{0:T(512)} %param.34) | copy-start | bytes 6148
  461.5 59.4 %copy-start.32 = (f32[4096]{0:T(1024)}, f32[4096]{0:T(1024)S(1)}, u32[]{:S(2)}) copy-start(f32[4096]{0:T(1024)S(1)} %add_rsqrt_fusion) | copy-start | bytes 49156
  617.9 26.8 copy-start.13
  776.0 26.8 copy-start.13
  1171.0 26.8 copy-start.13
  1336.3 400.9 %all-reduce.36.cloned.1.call-start = ((), (), s32[]{:S(2)}) async-start(), calls=%async_computation.6 | async-start | bytes 25821184 | tf_op jit(solution)/shard_map/psum | solution.py:232
  1385.4 108.2 %copy-start.6 = (f32[2,2048,2,16]{1,0,3,2:T(2,128)S(1)}, f32[2,2048,2,16]{1,0,3,2:T(2,128)}, u32[]{:S(2)}) copy-start(f32[2,2048,2,16]{1,0,3,2:T(2,128)} %copy-done.5) | copy-start | bytes 1572868
  1385.4 112.5 %copy-start.55 = (f32[2,16]{1,0:T(2,128)S(1)}, f32[2,16]{1,0:T(2,128)}, u32[]{:S(2)}) copy-start(f32[2,16]{1,0:T(2,128)} %copy-done.54) | copy-start | bytes 388
  1402.0 96.6 %copy-start.53 = (f32[2,16]{1,0:T(2,128)S(1)}, f32[2,16]{1,0:T(2,128)}, u32[]{:S(2)}) copy-start(f32[2,16]{1,0:T(2,128)} %copy-done.52) | copy-start | bytes 388
  1402.1 97.3 %copy-start.51 = (f32[2,16]{1,0:T(2,128)S(1)}, f32[2,16]{1,0:T(2,128)}, u32[]{:S(2)}) copy-start(f32[2,16]{1,0:T(2,128)} %copy-done.50) | copy-start | bytes 388
  1402.1 98.0 %copy-start.49 = (f32[2,16]{1,0:T(2,128)S(1)}, f32[2,16]{1,0:T(2,128)}, u32[]{:S(2)}) copy-start(f32[2,16]{1,0:T(2,128)} %copy-done.48) | copy-start | bytes 388
  1511.0 1205.1 %all-reduce.32.cloned.1.call-start = ((), (), s32[]{:S(2)}) async-start(), calls=%async_computation.4 | async-start | bytes 67108864 | tf_op jit(solution)/shard_map/psum | solution.py:209
  1585.5 1676.6 %reduce-scatter.2.cloned.1.call-start = ((), (), s32[]{:S(2)}) async-start(), calls=%async_computation.2 | async-start | bytes 37748736 | tf_op jit(solution)/shard_map/reduce_scatter | solution.py:167
  1737.2 978.9 %copy-start.29 = (f32[4096]{0:T(1024)S(1)}, f32[4096]{0:T(1024)}, u32[]{:S(2)}) copy-start(f32[4096]{0:T(1024)} %copy-done.28) | copy-start | bytes 49156
  1737.2 978.9 %copy-start.37 = (f32[2048]{0:T(1024)S(1)}, f32[2048]{0:T(1024)}, u32[]{:S(2)}) copy-start(f32[2048]{0:T(1024)} %param.23) | copy-start | bytes 24580
  1752.6 993.4 %copy-start.59 = (f32[512]{0:T(512)S(1)}, f32[512]{0:T(512)}, u32[]{:S(2)}) copy-start(f32[512]{0:T(512)} %get-tuple-element.748) | copy-start | bytes 6148
  1752.6 993.4 %copy-start.66 = (f32[2,16]{1,0:T(2,128)S(1)}, f32[2,16]{1,0:T(2,128)}, u32[]{:S(2)}) copy-start(f32[2,16]{1,0:T(2,128)} %get-tuple-element.750) | copy-start | bytes 388
  1752.6 993.4 %copy-start.72 = (f32[512]{0:T(512)S(1)}, f32[512]{0:T(512)}, u32[]{:S(2)}) copy-start(f32[512]{0:T(512)} %get-tuple-element.744) | copy-start | bytes 6148
  1752.6 993.4 %copy-start.73 = (f32[8]{0:T(128)S(1)}, f32[8]{0:T(128)}, u32[]{:S(2)}) copy-start(f32[8]{0:T(128)} %get-tuple-element.821) | copy-start | bytes 100
  2764.9 502.6 %copy-start.34 = (f32[2048,8]{0,1:T(8,128)S(1)}, f32[2048,8]{0,1:T(8,128)}, u32[]{:S(2)}) copy-start(f32[2048,8]{0,1:T(8,128)} %get-tuple-element.1196) | copy-start | bytes 196612
  2764.9 503.2 %copy-start.27 = (f32[2048,2,16]{0,2,1:T(8,128)S(1)}, f32[2048,2,16]{0,2,1:T(8,128)}, u32[]{:S(2)}) copy-start(f32[2048,2,16]{0,2,1:T(8,128)} %get-tuple-element.1197) | copy-start | bytes 786436
  (126 other events, 1260.9 us)
Sparse Core Ops, SparseCore 0:
  45.9 51.9 all-gather.2
  100.0 226.2 all-gather.4
  1336.4 153.5 all-reduce.33
  1511.1 226.0 all-reduce.35
  1741.9 974.2 all-reduce.31
  2720.3 541.7 reduce-scatter.1
where the time goes:
time: 3300 us; the launch traced here: 3280 us
  waiting for transfers between devices  1660 us (50%)
  matrix products  602 us (18%)
  local copies, waits for them, and re-layouts  478 us (14%)
  other arithmetic  433 us (13%)
  blocking collectives  84.2 us (3%)
    psum x1, waiting for transfers between devices, shards(): grad_normed = lax.psum(partial_in, 'state')  964 us
    reduce_scatter x1, waiting for transfers between devices, shards(): lax.psum_scatter(partial_out, 'state', scatter_dimension=1, tiled=True)  497 us
    dot_general x24, matrix products, block_step(): inside = jnp.einsum('sijh,sjhp->sihp', mixing, inflow, precision=HIGHEST)  171 us
    another operation x91, other arithmetic  117 us
    psum x1, waiting for transfers between devices, shards(): lax.psum((grad_gain, grad_w_zx, grad_w_dt, grad_w_bc, grad_conv_x_w, grad...  113 us
    unnamed x7, waiting for transfers between devices  88.7 us
    squeeze x56, local copies, waits for them, and re-layouts, state_space(): lax.scan(jax.checkpoint(block_step), initial, (split(inflow), split(log_r...  77.6 us
    dot_general x24, matrix products, block_step(): jnp.einsum('sjn,sjh,sjhp->shnp', b_rows, trailing, inflow, precision=HIGH...  72.3 us
  transfers between devices with their start and end apart: 6, of which 4 were waited for; matrix products, arithmetic and copies ran while one was open for 18% of the time, Pallas kernels for 0%

commit v1 on v0

v1 whole, which is shorter than its diff:
```python
import functools

import jax
import jax.numpy as jnp
from jax import lax
from jax.experimental import pallas as pl
from jax.experimental.pallas import tpu as pltpu
from jax.sharding import PartitionSpec as P

LEN = 2048
BLK = 256
NBLK = LEN // BLK
CHUNKS = 4
CT = LEN // CHUNKS
CB = CT // BLK
HD = 64
NS = 128
EPSILON = 1e-05
HIGHEST = lax.Precision.HIGHEST
f32 = jnp.float32
bf16 = jnp.bfloat16
VMEM_LIMIT = 56 * 1024 * 1024


def nn(a, b, **kw):
    return lax.dot_general(a, b, (((1,), (0,)), ((), ())), preferred_element_type=f32, **kw)


def nt(a, b):
    return lax.dot_general(a, b, (((1,), (1,)), ((), ())), preferred_element_type=f32)


def tn(a, b):
    return lax.dot_general(a, b, (((0,), (0,)), ((), ())), preferred_element_type=f32)


def iota(shape, dim):
    return lax.broadcasted_iota(jnp.int32, shape, dim)


def sigmoid(v):
    return 1.0 / (1.0 + jnp.exp(-v))


def fold(v):
    return v.reshape(v.shape[0] // 8, 8, v.shape[1]).sum(axis=0)


def expand(cols, off, heads):
    low = iota((cols.shape[0], 128), 1) < HD
    pieces = []
    for p in range(heads // 2):
        a = cols[:, off + 2 * p : off + 2 * p + 1]
        b = cols[:, off + 2 * p + 1 : off + 2 * p + 2]
        pieces.append(jnp.where(low, a, b))
    return jnp.concatenate(pieces, axis=1)


def quad_masks(rows):
    head = iota((rows, 4 * HD), 1) // HD
    return [head == h for h in range(4)]


def stacked(v, masks):
    zero = jnp.zeros_like(v)
    return jnp.concatenate([jnp.where(m, v, zero) for m in masks], axis=0)


def segment_sums(v, off):
    n = v.shape[1]
    pick = (iota((n, 128), 1) == iota((n, 128), 0) // HD + off).astype(bf16)
    high = v.astype(bf16)
    rest = (v - high.astype(f32)).astype(bf16)
    return nn(high, pick) + nn(rest, pick)


def conv_tile(step, x1, kern, msk, buf):
    @pl.when(step == 0)
    def _():
        buf[0:8, :] = jnp.zeros((8, buf.shape[1]), f32)

    buf[8 : 8 + BLK, :] = x1
    acc = kern[4:5, :] + kern[3:4, :] * x1
    for k in range(1, 4):
        acc = acc + kern[3 - k : 4 - k, :] * (buf[8 - k : 8 - k + BLK, :] * msk[:, k : k + 1])
    buf[0:8, :] = x1[BLK - 8 :, :]
    return acc


def project_tile(n, w, kern, msk, z, xp, a, xs, buf):
    lanes = w.shape[1] // 2
    p = nn(n, w[...])
    z[...] = p[:, :lanes]
    x1 = p[:, lanes:]
    xp[...] = x1
    acc = conv_tile(pl.program_id(0), x1, kern, msk, buf)
    a[...] = acc
    xs[...] = (acc * sigmoid(acc)).astype(bf16)


def first_kernel(which, hid, gain, w, kern, msk, normed, r, z, xp, a, xs, buf):
    x = hid[...].astype(f32)
    rr = lax.rsqrt(jnp.mean(x * x, axis=1, keepdims=True) + EPSILON)
    n = (x * rr * gain[...]).astype(bf16)
    normed[...] = n
    r[...] = jnp.broadcast_to(rr, (BLK, 128))
    project_tile(n, w, kern, msk, z, xp, a, xs, buf)


def second_kernel(normed, w, kern, msk, z, xp, a, xs, buf):
    project_tile(normed[...], w, kern, msk, z, xp, a, xs, buf)


def states_kernel(docl, normed, ws, kern, dtp, msk, bcp, bca, bc, dtr, dt, cum, cumt, buf):
    q = nt(normed[...], ws[...])
    x1 = q[:, : 2 * NS]
    bcp[...] = x1
    acc = conv_tile(pl.program_id(0), x1, kern, msk, buf)
    bca[...] = acc
    bc[...] = (acc * sigmoid(acc)).astype(bf16)
    d = q[:, 2 * NS :]
    dtr[...] = d
    v = d + dtp[0:1, :]
    e = jnp.exp(-jnp.abs(v))
    small = e * (1.0 - e * (0.5 - e * (1.0 / 3.0 - 0.25 * e)))
    step = jnp.maximum(v, 0.0) + jnp.where(e < 0.01, small, jnp.log(1.0 + e))
    lane = iota((BLK, 128), 1)
    step = jnp.where(lane < docl, step, 0.0)
    dt[...] = step
    ext = jnp.where(lane == docl, msk[:, 0:1], step * dtp[1:2, :])
    tri = (iota((BLK, BLK), 0) >= iota((BLK, BLK), 1)).astype(f32)
    c = nn(tri, ext, precision=HIGHEST)
    cum[...] = c
    cumt[...] = c.T


def block_scalars(docl, cum):
    lane = iota((BLK, 128), 1)
    doc = cum[:, docl : docl + 1]
    doc_last = cum[BLK - 1 : BLK, docl : docl + 1]
    rates = jnp.where(lane < docl, cum, 0.0)
    last = rates[BLK - 1 : BLK, :]
    lead = jnp.exp(rates) * (doc == 0.0).astype(f32)
    trail = jnp.exp(last - rates) * (doc == doc_last).astype(f32)
    retain = jnp.exp(last) * (doc_last == 0.0).astype(f32)
    return lead, trail, retain


def scan_kernel(docl, off, xs, z, bc, dt, cum, cumt, prm, y, gw, sin, pw, state):
    lanes = xs.shape[1]
    heads = lanes // HD

    @pl.when(pl.program_id(0) == 0)
    def _():
        state[...] = jnp.zeros_like(state)

    s_in = state[...]
    sin[0] = s_in
    b = bc[:, :NS]
    c = bc[:, NS:]
    cumv = cum[...]
    lead, trail, retain = block_scalars(docl, cumv)
    within = (cumv[:, docl : docl + 1] == cumt[docl : docl + 1, :]) & (
        iota((BLK, BLK), 0) >= iota((BLK, BLK), 1)
    )
    bias = jnp.where(within, 0.0, -1e30)
    g = nt(c, b)
    xf = xs[...].astype(f32)
    u = xf * expand(dt[...], off, heads)
    ub = u.astype(bf16)
    masks = quad_masks(BLK)
    parts = []
    for q in range(heads // 4):
        mixes = []
        for h in range(off + 4 * q, off + 4 * q + 4):
            decay = jnp.exp((cumv[:, h : h + 1] - cumt[h : h + 1, :]) + bias)
            mixes.append((decay * g).astype(bf16))
        uq = ub[:, q * 256 : q * 256 + 256]
        parts.append(nn(jnp.concatenate(mixes, axis=1), stacked(uq, masks)))
    yv = jnp.concatenate(parts, axis=1)
    yv = yv + nn(c, s_in.astype(bf16)) * expand(lead, off, heads) + prm[6:7, :] * xf
    y[...] = yv
    ut = (u * expand(trail, off, heads)).astype(bf16)
    state[...] = s_in * expand(retain, off, heads) + tn(b, ut)
    zz = z[...]
    gated = yv * zz * sigmoid(zz)
    gw[...] = (gated * prm[5:6, :]).astype(bf16)
    pw[...] = jnp.broadcast_to(jnp.sum(gated * gated, axis=1, keepdims=True), (BLK, 128))


def out_kernel(ga, gb, wa, wb, o):
    o[...] = (nn(ga[...], wa[...]) + nn(gb[...], wb[...])).astype(bf16)


def dyn_kernel(c, wa, wb, ga, gb, da, db, qs):
    cv = c[...]
    a = nt(cv, wa[...])
    b = nt(cv, wb[...])
    da[...] = a.astype(bf16)
    db[...] = b.astype(bf16)
    q = jnp.sum(a * ga[...].astype(f32), axis=1, keepdims=True)
    q = q + jnp.sum(b * gb[...].astype(f32), axis=1, keepdims=True)
    qs[...] = jnp.broadcast_to(q, (BLK, 128))


def gate_kernel(sq, da, db, ya, yb, za, zb, prma, prmb, dz, dy, yn, mt, gg):
    lanes = da.shape[1]
    s = sq[:, 0:1]
    kq = sq[:, 1:2]

    @pl.when(pl.program_id(0) == 0)
    def _():
        gg[...] = jnp.zeros_like(gg)

    total = jnp.zeros((BLK, 1), f32)
    for half, (dref, yref, zref, prm) in enumerate(((da, ya, za, prma), (db, yb, zb, prmb))):
        at = slice(half * lanes, half * lanes + lanes)
        dn = dref[...].astype(f32)
        y = yref[...]
        z = zref[...]
        gn = prm[5:6, :]
        sg = sigmoid(z)
        act = z * sg
        g = y * act
        gs = g * s
        yn[:, at] = (gs * gn).astype(bf16)
        gg[:, at] += fold(dn * gs)
        dg = s * (dn * gn) - g * kq
        dy[:, at] = (dg * act).astype(bf16)
        low = (dg * y * (sg * (1.0 + z * (1.0 - sg)))).astype(bf16)
        dz[:, at] = low
        total = total + jnp.sum(low.astype(f32) * z, axis=1, keepdims=True)
    mt[...] = jnp.broadcast_to(total, (BLK, 128))


def conv_back(da, xp, kern, buf, mbuf):
    dx = kern[3:4, :] * da
    taps = [None, None, None, fold(xp * da)]
    for k in range(1, 4):
        sh = buf[k : k + BLK, :] * mbuf[k : k + BLK, k : k + 1]
        dx = dx + kern[3 - k : 4 - k, :] * sh
        taps[3 - k] = fold(xp * sh)
    return dx, taps


def back_kernel(
    docl,
    dy, bc, dt, cum, cumt, dtr, msk, dtp,
    ya, yb, xsa, xsb, aa, ab, xpa, xpb, sia, sib, prma, prmb,
    ds_in, cda_in, cm_in,
    dxp, ddt, dbc, mt, acc, accs, ds, cda, cm,
    buf, mbuf,
):
    lanes = xsa.shape[1]
    heads = lanes // HD
    step = pl.program_id(0)

    @pl.when(step == 0)
    def _():
        ds[...] = ds_in[...]
        buf[:, 0:8, :] = cda_in[...]
        mbuf[0:8, :] = cm_in[...]
        acc[...] = jnp.zeros_like(acc)
        accs[...] = jnp.zeros_like(accs)

    mbuf[BLK : BLK + 8, :] = mbuf[0:8, :]
    mbuf[0:BLK, :] = msk[...]
    b = bc[:, :NS]
    c = bc[:, NS:]
    cumv = cum[...]
    lead, trail, retain = block_scalars(docl, cumv)
    within = (cumv[:, docl : docl + 1] == cumt[docl : docl + 1, :]) & (
        iota((BLK, BLK), 0) <= iota((BLK, BLK), 1)
    )
    bias = jnp.where(within, 0.0, -1e30)
    gt = nt(b, c)
    masks = quad_masks(BLK)
    dgt = jnp.zeros((BLK, BLK), f32)
    d_c = jnp.zeros((BLK, NS), f32)
    d_b = jnp.zeros((BLK, NS), f32)
    r1 = jnp.zeros((BLK, 128), f32)
    r2 = jnp.zeros((BLK, 128), f32)
    r3 = jnp.zeros((BLK, 128), f32)
    held = jnp.zeros((8, 128), f32)
    total = jnp.zeros((BLK, 1), f32)
    refs = ((ya, xsa, aa, xpa, sia, prma), (yb, xsb, ab, xpb, sib, prmb))
    for half, (yr, xsr, ar, xpr, sir, prm) in enumerate(refs):
        off = half * heads
        at = slice(half * lanes, half * lanes + lanes)
        dyb = dy[:, at]
        dyf = dyb.astype(f32)
        skip = prm[6:7, :]
        xf = xsr[...].astype(f32)
        dte = expand(dt[...], off, heads)
        u = xf * dte
        ub = u.astype(bf16)
        ubf = ub.astype(f32)
        s_in = sir[0]
        d_state = ds[half]
        dsb = d_state.astype(bf16)
        te = expand(trail, off, heads)
        tb = te * nn(b, dsb)
        parts = []
        for q in range(heads // 4):
            uq = ub[:, q * 256 : q * 256 + 256]
            dq = dyb[:, q * 256 : q * 256 + 256]
            dmt = nt(stacked(uq, masks), dq)
            mixes = []
            for i in range(4):
                h = off + 4 * q + i
                decay = jnp.exp((cumt[h : h + 1, :] - cumv[:, h : h + 1]) + bias)
                mixes.append((decay * gt).astype(bf16))
                dgt = dgt + dmt[i * BLK : i * BLK + BLK, :] * decay
            parts.append(nn(jnp.concatenate(mixes, axis=1), stacked(dq, masks)))
        du = jnp.concatenate(parts, axis=1) + tb
        ldy = (expand(lead, off, heads) * dyf).astype(bf16)
        d_c = d_c + nt(ldy, s_in.astype(bf16))
        d_b = d_b + nt((te * u).astype(bf16), dsb)
        ds[half] = d_state * expand(retain, off, heads) + tn(c, ldy)
        r1 = r1 + segment_sums(dyf * (yr[...] - skip * xf) - ubf * du, off)
        r2 = r2 + segment_sums(ubf * tb, off)
        r3 = r3 + segment_sums(xf * du, off)
        held = held + segment_sums(fold(d_state * s_in), off)
        a = ar[...]
        sa = sigmoid(a)
        da = (dte * du + skip * dyf) * (sa * (1.0 + a * (1.0 - sa)))
        buf[half, BLK : BLK + 8, :] = buf[half, 0:8, :]
        buf[half, 0:BLK, :] = da
        xp = xpr[...]
        dx, taps = conv_back(da, xp, prm, buf.at[half], mbuf)
        low = dx.astype(bf16)
        dxp[:, at] = low
        total = total + jnp.sum(low.astype(f32) * xp, axis=1, keepdims=True)
        for k in range(4):
            acc[half, 8 * k : 8 * k + 8, :] += taps[k]
        acc[half, 32:40, :] += fold(da)
        acc[half, 40:48, :] += fold(dyf * xf)
    dgb = dgt.astype(bf16)
    dbc[:, :NS] = (d_b + nn(dgb, c)).astype(bf16)
    dbc[:, NS:] = (d_c + tn(dgb, b)).astype(bf16)
    at_last = jnp.sum(r2, axis=0, keepdims=True) + retain * jnp.sum(held, axis=0, keepdims=True)
    dcum = r1 + jnp.where(iota((BLK, 128), 0) == BLK - 1, at_last, 0.0)
    later = (iota((BLK, BLK), 1) >= iota((BLK, BLK), 0)).astype(f32)
    drate = nn(later, dcum, precision=HIGHEST)
    rate = dtp[1:2, :]
    lane = iota((BLK, 128), 1)
    draw = jnp.where(lane < docl, (r3 + rate * drate) * sigmoid(dtr[...] + dtp[0:1, :]), 0.0)
    low = draw.astype(bf16)
    ddt[...] = low
    accs[0:8, :] += fold(drate * dt[...]) * rate
    accs[8:16, :] += fold(draw)
    total = total + jnp.sum(low.astype(f32) * dtr[...], axis=1, keepdims=True)
    mt[...] = jnp.broadcast_to(total, (BLK, 128))
    cda[...] = buf[:, 0:8, :]
    cm[...] = mbuf[0:8, :]


def states_back_kernel(dbc, bca, bcp, msk, kern, cda_in, cm_in, dsp, mt, acc, cda, cm, buf, mbuf):
    @pl.when(pl.program_id(0) == 0)
    def _():
        buf[0:8, :] = cda_in[...]
        mbuf[0:8, :] = cm_in[...]
        acc[...] = jnp.zeros_like(acc)

    mbuf[BLK : BLK + 8, :] = mbuf[0:8, :]
    mbuf[0:BLK, :] = msk[...]
    a = bca[...]
    sa = sigmoid(a)
    da = dbc[...] * (sa * (1.0 + a * (1.0 - sa)))
    buf[BLK : BLK + 8, :] = buf[0:8, :]
    buf[0:BLK, :] = da
    xp = bcp[...]
    dx, taps = conv_back(da, xp, kern, buf, mbuf)
    low = dx.astype(bf16)
    dsp[...] = low
    mt[...] = jnp.broadcast_to(jnp.sum(low.astype(f32) * xp, axis=1, keepdims=True), (BLK, 128))
    for k in range(4):
        acc[8 * k : 8 * k + 8, :] += taps[k]
    acc[32:40, :] += fold(da)
    cda[...] = buf[0:8, :]
    cm[...] = mbuf[0:8, :]


def dn_kernel(dz, dxp, ddt, wa, wb, wdt, o):
    n = wa.shape[1] // 2
    v = nt(dz[:, :n], wa[:, :n]) + nt(dxp[:, :n], wa[:, n:])
    v = v + nt(dz[:, n:], wb[:, :n]) + nt(dxp[:, n:], wb[:, n:])
    o[...] = (v + nt(ddt[...], wdt[...])).astype(bf16)


def tile(width, first=0):
    return pl.BlockSpec((BLK, width), lambda i, *_: (first + i, 0))


def back_tile(width, last):
    return pl.BlockSpec((BLK, width), lambda i, *_: (last - i, 0))


def whole(*shape):
    zeros = (0,) * len(shape)
    return pl.BlockSpec(shape, lambda i, *_: zeros)


def sds(shape, dtype):
    return jax.ShapeDtypeStruct(shape, dtype)


def call(kernel, grid, in_specs, out_specs, out_shape, scratch=(), flops=0, moved=0, prefetch=0):
    return pl.pallas_call(
        kernel,
        grid_spec=pltpu.PrefetchScalarGridSpec(
            num_scalar_prefetch=prefetch,
            grid=(grid,),
            in_specs=in_specs,
            out_specs=out_specs,
            scratch_shapes=list(scratch),
        ),
        out_shape=out_shape,
        compiler_params=pltpu.CompilerParams(
            dimension_semantics=("arbitrary",), vmem_limit_bytes=VMEM_LIMIT
        ),
        cost_estimate=pl.CostEstimate(flops=flops, bytes_accessed=moved, transcendentals=0),
    )


def shards(
    hidden_in, starts, cotangent, norm_gain, w_zx, w_dt, w_bc, conv_x_w, conv_x_b,
    conv_bc_w, conv_bc_b, dt_bias, a_log, d_skip, gnorm_w, w_out,
):
    parts = lax.axis_size("state")
    nrows = lax.axis_size("rows")
    groups = parts // 2
    me = lax.axis_index("state")
    mine = me % 2
    zpos = me // 2
    core = lax.axis_index("rows") % 2
    dim = hidden_in.shape[1]
    local_dim = cotangent.shape[1]
    lanes = w_zx.shape[2]
    heads = w_dt.shape[1]
    inner = lanes * parts
    docl = 2 * heads
    wide = dim // groups

    pair = [(i, i ^ 1) for i in range(parts)]

    def swap(v):
        return lax.ppermute(v, "state", pair)

    def cross(v, bit):
        return lax.ppermute(v, "rows", [(i, i ^ bit) for i in range(nrows)])

    def line_sum(v):
        bit = 2
        while bit < parts:
            v = v + lax.ppermute(v, "state", [(i, i ^ bit) for i in range(parts)])
            bit *= 2
        return v

    def rows_of(v, start, size):
        return lax.dynamic_slice_in_dim(v, start, size, 0)

    def fetch(own):
        half = own.shape[0] // 2
        got = swap(rows_of(own, core * half, half))
        other = cross(got, 1)
        first = core == 0
        return jnp.concatenate([jnp.where(first, got, other), jnp.where(first, other, got)], axis=0)

    w_a = w_zx.reshape(dim, 2 * lanes)
    w_b = fetch(w_a)
    o_a = w_out
    o_b = fetch(w_out)
    small = jnp.stack([dt_bias, a_log, d_skip]).reshape(-1)
    prm_a = jnp.concatenate(
        [
            conv_x_w,
            conv_x_b[None],
            gnorm_w[None],
            jnp.repeat(d_skip, HD)[None],
            jnp.pad(small, (0, lanes - small.shape[0]))[None],
        ],
        axis=0,
    )
    prm_b = swap(prm_a)
    small_b = prm_b[7, : 3 * heads].reshape(3, heads)
    wdt_a = w_dt.T
    wdt_b = swap(wdt_a)
    bias_all = jnp.concatenate([dt_bias, small_b[0]])
    rate_all = -jnp.exp(jnp.concatenate([a_log, small_b[1]]))
    dtp = jnp.pad(jnp.stack([bias_all, rate_all]), ((0, 6), (0, 128 - docl)))
    wbc = lax.all_gather(w_bc.transpose(1, 2, 0), "state", axis=1, tiled=True)
    wbc = wbc.reshape(2 * NS, dim)
    wdt = jnp.concatenate([wdt_a, wdt_b, jnp.zeros((128 - docl, dim), bf16)], axis=0)
    wst = jnp.concatenate([wbc, wdt], axis=0)
    kern_bc = jnp.concatenate([conv_bc_w, conv_bc_b[None]], axis=0)
    kern_bc = lax.all_gather(kern_bc, "state", axis=2, tiled=True).reshape(5, 2 * NS)
    kern_bc = jnp.pad(kern_bc, ((0, 3), (0, 0)))

    st = rows_of(starts, mine * LEN, LEN).astype(f32)
    open1 = jnp.where(jnp.arange(LEN) == 0, 0.0, 1.0 - st)
    open2 = open1 * jnp.concatenate([jnp.zeros((1,), f32), open1[:-1]])
    open3 = open2 * jnp.concatenate([jnp.zeros((2,), f32), open1[:-2]])
    msk = jnp.pad(jnp.stack([st, open1, open2, open3], axis=1), ((0, 0), (0, 124)))
    which = mine.astype(jnp.int32).reshape(1)

    tl = (BLK, lanes)
    proj_out = [tile(lanes), tile(lanes), tile(lanes), tile(lanes)]
    proj_shape = [sds((LEN, lanes), f32)] * 3 + [sds((LEN, lanes), bf16)]
    pf = 2 * LEN * dim * 2 * lanes
    normed, r_wide, z_a, xp_a, a_a, xs_a = call(
        first_kernel,
        NBLK,
        [
            pl.BlockSpec((BLK, dim), lambda i, which: (which[0] * NBLK + i, 0)),
            whole(1, dim),
            whole(dim, 2 * lanes),
            whole(8, lanes),
            tile(128),
        ],
        [tile(dim), tile(128)] + proj_out,
        [sds((LEN, dim), bf16), sds((LEN, 128), f32)] + proj_shape,
        [pltpu.VMEM((BLK + 8, lanes), f32)],
        flops=pf,
        moved=40 << 20,
        prefetch=1,
    )(which, hidden_in, norm_gain.reshape(1, dim), w_a, prm_a, msk)
    bcp, bca, bc, dtr, dt, cum, cumt = call(
        functools.partial(states_kernel, docl),
        NBLK,
        [tile(dim), whole(2 * NS + 128, dim), whole(8, 2 * NS), whole(8, 128), tile(128)],
        [tile(2 * NS)] * 3 + [tile(128)] * 3 + [pl.BlockSpec((128, BLK), lambda i: (0, i))],
        [sds((LEN, 2 * NS), f32)] * 2
        + [sds((LEN, 2 * NS), bf16)]
        + [sds((LEN, 128), f32)] * 3
        + [sds((128, LEN), f32)],
        [pltpu.VMEM((BLK + 8, 2 * NS), f32)],
        flops=2 * LEN * dim * 512,
        moved=18 << 20,
    )(normed, wst, kern_bc, dtp, msk)

    def scan(off, xs, z, prm):
        return call(
            functools.partial(scan_kernel, docl, off),
            NBLK,
            [
                tile(lanes), tile(lanes), tile(2 * NS), tile(128), tile(128),
                pl.BlockSpec((128, BLK), lambda i: (0, i)), whole(8, lanes),
            ],
            [tile(lanes), tile(lanes), pl.BlockSpec((1, NS, lanes), lambda i: (i, 0, 0)), tile(128)],
            [
                sds((LEN, lanes), f32),
                sds((LEN, lanes), bf16),
                sds((NBLK, NS, lanes), f32),
                sds((LEN, 128), f32),
            ],
            [pltpu.VMEM((NS, lanes), f32)],
            flops=10 << 30,
            moved=20 << 20,
        )(xs, z, bc, dt, cum, cumt, prm)

    y_a, gw_a, sin_a, pw_a = scan(0, xs_a, z_a, prm_a)
    z_b, xp_b, a_b, xs_b = call(
        second_kernel,
        NBLK,
        [tile(dim), whole(dim, 2 * lanes), whole(8, lanes), tile(128)],
        proj_out,
        proj_shape,
        [pltpu.VMEM((BLK + 8, lanes), f32)],
        flops=pf,
        moved=28 << 20,
    )(normed, w_b, prm_b, msk)
    y_b, gw_b, sin_b, pw_b = scan(heads, xs_b, z_b, prm_b)

    c_mine = rows_of(cotangent, mine * LEN, LEN)
    c_got = swap(rows_of(cotangent, (1 - mine) * LEN, LEN))
    is0 = mine == 0
    c_pair = jnp.concatenate([jnp.where(is0, c_mine, c_got), jnp.where(is0, c_got, c_mine)], axis=1)

    def right(k):
        return [(i, i + 2) for i in range(parts - 2) if i // 2 >= k - 1]

    def left(k):
        return [(i, i - 2) for i in range(2, parts) if i // 2 <= groups - k]

    def gather_line(v):
        up, down = {}, {}
        cur_u = cur_d = v
        for k in range(1, groups):
            cur_u = lax.ppermute(cur_u, "state", right(k))
            cur_d = lax.ppermute(cur_d, "state", left(k))
            up[k], down[k] = cur_u, cur_d
        pieces = [v]
        for k in range(1, groups):
            pieces.append(jnp.where(zpos >= k, up[k], down[groups - k]))
        return jnp.concatenate(pieces, axis=1)

    def relative(w):
        return jnp.concatenate(
            [
                lax.dynamic_slice_in_dim(w, (zpos + groups - k) % groups * wide, wide, 1)
                for k in range(groups)
            ],
            axis=1,
        )

    def scatter_line(v):
        def own(j):
            return lax.dynamic_slice_in_dim(v, jnp.clip(j, 0, groups - 1) * wide, wide, 1)

        up = down = None
        for d in range(groups - 1, 0, -1):
            send_u, send_d = own(zpos + d), own(zpos - d)
            if up is not None:
                send_u = (send_u.astype(f32) + up.astype(f32)).astype(bf16)
                send_d = (send_d.astype(f32) + down.astype(f32)).astype(bf16)
            up = lax.ppermute(
                send_u, "state", [(i, i + 2) for i in range(parts - 2) if i // 2 + d < groups]
            )
            down = lax.ppermute(
                send_d, "state", [(i, i - 2) for i in range(2, parts) if i // 2 - d >= 0]
            )
        return own(zpos).astype(f32) + up.astype(f32) + down.astype(f32)

    c_rel = [None] * CHUNKS
    for j in reversed(range(CHUNKS)):
        c_rel[j] = gather_line(c_pair[j * CT : (j + 1) * CT])
    or_a, or_b = relative(o_a), relative(o_b)

    partial_out = call(
        out_kernel,
        NBLK,
        [tile(lanes), tile(lanes), whole(lanes, dim), whole(lanes, dim)],
        tile(dim),
        sds((LEN, dim), bf16),
        flops=4 * LEN * lanes * dim,
        moved=14 << 20,
    )(gw_a, gw_b, o_a, o_b)
    mixer = scatter_line(partial_out)

    def dyn_call(j):
        return call(
            dyn_kernel,
            CB,
            [tile(dim), whole(lanes, dim), whole(lanes, dim), tile(lanes, j * CB), tile(lanes, j * CB)],
            [tile(lanes), tile(lanes), tile(128)],
            [sds((CT, lanes), bf16)] * 2 + [sds((CT, 128), f32)],
            flops=4 * CT * lanes * dim,
            moved=10 << 20,
        )(c_rel[j], or_a, or_b, gw_a, gw_b)

    power = pw_a[:, 0] + pw_b[:, 0]
    dz, dy, yn, mtg, ggs, scales = ([None] * CHUNKS for _ in range(6))
    for j in reversed(range(CHUNKS)):
        d_a, d_b, qs = dyn_call(j)
        sums = line_sum(jnp.concatenate([power[j * CT : (j + 1) * CT], qs[:, 0]]))
        s = lax.rsqrt(sums[:CT] / inner + EPSILON)
        kq = s * s * s * (sums[CT:] / inner)
        scales[j] = s
        sq = jnp.pad(jnp.stack([s, kq], axis=1), ((0, 0), (0, 126)))
        dz[j], dy[j], yn[j], mtg[j], gg = call(
            gate_kernel,
            CB,
            [tile(128)]
            + [tile(lanes)] * 2
            + [tile(lanes, j * CB)] * 4
            + [whole(8, lanes)] * 2,
            [tile(2 * lanes)] * 3 + [tile(128), whole(8, 2 * lanes)],
            [sds((CT, 2 * lanes), bf16)] * 3 + [sds((CT, 128), f32), sds((8, 2 * lanes), f32)],
            flops=100 * CT * lanes,
            moved=12 << 20,
        )(sq, d_a, d_b, y_a, y_b, z_a, z_b, prm_a, prm_b)
        ggs[j] = gg.sum(axis=0)

    wdt_t = wdt.T
    wbc_near = lax.dynamic_slice_in_dim(wbc, zpos * wide, wide, 1)
    ds = jnp.zeros((2, NS, lanes), f32)
    cda = jnp.zeros((2, 8, lanes), f32)
    cm = jnp.zeros((8, 128), f32)
    sda = jnp.zeros((8, 2 * NS), f32)
    scm = cm
    dxp, ddt, dsp, mts, near, far = ([None] * CHUNKS for _ in range(6))
    accs, accs_dt, accs_bc = [], [], []
    for j in reversed(range(CHUNKS)):
        last = j * CB + CB - 1

        def bt(width, last=last):
            return back_tile(width, last)

        def loc(width):
            return back_tile(width, CB - 1)

        cols = pl.BlockSpec((128, BLK), lambda i, last=last: (0, last - i))
        sins = pl.BlockSpec((1, NS, lanes), lambda i, last=last: (last - i, 0, 0))
        dxp[j], ddt[j], dbc, mtb, acc, acc_dt, ds, cda, cm = call(
            functools.partial(back_kernel, docl),
            CB,
            [
                loc(2 * lanes), bt(2 * NS), bt(128), bt(128), cols, bt(128), bt(128), whole(8, 128),
                bt(lanes), bt(lanes), bt(lanes), bt(lanes), bt(lanes), bt(lanes), bt(lanes), bt(lanes),
                sins, sins, whole(8, lanes), whole(8, lanes),
                whole(2, NS, lanes), whole(2, 8, lanes), whole(8, 128),
            ],
            [
                loc(2 * lanes), loc(128), loc(2 * NS), loc(128), whole(2, 48, lanes), whole(16, 128),
                whole(2, NS, lanes), whole(2, 8, lanes), whole(8, 128),
            ],
            [
                sds((CT, 2 * lanes), bf16), sds((CT, 128), bf16), sds((CT, 2 * NS), bf16),
                sds((CT, 128), f32), sds((2, 48, lanes), f32), sds((16, 128), f32),
                sds((2, NS, lanes), f32), sds((2, 8, lanes), f32), sds((8, 128), f32),
            ],
            [pltpu.VMEM((2, BLK + 8, lanes), f32), pltpu.VMEM((BLK + 8, 128), f32)],
            flops=24 << 30,
            moved=20 << 20,
        )(
            dy[j], bc, dt, cum, cumt, dtr, msk, dtp,
            y_a, y_b, xs_a, xs_b, a_a, a_b, xp_a, xp_b, sin_a, sin_b, prm_a, prm_b,
            ds, cda, cm,
        )
        accs.append(acc)
        accs_dt.append(acc_dt)

        whole_dbc = dbc
        bit = 2
        while bit < parts:
            got = lax.ppermute(
                whole_dbc.astype(bf16), "state", [(i, i ^ bit) for i in range(parts)]
            )
            whole_dbc = whole_dbc.astype(f32) + got.astype(f32)
            bit *= 2
        dsp[j], mtc, acc_bc, sda, scm = call(
            states_back_kernel,
            CB,
            [loc(2 * NS), bt(2 * NS), bt(2 * NS), bt(128), whole(8, 2 * NS), whole(8, 2 * NS), whole(8, 128)],
            [loc(2 * NS), loc(128), whole(40, 2 * NS), whole(8, 2 * NS), whole(8, 128)],
            [
                sds((CT, 2 * NS), bf16), sds((CT, 128), f32), sds((40, 2 * NS), f32),
                sds((8, 2 * NS), f32), sds((8, 128), f32),
            ],
            [pltpu.VMEM((BLK + 8, 2 * NS), f32), pltpu.VMEM((BLK + 8, 128), f32)],
            flops=100 * CT * 2 * NS,
            moved=3 << 20,
        )(whole_dbc, bca, bcp, msk, kern_bc, sda, scm)
        accs_bc.append(acc_bc)

        dn = call(
            dn_kernel,
            4,
            [
                whole(CT, 2 * lanes), whole(CT, 2 * lanes), whole(CT, 128),
                pl.BlockSpec((dim // 4, 2 * lanes), lambda i: (i, 0)),
                pl.BlockSpec((dim // 4, 2 * lanes), lambda i: (i, 0)),
                pl.BlockSpec((dim // 4, 128), lambda i: (i, 0)),
            ],
            pl.BlockSpec((CT, dim // 4), lambda i: (0, i)),
            sds((CT, dim), bf16),
            flops=8 * CT * lanes * dim,
            moved=14 << 20,
        )(dz[j], dxp[j], ddt[j], w_a, w_b, wdt_t)
        near_sum = scatter_line(dn) + jnp.dot(dsp[j], wbc_near, preferred_element_type=f32)
        near[j] = lax.dynamic_slice_in_dim(near_sum, mine * local_dim, local_dim, 1)
        far[j] = swap(
            lax.dynamic_slice_in_dim(near_sum, (1 - mine) * local_dim, local_dim, 1).astype(bf16)
        )
        mts[j] = line_sum(mtg[j][:, 0] + mtb[:, 0]) + mtc[:, 0]

    def halves(v, bit):
        size = v.shape[-2] // 2
        up = (lax.axis_index("rows") // bit) % 2
        keep = lax.dynamic_slice_in_dim(v, up * size, size, v.ndim - 2)
        give = lax.dynamic_slice_in_dim(v, (1 - up) * size, size, v.ndim - 2)
        return keep, give

    def reduce_pair(v):
        keep, give = halves(v, 1)
        v = keep + cross(give, 1)
        v = v[0] + swap(v[1].astype(bf16)).astype(f32)
        bit = 2
        while bit < nrows:
            keep, give = halves(v, bit)
            v = keep + cross(give.astype(bf16), bit).astype(f32)
            bit *= 2
        while bit > 1:
            bit //= 2
            got = cross(v, bit)
            low = (lax.axis_index("rows") // bit) % 2 == 0
            v = jnp.concatenate([jnp.where(low, v, got), jnp.where(low, got, v)], axis=0)
        return v

    def weight_grad(a, b):
        return jnp.einsum("ta,tb->ab", a, b, preferred_element_type=f32)

    c_all = jnp.concatenate(c_rel, axis=0)
    yn_all = jnp.concatenate(yn, axis=0)
    g_out = reduce_pair(weight_grad(yn_all, c_all).reshape(2, lanes, dim))
    back = [(zpos + groups - q) % groups for q in range(groups)]
    grad_w_out = jnp.concatenate(
        [lax.dynamic_slice_in_dim(g_out, k * wide, wide, 1) for k in back], axis=1
    )

    def zx_grad(v):
        v = jnp.concatenate(v, axis=0)
        return reduce_pair(
            jnp.stack([weight_grad(normed, v[:, :lanes]), weight_grad(normed, v[:, lanes:])])
        )

    grad_w_zx = jnp.stack([zx_grad(dz), zx_grad(dxp)], axis=1)
    cols = w_bc.shape[2]
    dsp_all = jnp.concatenate(dsp, axis=0).reshape(LEN, 2, NS)
    dsp_near = lax.dynamic_slice_in_dim(dsp_all, zpos * 2 * cols, 2 * cols, 2)
    dsp_near = dsp_near.reshape(LEN, 2, 2, cols)
    ddt_all = jnp.concatenate(ddt, axis=0)

    def few(q):
        sel = lax.dynamic_index_in_dim(dsp_near, q, 2, keepdims=False).reshape(LEN, 2 * cols)
        dts = lax.dynamic_slice_in_dim(ddt_all, jnp.where(q == mine, 0, heads), heads, 1)
        return jnp.concatenate([sel, dts], axis=1)

    both = jnp.concatenate([few(mine), few(1 - mine)], axis=1)
    g_few = weight_grad(normed, both)
    width = 2 * cols + heads
    g_few = reduce_pair(jnp.stack([g_few[:, :width], g_few[:, width:]]))
    grad_w_bc = g_few[:, : 2 * cols].reshape(dim, 2, cols)
    grad_w_dt = g_few[:, 2 * cols :]

    acc = sum(accs).reshape(2, 6, 8, lanes).sum(axis=2)
    gg = sum(ggs).reshape(2, 1, lanes)
    acc_dt = sum(accs_dt).reshape(2, 8, 128).sum(axis=1)[:, :docl].reshape(2, 2, heads)
    acc_dt = jnp.pad(acc_dt.transpose(1, 0, 2).reshape(2, 1, -1), ((0, 0), (0, 0), (0, lanes - docl)))
    vec = jnp.concatenate([acc, gg, acc_dt], axis=1)
    acc_bc = sum(accs_bc).reshape(5, 8, 2 * NS).sum(axis=1)

    def rows_sum(v):
        bit = 1
        while bit < nrows:
            v = v + cross(v, bit)
            bit *= 2
        return v

    vec = rows_sum(vec[0] + swap(vec[1]))
    acc_bc = rows_sum(acc_bc + swap(acc_bc)).reshape(5, 2, NS)
    acc_bc = lax.dynamic_slice_in_dim(acc_bc, me * cols, cols, 2)

    s_all = jnp.concatenate(scales)
    out_near = mixer * s_all[:, None]
    o_own = lax.dynamic_slice_in_dim(out_near, mine * local_dim, local_dim, 1)
    o_far = swap(
        lax.dynamic_slice_in_dim(out_near, (1 - mine) * local_dim, local_dim, 1).astype(bf16)
    )
    r_own = r_wide[:, 0]
    m_own = jnp.concatenate(mts)
    r_far = swap(r_own)
    m_far = swap(m_own)
    d_own = jnp.concatenate(near, axis=0)
    d_far = jnp.concatenate(far, axis=0)
    x_near = lax.dynamic_slice_in_dim(hidden_in, me * local_dim, local_dim, 1).astype(f32)
    gain = lax.dynamic_slice_in_dim(norm_gain, me * local_dim, local_dim, 0)
    outs, grads, gain_sum = [], [], 0.0
    for q in range(2):
        sel = mine == q
        x = x_near[q * LEN : (q + 1) * LEN]
        cot = cotangent[q * LEN : (q + 1) * LEN].astype(f32)
        outs.append((x + jnp.where(sel, o_own, o_far.astype(f32))).astype(bf16))
        d = jnp.where(sel, d_own, d_far.astype(f32))
        r = jnp.where(sel, r_own, r_far)[:, None]
        m = jnp.where(sel, m_own, m_far)[:, None]
        grads.append(cot + r * (d * gain) - x * (r * r) * (m / dim))
        gain_sum = gain_sum + jnp.sum(d * x * r, axis=0)
    return (
        jnp.concatenate(outs, axis=0),
        jnp.concatenate(grads, axis=0),
        rows_sum(gain_sum),
        grad_w_zx,
        grad_w_dt,
        grad_w_bc,
        vec[:4],
        vec[4],
        acc_bc[:4],
        acc_bc[4],
        vec[7, heads : 2 * heads],
        vec[7, :heads],
        vec[5].reshape(heads, HD).sum(axis=1),
        vec[6],
        grad_w_out,
    )


def solution(mesh):
    placed = (
        P("rows", None),
        P("rows"),
        P("rows", "state"),
        P(),
        P(None, None, "state"),
        P(None, "state"),
        P(None, None, "state"),
        P(None, "state"),
        P("state"),
        P(None, None, "state"),
        P(None, "state"),
        P("state"),
        P("state"),
        P("state"),
        P("state"),
        P("state", None),
    )
    return jax.shard_map(
        shards,
        mesh=mesh,
        in_specs=placed,
        out_specs=(
            P("rows", "state"),
            P("rows", "state"),
            P("state"),
            P(None, None, "state"),
            P(None, "state"),
            P(None, None, "state"),
            P(None, "state"),
            P("state"),
            P(None, None, "state"),
            P(None, "state"),
            P("state"),
            P("state"),
            P("state"),
            P("state"),
            P("state", None),
        ),
        check_vma=False,
    )
```

time: 3300 us -> 1250 us (0.38)
  waiting for transfers between devices: 1660 us -> 361 us
  matrix products: 602 us -> 76.1 us
  local copies, waits for them, and re-layouts: 478 us -> 96.6 us
  other arithmetic: 433 us -> 130 us
  Pallas kernels: 0 us -> 273 us
  starting transfers between devices: 0.46 us -> 246 us
  blocking collectives: 84.2 us -> 33.5 us
    psum x2 -> x0, waiting for transfers between devices: 1080 us -> none  [the longest x1 964 us: shards(): grad_normed = lax.psum(partial_in, 'state')]
    reduce_scatter x1 -> x0, waiting for transfers between devices: 497 us -> none  [shards(): lax.psum_scatter(partial_out, 'state', scatter_dimension=1, tiled=True)]
    dot_general x106 -> x10, matrix products: 555 us -> 76.1 us  [the longest x6 74.9 us: weight_grad(): return jnp.einsum('ta,tb->ab', a, b, preferred_element_type=f32)]
    ppermute x0 -> x120, waiting for transfers between devices: none -> 361 us  [the longest x15 94.7 us: scatter_line(): lax.ppermute(send_u, 'state', [(i, i + 2) for i in range(parts - 2) if i...]
    pallas_call x0 -> x26, Pallas kernels: none -> 273 us  [the longest x4 74 us: shards(): call(functools.partial(back_kernel, docl), CB, [loc(2 * lanes), bt(2 * NS...]
    ppermute x0 -> x120, starting transfers between devices: none -> 246 us  [the longest x15 80.8 us: scatter_line(): lax.ppermute(send_u, 'state', [(i, i + 2) for i in range(parts - 2) if i...]
    reduce_sum x29 -> x9, other arithmetic: 155 us -> 8.59 us  [the longest x4 3.08 us: shards(): ggs[j] = gg.sum(axis=0)]
    another operation x100 -> x14, other arithmetic: 136 us -> 12 us  [the longest x3 6.21 us: shards(): grad_w_zx = jnp.stack([zx_grad(dz), zx_grad(dxp)], axis=1)]
  transfers between devices with their start and end apart: 6 -> 121, of which waited for: 4 -> 43; matrix products, arithmetic and copies ran while one was open for 18% -> 16% of each run, Pallas kernels for 0% -> 11%
where the time goes in v1:
time: 1250 us; the launch traced here: 1230 us
  waiting for transfers between devices  361 us (29%)
  Pallas kernels  273 us (22%)
  starting transfers between devices  246 us (20%)
  other arithmetic  130 us (10%)
  local copies, waits for them, and re-layouts  96.6 us (8%)
  matrix products  76.1 us (6%)
  blocking collectives  33.5 us (3%)
  between operations  17.7 us (1%)
    ppermute x15, waiting for transfers between devices, scatter_line(): lax.ppermute(send_u, 'state', [(i, i + 2) for i in range(parts - 2) if i...  94.7 us
    ppermute x15, starting transfers between devices, scatter_line(): lax.ppermute(send_u, 'state', [(i, i + 2) for i in range(parts - 2) if i...  80.8 us
    dot_general x6, matrix products, weight_grad(): return jnp.einsum('ta,tb->ab', a, b, preferred_element_type=f32)  74.9 us
    pallas_call x4, Pallas kernels, shards(): call(functools.partial(back_kernel, docl), CB, [loc(2 * lanes), bt(2 * NS...  74 us
    ppermute x24, waiting for transfers between devices, cross(): return lax.ppermute(v, 'rows', [(i, i ^ bit) for i in range(nrows)])  72 us
    ppermute x12, waiting for transfers between devices, gather_line(): cur_d = lax.ppermute(cur_d, 'state', left(k))  70.6 us
    ppermute x18, waiting for transfers between devices, swap(): return lax.ppermute(v, 'state', pair)  66 us
    unnamed x287, local copies, waits for them, and re-layouts  40.7 us
  transfers between devices with their start and end apart: 121, of which 43 were waited for; matrix products, arithmetic and copies ran while one was open for 16% of the time, Pallas kernels for 11%

profile of v1, /device:TPU:0, one launch (start us, length us, event | category | flops | bytes accessed | tf_op | source)
XLA Modules:
  0.0 1233.1 jit_solution(10966896917126268474)
XLA Ops:
  29.1 20.4 %shard_map.271 = (bf16[2048,2048]{1,0:T(8,128)(2,1)}, f32[2048,128]{1,0:T(8,128)}, f32[2048,512]{1,0:T(8,128)}, f32[2048,512]{1,0:T(8,128)}, f32[2048,512]{1,0:T(8,128)}, /*index=5*/bf16[2048,512]{1,0:T(8,128)(2,1)}) custom-call(s32[1]{0:T(128)} %bitcast.which, bf16[4096,2048]{1,0:T(8,128)(2,1)} %hid.1, f32[1,2048]{1,0:T(1,128)} %bitcast.176, ...), custom_call_target="tpu_custom_call" | custom-call | flops 8589934592 | bytes 41943040 | tf_op jit(solution)/shard_map/pallas_call | solution.py:511
  68.3 33.5 %all_gather.7 = f32[5,2,128]{0,1,2:T(2,128)S(1)} all-gather(f32[5,2,16]{0,1,2:T(2,128)S(1)} %copy.83), channel_id=1, replica_groups=mesh['rows'=4,'state'=8] {'state'}, dimensions={2}, use_global_device_ids=true | all-gather | bytes 5760 | tf_op jit(solution)/shard_map/all_gather | solution.py:497
  122.3 15.6 %shard_map.272 = (f32[2048,256]{1,0:T(8,128)}, f32[2048,256]{1,0:T(8,128)}, bf16[2048,256]{1,0:T(8,128)(2,1)}, f32[2048,128]{1,0:T(8,128)}, f32[2048,128]{1,0:T(...) custom-call(bf16[2048,2048]{1,0:T(8,128)(2,1)} %get-tuple-element.125.normed, ...), custom_call_target="tpu_custom_call" | custom-call | flops 4294967296 | bytes 18874368 | tf_op jit(solution)/shard_map/pallas_call | solution.py:528
  137.9 16.4 %shard_map.273 = (f32[2048,512]{1,0:T(8,128)}, bf16[2048,512]{1,0:T(8,128)(2,1)}, f32[8,128,512]{2,1,0:T(8,128)}, f32[2048,128]{1,0:T(8,128)}) custom-call(bf16[2048,512]{1,0:T(8,128)(2,1)} %get-tuple-element.123.xs.xsa, f32[2048,512]{1,0:T(8,128)} %get-tuple-element.124.z.za, bf16[2048,256]{1,0:T(8,128)(2,1)} %get-tuple-element.126.bc, ...), custom_call_target="tpu_custom_call" | custom-call | flops 10737418240 | bytes 20971520 | tf_op jit(solution)/shard_map/pallas_call | solution.py:543
  248.5 14.2 %collective-permute-start.32 = (bf16[512,512]{1,0:T(8,128)(2,1)S(1)}, bf16[512,512]{1,0:T(8,128)(2,1)S(1)}, u32[]{:S(2)}, u32[]{:S(2)}) collective-permute-start(bf16[512,512]{1,0:T(8,128)(2,1)S(1)} %collective-permute-done.31), channel_id=1, source_target_pairs={{2,0},{3,1},{10,8},{11,9},{18,16},{19,17},{26,24},{27,25}} | collective-permute-start | bytes 1572872 | tf_op jit(solution)/shard_map/ppermute | solution.py:591
  266.6 11.4 collective-permute-done.32
  278.1 10.6 collective-permute-done.40
  298.1 18.1 %shard_map.274 = (f32[2048,512]{1,0:T(8,128)}, f32[2048,512]{1,0:T(8,128)}, f32[2048,512]{1,0:T(8,128)}, bf16[2048,512]{1,0:T(8,128)(2,1)}) custom-call(bf16[2048,2048]{1,0:T(8,128)(2,1)} %get-tuple-element.125.normed, bf16[2048,1024]{1,0:T(8,128)(2,1)} %pad_maximum_fusion.1.w.wb, f32[8,512]{1,0:T(8,128)} %copy-done.82, f32[2048,128]{1,0:T(8,128)} %pad.35.msk), custom_call_target="tpu_custom_call" | custom-call | flops 8589934592 | bytes 29360128 | tf_op jit(solution)/shard_map/pallas_call | solution.py:563
  316.2 16.5 %shard_map.275 = (f32[2048,512]{1,0:T(8,128)}, bf16[2048,512]{1,0:T(8,128)(2,1)}, f32[8,128,512]{2,1,0:T(8,128)}, f32[2048,128]{1,0:T(8,128)}) custom-call(bf16[2048,512]{1,0:T(8,128)(2,1)} %get-tuple-element.131.xs.xsb, f32[2048,512]{1,0:T(8,128)} %get-tuple-element.132.z.zb, bf16[2048,256]{1,0:T(8,128)(2,1)} %get-tuple-element.126.bc, ...), custom_call_target="tpu_custom_call" | custom-call | flops 10737418240 | bytes 20971520 | tf_op jit(solution)/shard_map/pallas_call | solution.py:543
  366.9 14.0 %shard_map.276 = bf16[2048,2048]{1,0:T(8,128)(2,1)} custom-call(bf16[2048,512]{1,0:T(8,128)(2,1)} %get-tuple-element.130.ga, bf16[2048,512]{1,0:T(8,128)(2,1)} %get-tuple-element.133.gb, bf16[512,2048]{1,0:T(8,128)(2,1)} %wa.1, bf16[512,2048]{1,0:T(8,128)(2,1)} %pad_maximum_fusion.4.wb), custom_call_target="tpu_custom_call" | custom-call | flops 8589934592 | bytes 14680064 | tf_op jit(solution)/shard_map/pallas_call | solution.py:630
  429.3 10.7 convolution_bitcast_fusion.2
  448.5 18.4 %shard_map.285 = (bf16[512,1024]{1,0:T(8,128)(2,1)}, bf16[512,128]{1,0:T(8,128)(2,1)}, bf16[512,256]{1,0:T(8,128)(2,1)}, f32[512,128]{1,0:T(8,128)}, f32[2,48,51...) custom-call(bf16[512,1024]{1,0:T(8,128)(2,1)} %get-tuple-element.162.dy, ...), custom_call_target="tpu_custom_call" | custom-call | flops 25769803776 | bytes 20971520 | tf_op jit(solution)/shard_map/pallas_call | solution.py:695
  466.8 18.5 %shard_map.286 = (bf16[512,1024]{1,0:T(8,128)(2,1)}, bf16[512,128]{1,0:T(8,128)(2,1)}, bf16[512,256]{1,0:T(8,128)(2,1)}, f32[512,128]{1,0:T(8,128)}, f32[2,48,51...) custom-call(bf16[512,1024]{1,0:T(8,128)(2,1)} %get-tuple-element.159.dy, ...), custom_call_target="tpu_custom_call" | custom-call | flops 25769803776 | bytes 20971520 | tf_op jit(solution)/shard_map/pallas_call | solution.py:695
  485.3 18.7 %shard_map.287 = (bf16[512,1024]{1,0:T(8,128)(2,1)}, bf16[512,128]{1,0:T(8,128)(2,1)}, bf16[512,256]{1,0:T(8,128)(2,1)}, f32[512,128]{1,0:T(8,128)}, f32[2,48,51...) custom-call(bf16[512,1024]{1,0:T(8,128)(2,1)} %get-tuple-element.156.dy, ...), custom_call_target="tpu_custom_call" | custom-call | flops 25769803776 | bytes 20971520 | tf_op jit(solution)/shard_map/pallas_call | solution.py:695
  504.1 18.4 %shard_map.288 = (bf16[512,1024]{1,0:T(8,128)(2,1)}, bf16[512,128]{1,0:T(8,128)(2,1)}, bf16[512,256]{1,0:T(8,128)(2,1)}, f32[512,128]{1,0:T(8,128)}, f32[2,48,51...) custom-call(bf16[512,1024]{1,0:T(8,128)(2,1)} %get-tuple-element.146.dy, ...), custom_call_target="tpu_custom_call" | custom-call | flops 25769803776 | bytes 20971520 | tf_op jit(solution)/shard_map/pallas_call | solution.py:695
  525.4 10.0 convolution_bitcast_fusion
  545.5 36.1 %fusion = f32[1024,2048]{1,0:T(8,128)} fusion(bf16[512,512]{1,0:T(8,128)(2,1)} %copy-done.53, bf16[512,512]{1,0:T(8,128)(2,1)S(1)} %copy-done.44, bf16[512,512]{1,0:T(8,128)(2,1)} %copy-done.54, bf16[512,512]{1,0:T(8,128)(2,1)} %copy-done.57, bf16[512,512]{1,0:T(8,128)(2,1)} %copy-done.51, bf16[512,512]{1,0:T(8,128)(2,1)S(1)} %copy-done.42, ...), kind=kOutput, calls=%fused_computation.9 | convolution fusion | flops 8724152320 | bytes 20971520 | tf_op jit(solution)/shard_map/ta,tb->ab/dot_general | solution.py:792
  618.0 10.1 shard_map.296
  714.9 14.9 %collective-permute-done.58 = bf16[512,256]{1,0:T(8,128)(2,1)S(1)} collective-permute-done((bf16[512,256]{1,0:T(8,128)(2,1)S(1)}, bf16[512,256]{1,0:T(8,128)(2,1)S(1)}, u32[]{:S(2)}, u32[]{:S(2)}) %collective-permute-start.58) | collective-permute-done | bytes 262176 | tf_op jit(solution)/shard_map/ppermute | solution.py:727
  812.9 49.5 %collective-permute-done.68 = bf16[512,512]{1,0:T(8,128)(2,1)S(1)} collective-permute-done((bf16[512,512]{1,0:T(8,128)(2,1)}, bf16[512,512]{1,0:T(8,128)(2,1)S(1)}, u32[]{:S(2)}, u32[]{:S(2)}) %collective-permute-start.68) | collective-permute-done | bytes 524320 | tf_op jit(solution)/shard_map/ppermute | solution.py:617
  885.3 13.8 %collective-permute-start.49 = (bf16[512,512]{1,0:T(8,128)(2,1)S(1)}, bf16[512,512]{1,0:T(8,128)(2,1)S(1)}, u32[]{:S(2)}, u32[]{:S(2)}) collective-permute-start(bf16[512,512]{1,0:T(8,128)(2,1)S(1)} %get-tuple-element.330), channel_id=1, source_target_pairs={{0,2},{1,3},{2,4},{3,5},{4,6},{5,7},{8,10},{9,11},{10,12},{11,13},... | collective-permute-start | bytes 1572872 | tf_op jit(solution)/shard_map/ppermute | solution.py:617
  899.2 11.0 collective-permute-start.63
  984.8 25.5 %collective-permute-done.7 = bf16[2048,512]{1,0:T(8,128)(2,1)S(1)} collective-permute-done((bf16[2048,512]{1,0:T(8,128)(2,1)S(1)}, bf16[2048,512]{1,0:T(8,128)(2,1)S(1)}, u32[]{:S(2)}, u32[]{:S(2)}) %collective-permute-start.7) | collective-permute-done | bytes 2097184 | tf_op jit(solution)/shard_map/ppermute | solution.py:617
  1041.8 11.5 collective-permute-done.116
  1055.6 20.2 %collective-permute-done.95 = bf16[1024,512]{1,0:T(8,128)(2,1)} collective-permute-done((bf16[1024,512]{1,0:T(8,128)(2,1)}, bf16[1024,512]{1,0:T(8,128)(2,1)}, u32[]{:S(2)}, u32[]{:S(2)}) %collective-permute-start.95) | collective-permute-done | bytes 1048608 | tf_op jit(solution)/shard_map/ppermute | solution.py:448
  1078.1 13.7 %collective-permute-done.100 = bf16[1024,512]{1,0:T(8,128)(2,1)S(1)} collective-permute-done((bf16[1024,512]{1,0:T(8,128)(2,1)S(1)}, bf16[1024,512]{1,0:T(8,128)(2,1)S(1)}, u32[]{:S(2)}, u32[]{:S(2)}) %collective-permute-start.100) | collective-permute-done | bytes 1048608 | tf_op jit(solution)/shard_map/ppermute | solution.py:448
  1096.6 10.6 collective-permute-done.101
  1113.2 16.4 %collective-permute-done.118 = f32[128,2048]{1,0:T(8,128)S(1)} collective-permute-done((f32[128,2048]{1,0:T(8,128)S(1)}, f32[128,2048]{1,0:T(8,128)S(1)}, u32[]{:S(2)}, u32[]{:S(2)}) %collective-permute-start.118) | collective-permute-done | bytes 1048608 | tf_op jit(solution)/shard_map/ppermute | solution.py:451
  1134.0 18.1 %collective-permute-done.97 = f32[512,512]{1,0:T(8,128)S(1)} collective-permute-done((f32[512,512]{1,0:T(8,128)S(1)}, f32[512,512]{1,0:T(8,128)S(1)}, u32[]{:S(2)}, u32[]{:S(2)}) %collective-permute-start.97) | collective-permute-done | bytes 1048608 | tf_op jit(solution)/shard_map/ppermute | solution.py:451
  1152.6 16.1 %collective-permute-done.102 = f32[512,512]{1,0:T(8,128)S(1)} collective-permute-done((f32[512,512]{1,0:T(8,128)S(1)}, f32[512,512]{1,0:T(8,128)S(1)}, u32[]{:S(2)}, u32[]{:S(2)}) %collective-permute-start.102) | collective-permute-done | bytes 1048608 | tf_op jit(solution)/shard_map/ppermute | solution.py:451
  1186.5 13.0 %collective-permute-done.45 = bf16[2048,256]{1,0:T(8,128)(2,1)} collective-permute-done((bf16[2048,256]{1,0:T(8,128)(2,1)}, bf16[2048,256]{1,0:T(8,128)(2,1)}, u32[]{:S(2)}, u32[]{:S(2)}) %collective-permute-start.45) | collective-permute-done | bytes 1048608 | tf_op jit(solution)/shard_map/ppermute | solution.py:448
  1205.3 16.5 %copy.94 = f32[2048,2,512]{2,1,0:T(2,128)} copy(f32[2048,2,512]{2,0,1:T(8,128)S(1)} %pad_maximum_fusion) | data formatting | bytes 16777216
  (781 shorter events, 653.0 us)
Async XLA Ops:
  7.3 112.4 %all-gather.2.cloned.1.call-start = ((), (), s32[]{:S(2)}) async-start(), calls=%async_computation | async-start | bytes 1179648 | tf_op jit(solution)/shard_map/all_gather | solution.py:492
  9.8 109.7 %collective-permute-start.4 = (bf16[256,2048]{1,0:T(8,128)(2,1)}, bf16[256,2048]{1,0:T(8,128)(2,1)}, u32[]{:S(2)}, u32[]{:S(2)}) collective-permute-start(bf16[256,2048]{1,0:T(8,128)(2,1)} %constant_dynamic-slice_fusion.26), channel_id=1, source_target_pairs={{0,1},{1,0},{2,3},{3,2},{4,5},{5,4},{6,7},{7,6},{8,9},{9,8},{10,11... | collective-permute-start | bytes 3145736 | tf_op jit(solution)/shard_map/ppermute | solution.py:448
  13.1 90.1 %collective-permute-start.1 = (f32[8,512]{1,0:T(8,128)S(1)}, f32[8,512]{1,0:T(8,128)S(1)}, u32[]{:S(2)}, u32[]{:S(2)}) collective-permute-start(f32[8,512]{1,0:T(8,128)S(1)} %concatenate.140.kern.prm.prma), channel_id=1, source_target_pairs={{0,1},{1,0},{2,3},{3,2},{4,5},{5,4},{6,7},{7,6},{8,9},{9,8},{10,11... | collective-permute-start | bytes 49160 | tf_op jit(solution)/shard_map/ppermute | solution.py:448
  14.3 89.8 %collective-permute-start = (bf16[8,2048]{0,1:T(8,128)(2,1)}, bf16[8,2048]{0,1:T(8,128)(2,1)}, u32[]{:S(2)}, u32[]{:S(2)}) collective-permute-start(bf16[8,2048]{0,1:T(8,128)(2,1)} %bitcast.14), channel_id=1, source_target_pairs={{0,1},{1,0},{2,3},{3,2},{4,5},{5,4},{6,7},{7,6},{8,9},{9,8},{10,11... | collective-permute-start | bytes 98312 | tf_op jit(solution)/shard_map/ppermute | solution.py:448
  17.3 90.3 %collective-permute-start.12 = (bf16[2048,256]{1,0:T(8,128)(2,1)}, bf16[2048,256]{1,0:T(8,128)(2,1)}, u32[]{:S(2)}, u32[]{:S(2)}) collective-permute-start(bf16[2048,256]{1,0:T(8,128)(2,1)} %constant_dynamic-slice_fusion.23), channel_id=1, source_target_pairs={{0,1},{1,0},{2,3},{3,2},{4,5},{5,4},{6,7},{7,6},{8,9},{9,8},{10,11... | collective-permute-start | bytes 3145736 | tf_op jit(solution)/shard_map/ppermute | solution.py:448
  51.1 51.5 %collective-permute-start.46 = (f32[2048]{0:T(1024)S(1)}, f32[2048]{0:T(1024)S(1)}, u32[]{:S(2)}, u32[]{:S(2)}) collective-permute-start(f32[2048]{0:T(1024)S(1)} %slice_reduce_fusion), channel_id=1, source_target_pairs={{0,1},{1,0},{2,3},{3,2},{4,5},{5,4},{6,7},{7,6},{8,9},{9,8},{10,11... | collective-permute-start | bytes 24584 | tf_op jit(solution)/shard_map/ppermute | solution.py:448
  109.5 56.4 %collective-permute-start.13 = (bf16[512,512]{1,0:T(8,128)(2,1)S(1)}, bf16[512,512]{1,0:T(8,128)(2,1)}, u32[]{:S(2)}, u32[]{:S(2)}) collective-permute-start(bf16[512,512]{1,0:T(8,128)(2,1)S(1)} %get-tuple-element.346), channel_id=1, source_target_pairs={{0,2},{1,3},{2,4},{3,5},{4,6},{5,7},{8,10},{9,11},{10,12},{11,13},... | collective-permute-start | bytes 1572872 | tf_op jit(solution)/shard_map/ppermute | solution.py:590
  111.6 60.0 %collective-permute-start.14 = (bf16[512,512]{1,0:T(8,128)(2,1)S(1)}, bf16[512,512]{1,0:T(8,128)(2,1)}, u32[]{:S(2)}, u32[]{:S(2)}) collective-permute-start(bf16[512,512]{1,0:T(8,128)(2,1)S(1)} %get-tuple-element.346), channel_id=1, source_target_pairs={{2,0},{3,1},{4,2},{5,3},{6,4},{7,5},{10,8},{11,9},{12,10},{13,11},... | collective-permute-start | bytes 1572872 | tf_op jit(solution)/shard_map/ppermute | solution.py:591
  112.9 63.2 %collective-permute-start.21 = (bf16[512,512]{1,0:T(8,128)(2,1)S(1)}, bf16[512,512]{1,0:T(8,128)(2,1)}, u32[]{:S(2)}, u32[]{:S(2)}) collective-permute-start(bf16[512,512]{1,0:T(8,128)(2,1)S(1)} %get-tuple-element.347), channel_id=1, source_target_pairs={{0,2},{1,3},{2,4},{3,5},{4,6},{5,7},{8,10},{9,11},{10,12},{11,13},... | collective-permute-start | bytes 1572872 | tf_op jit(solution)/shard_map/ppermute | solution.py:590
  118.3 59.4 %collective-permute-start.22 = (bf16[512,512]{1,0:T(8,128)(2,1)S(1)}, bf16[512,512]{1,0:T(8,128)(2,1)}, u32[]{:S(2)}, u32[]{:S(2)}) collective-permute-start(bf16[512,512]{1,0:T(8,128)(2,1)S(1)} %get-tuple-element.347), channel_id=1, source_target_pairs={{2,0},{3,1},{4,2},{5,3},{6,4},{7,5},{10,8},{11,9},{12,10},{13,11},... | collective-permute-start | bytes 1572872 | tf_op jit(solution)/shard_map/ppermute | solution.py:591
  186.8 77.8 %collective-permute-start.2 = (bf16[1024,1024]{1,0:T(8,128)(2,1)S(1)}, bf16[1024,1024]{1,0:T(8,128)(2,1)S(1)}, u32[]{:S(2)}, u32[]{:S(2)}) collective-permute-start(bf16[1024,1024]{1,0:T(8,128)(2,1)S(1)} %copy-done.34), channel_id=1, source_target_pairs={{0,1},{1,0},{2,3},{3,2},{4,5},{5,4},{6,7},{7,6},{8,9},{9,8},{10,11... | collective-permute-start | bytes 6291464 | tf_op jit(solution)/shard_map/ppermute | solution.py:448
  340.6 44.8 %collective-permute-start.19 = (f32[1024]{0:T(1024)S(1)}, f32[1024]{0:T(1024)S(1)}, u32[]{:S(2)}, u32[]{:S(2)}) collective-permute-start(f32[1024]{0:T(1024)S(1)} %pad_maximum_fusion.26), channel_id=1, source_target_pairs={{0,2},{1,3},{2,0},{3,1},{4,6},{5,7},{6,4},{7,5},{8,10},{9,11},{10,... | collective-permute-start | bytes 12296 | tf_op jit(solution)/shard_map/ppermute | solution.py:456
  586.8 64.5 %collective-permute-start.109 = (f32[8,512]{1,0:T(8,128)S(1)}, f32[8,512]{1,0:T(8,128)S(1)}, u32[]{:S(2)}, u32[]{:S(2)}) collective-permute-start(f32[8,512]{1,0:T(8,128)S(1)} %slice_bitcast_fusion.6), channel_id=1, source_target_pairs={{0,1},{1,0},{2,3},{3,2},{4,5},{5,4},{6,7},{7,6},{8,9},{9,8},{10,11... | collective-permute-start | bytes 49160 | tf_op jit(solution)/shard_map/ppermute | solution.py:448
  665.0 136.2 %collective-permute-start.50 = (bf16[512,512]{1,0:T(8,128)(2,1)}, bf16[512,512]{1,0:T(8,128)(2,1)}, u32[]{:S(2)}, u32[]{:S(2)}) collective-permute-start(bf16[512,512]{1,0:T(8,128)(2,1)} %get-tuple-element.333), channel_id=1, source_target_pairs={{6,4},{7,5},{14,12},{15,13},{22,20},{23,21},{30,28},{31,29}} | collective-permute-start | bytes 1572872 | tf_op jit(solution)/shard_map/ppermute | solution.py:620
  675.1 130.2 %collective-permute-start.64 = (bf16[512,512]{1,0:T(8,128)(2,1)}, bf16[512,512]{1,0:T(8,128)(2,1)}, u32[]{:S(2)}, u32[]{:S(2)}) collective-permute-start(bf16[512,512]{1,0:T(8,128)(2,1)} %get-tuple-element.337), channel_id=1, source_target_pairs={{6,4},{7,5},{14,12},{15,13},{22,20},{23,21},{30,28},{31,29}} | collective-permute-start | bytes 1572872 | tf_op jit(solution)/shard_map/ppermute | solution.py:620
  690.6 85.3 %collective-permute-start.73 = (bf16[512,512]{1,0:T(8,128)(2,1)}, bf16[512,512]{1,0:T(8,128)(2,1)}, u32[]{:S(2)}, u32[]{:S(2)}) collective-permute-start(bf16[512,512]{1,0:T(8,128)(2,1)} %get-tuple-element.344), channel_id=1, source_target_pairs={{0,2},{1,3},{8,10},{9,11},{16,18},{17,19},{24,26},{25,27}} | collective-permute-start | bytes 1572872 | tf_op jit(solution)/shard_map/ppermute | solution.py:617
  799.7 112.2 %collective-permute-start.6 = (bf16[2048,512]{1,0:T(8,128)(2,1)}, bf16[2048,512]{1,0:T(8,128)(2,1)S(1)}, u32[]{:S(2)}, u32[]{:S(2)}) collective-permute-start(bf16[2048,512]{1,0:T(8,128)(2,1)} %get-tuple-element.307), channel_id=1, source_target_pairs={{0,2},{1,3},{8,10},{9,11},{16,18},{17,19},{24,26},{25,27}} | collective-permute-start | bytes 6291464 | tf_op jit(solution)/shard_map/ppermute | solution.py:617
  801.9 60.4 %collective-permute-start.68 = (bf16[512,512]{1,0:T(8,128)(2,1)}, bf16[512,512]{1,0:T(8,128)(2,1)S(1)}, u32[]{:S(2)}, u32[]{:S(2)}) collective-permute-start(bf16[512,512]{1,0:T(8,128)(2,1)} %add_convert_fusion.11), channel_id=1, source_target_pairs={{0,2},{1,3},{2,4},{3,5},{8,10},{9,11},{10,12},{11,13},{16,18},{17,... | collective-permute-start | bytes 1572872 | tf_op jit(solution)/shard_map/ppermute | solution.py:617
  805.3 215.8 %collective-permute-start.115 = (f32[2,256,2048]{2,1,0:T(8,128)}, f32[2,256,2048]{2,1,0:T(8,128)}, u32[]{:S(2)}, u32[]{:S(2)}) collective-permute-start(f32[2,256,2048]{2,1,0:T(8,128)} %constant_dynamic-slice_fusion.1), channel_id=1, source_target_pairs={{0,8},{8,0},{16,24},{24,16},{1,9},{9,1},{17,25},{25,17},{2,10},{10... | collective-permute-start | bytes 12582920 | tf_op jit(solution)/shard_map/ppermute | solution.py:451
  806.1 61.4 %collective-permute-start.76 = (bf16[512,512]{1,0:T(8,128)(2,1)}, bf16[512,512]{1,0:T(8,128)(2,1)S(1)}, u32[]{:S(2)}, u32[]{:S(2)}) collective-permute-start(bf16[512,512]{1,0:T(8,128)(2,1)} %get-tuple-element.345), channel_id=1, source_target_pairs={{6,4},{7,5},{14,12},{15,13},{22,20},{23,21},{30,28},{31,29}} | collective-permute-start | bytes 1572872 | tf_op jit(solution)/shard_map/ppermute | solution.py:620
  808.4 66.0 %collective-permute-start.74 = (bf16[512,512]{1,0:T(8,128)(2,1)}, bf16[512,512]{1,0:T(8,128)(2,1)S(1)}, u32[]{:S(2)}, u32[]{:S(2)}) collective-permute-start(bf16[512,512]{1,0:T(8,128)(2,1)} %add_convert_fusion.7), channel_id=1, source_target_pairs={{0,2},{1,3},{2,4},{3,5},{8,10},{9,11},{10,12},{11,13},{16,18},{17,... | collective-permute-start | bytes 1572872 | tf_op jit(solution)/shard_map/ppermute | solution.py:617
  944.7 83.3 %collective-permute-start.94 = (f32[2,1024,512]{2,1,0:T(8,128)}, f32[2,1024,512]{2,1,0:T(8,128)}, u32[]{:S(2)}, u32[]{:S(2)}) collective-permute-start(f32[2,1024,512]{2,1,0:T(8,128)} %fusion.35), channel_id=1, source_target_pairs={{0,8},{8,0},{16,24},{24,16},{1,9},{9,1},{17,25},{25,17},{2,10},{10... | collective-permute-start | bytes 12582920 | tf_op jit(solution)/shard_map/ppermute | solution.py:451
  965.2 45.2 %collective-permute-start.7 = (bf16[2048,512]{1,0:T(8,128)(2,1)S(1)}, bf16[2048,512]{1,0:T(8,128)(2,1)S(1)}, u32[]{:S(2)}, u32[]{:S(2)}) collective-permute-start(bf16[2048,512]{1,0:T(8,128)(2,1)S(1)} %add_convert_fusion.3), channel_id=1, source_target_pairs={{0,2},{1,3},{2,4},{3,5},{8,10},{9,11},{10,12},{11,13},{16,18},{17,... | collective-permute-start | bytes 6291464 | tf_op jit(solution)/shard_map/ppermute | solution.py:617
  976.3 60.8 %collective-permute-start.99 = (f32[2,1024,512]{2,1,0:T(8,128)}, f32[2,1024,512]{2,1,0:T(8,128)}, u32[]{:S(2)}, u32[]{:S(2)}) collective-permute-start(f32[2,1024,512]{2,1,0:T(8,128)} %fusion.32), channel_id=1, source_target_pairs={{0,8},{8,0},{16,24},{24,16},{1,9},{9,1},{17,25},{25,17},{2,10},{10... | collective-permute-start | bytes 12582920 | tf_op jit(solution)/shard_map/ppermute | solution.py:451
  1014.1 95.1 %collective-permute-start.10 = (bf16[2048,512]{1,0:T(8,128)(2,1)}, bf16[2048,512]{1,0:T(8,128)(2,1)}, u32[]{:S(2)}, u32[]{:S(2)}) collective-permute-start(bf16[2048,512]{1,0:T(8,128)(2,1)} %get-tuple-element.306), channel_id=1, source_target_pairs={{4,2},{5,3},{6,4},{7,5},{12,10},{13,11},{14,12},{15,13},{20,18},{2... | collective-permute-start | bytes 6291464 | tf_op jit(solution)/shard_map/ppermute | solution.py:620
  1016.1 153.2 %collective-permute-start.8 = (bf16[2048,512]{1,0:T(8,128)(2,1)}, bf16[2048,512]{1,0:T(8,128)(2,1)}, u32[]{:S(2)}, u32[]{:S(2)}) collective-permute-start(bf16[2048,512]{1,0:T(8,128)(2,1)} %get-tuple-element.305), channel_id=1, source_target_pairs={{0,2},{1,3},{2,4},{3,5},{4,6},{5,7},{8,10},{9,11},{10,12},{11,13},... | collective-permute-start | bytes 6291464 | tf_op jit(solution)/shard_map/ppermute | solution.py:617
  1036.1 39.7 %collective-permute-start.95 = (bf16[1024,512]{1,0:T(8,128)(2,1)}, bf16[1024,512]{1,0:T(8,128)(2,1)}, u32[]{:S(2)}, u32[]{:S(2)}) collective-permute-start(bf16[1024,512]{1,0:T(8,128)(2,1)} %fusion.56), channel_id=1, source_target_pairs={{0,1},{1,0},{2,3},{3,2},{4,5},{5,4},{6,7},{7,6},{8,9},{9,8},{10,11... | collective-permute-start | bytes 3145736 | tf_op jit(solution)/shard_map/ppermute | solution.py:448
  1040.7 51.2 %collective-permute-start.100 = (bf16[1024,512]{1,0:T(8,128)(2,1)S(1)}, bf16[1024,512]{1,0:T(8,128)(2,1)S(1)}, u32[]{:S(2)}, u32[]{:S(2)}) collective-permute-start(bf16[1024,512]{1,0:T(8,128)(2,1)S(1)} %fusion.57), channel_id=1, source_target_pairs={{0,1},{1,0},{2,3},{3,2},{4,5},{5,4},{6,7},{7,6},{8,9},{9,8},{10,11... | collective-permute-start | bytes 3145736 | tf_op jit(solution)/shard_map/ppermute | solution.py:448
  1094.7 57.4 %collective-permute-start.97 = (f32[512,512]{1,0:T(8,128)S(1)}, f32[512,512]{1,0:T(8,128)S(1)}, u32[]{:S(2)}, u32[]{:S(2)}) collective-permute-start(f32[512,512]{1,0:T(8,128)S(1)} %convert_add_fusion.2), channel_id=1, source_target_pairs={{0,16},{8,24},{16,0},{24,8},{1,17},{9,25},{17,1},{25,9},{2,18},{10... | collective-permute-start | bytes 3145736 | tf_op jit(solution)/shard_map/ppermute | solution.py:451
  1107.3 61.4 %collective-permute-start.102 = (f32[512,512]{1,0:T(8,128)S(1)}, f32[512,512]{1,0:T(8,128)S(1)}, u32[]{:S(2)}, u32[]{:S(2)}) collective-permute-start(f32[512,512]{1,0:T(8,128)S(1)} %convert_add_fusion.1), channel_id=1, source_target_pairs={{0,16},{8,24},{16,0},{24,8},{1,17},{9,25},{17,1},{25,9},{2,18},{10... | collective-permute-start | bytes 3145736 | tf_op jit(solution)/shard_map/ppermute | solution.py:451
  1111.6 57.6 %collective-permute-start.11 = (bf16[2048,512]{1,0:T(8,128)(2,1)S(1)}, bf16[2048,512]{1,0:T(8,128)(2,1)}, u32[]{:S(2)}, u32[]{:S(2)}) collective-permute-start(bf16[2048,512]{1,0:T(8,128)(2,1)S(1)} %add_convert_fusion), channel_id=1, source_target_pairs={{2,0},{3,1},{4,2},{5,3},{6,4},{7,5},{10,8},{11,9},{12,10},{13,11},... | collective-permute-start | bytes 6291464 | tf_op jit(solution)/shard_map/ppermute | solution.py:620
  1130.1 43.6 %collective-permute-start.119 = (f32[256,2048]{1,0:T(8,128)S(1)}, f32[256,2048]{1,0:T(8,128)}, u32[]{:S(2)}, u32[]{:S(2)}) collective-permute-start(f32[256,2048]{1,0:T(8,128)S(1)} %pad_maximum_fusion.15), channel_id=1, source_target_pairs={{0,8},{8,0},{16,24},{24,16},{1,9},{9,1},{17,25},{25,17},{2,10},{10... | collective-permute-start | bytes 6291464 | tf_op jit(solution)/shard_map/ppermute | solution.py:451
  (226 other events, 4075.4 us)
Sparse Core Ops, SparseCore 0:
  13.3 47.5 all-gather.1

commit v2 on v1

--- a/solution.py
+++ b/solution.py
@@ -5,12 +5,13 @@
 from jax import lax
 from jax.experimental import pallas as pl
 from jax.experimental.pallas import tpu as pltpu
+from jax.sharding import Mesh
 from jax.sharding import PartitionSpec as P
 
 LEN = 2048
 BLK = 256
 NBLK = LEN // BLK
-CHUNKS = 4
+CHUNKS = 2
 CT = LEN // CHUNKS
 CB = CT // BLK
 HD = 64
@@ -19,6 +20,8 @@
 HIGHEST = lax.Precision.HIGHEST
 f32 = jnp.float32
 bf16 = jnp.bfloat16
+COST = 1
+CHEAP = 1 << 16
 VMEM_LIMIT = 56 * 1024 * 1024
 
 
@@ -74,10 +77,10 @@
     return nn(high, pick) + nn(rest, pick)
 
 
-def conv_tile(step, x1, kern, msk, buf):
+def conv_tile(step, x1, kern, msk, buf, start=None):
     @pl.when(step == 0)
     def _():
-        buf[0:8, :] = jnp.zeros((8, buf.shape[1]), f32)
+        buf[0:8, :] = jnp.zeros((8, buf.shape[1]), f32) if start is None else start[...]
 
     buf[8 : 8 + BLK, :] = x1
     acc = kern[4:5, :] + kern[3:4, :] * x1
@@ -87,24 +90,25 @@
     return acc
 
 
-def project_tile(n, w, kern, msk, z, xp, a, xs, buf):
+def project_tile(n, w, kern, msk, z, xp, a, xs, buf, start=None):
     lanes = w.shape[1] // 2
     p = nn(n, w[...])
-    z[...] = p[:, :lanes]
+    z[...] = p[:, :lanes].astype(bf16)
     x1 = p[:, lanes:]
-    xp[...] = x1
-    acc = conv_tile(pl.program_id(0), x1, kern, msk, buf)
-    a[...] = acc
+    xp[...] = x1.astype(bf16)
+    acc = conv_tile(pl.program_id(0), x1, kern, msk, buf, start)
+    a[...] = acc.astype(bf16)
     xs[...] = (acc * sigmoid(acc)).astype(bf16)
 
 
-def first_kernel(which, hid, gain, w, kern, msk, normed, r, z, xp, a, xs, buf):
+def first_kernel(which, hid, gain, w, kern, msk, start, normed, r, z, xp, a, xs, tail, buf):
     x = hid[...].astype(f32)
     rr = lax.rsqrt(jnp.mean(x * x, axis=1, keepdims=True) + EPSILON)
     n = (x * rr * gain[...]).astype(bf16)
     normed[...] = n
     r[...] = jnp.broadcast_to(rr, (BLK, 128))
-    project_tile(n, w, kern, msk, z, xp, a, xs, buf)
+    project_tile(n, w, kern, msk, z, xp, a, xs, buf, start)
+    tail[...] = buf[0:8, :]
 
 
 def second_kernel(normed, w, kern, msk, z, xp, a, xs, buf):
@@ -182,7 +186,7 @@
     y[...] = yv
     ut = (u * expand(trail, off, heads)).astype(bf16)
     state[...] = s_in * expand(retain, off, heads) + tn(b, ut)
-    zz = z[...]
+    zz = z[...].astype(f32)
     gated = yv * zz * sigmoid(zz)
     gw[...] = (gated * prm[5:6, :]).astype(bf16)
     pw[...] = jnp.broadcast_to(jnp.sum(gated * gated, axis=1, keepdims=True), (BLK, 128))
@@ -217,7 +221,7 @@
         at = slice(half * lanes, half * lanes + lanes)
         dn = dref[...].astype(f32)
         y = yref[...]
-        z = zref[...]
+        z = zref[...].astype(f32)
         gn = prm[5:6, :]
         sg = sigmoid(z)
         act = z * sg
@@ -321,12 +325,12 @@
         r2 = r2 + segment_sums(ubf * tb, off)
         r3 = r3 + segment_sums(xf * du, off)
         held = held + segment_sums(fold(d_state * s_in), off)
-        a = ar[...]
+        a = ar[...].astype(f32)
         sa = sigmoid(a)
         da = (dte * du + skip * dyf) * (sa * (1.0 + a * (1.0 - sa)))
         buf[half, BLK : BLK + 8, :] = buf[half, 0:8, :]
         buf[half, 0:BLK, :] = da
-        xp = xpr[...]
+        xp = xpr[...].astype(f32)
         dx, taps = conv_back(da, xp, prm, buf.at[half], mbuf)
         low = dx.astype(bf16)
         dxp[:, at] = low
@@ -388,6 +392,49 @@
     o[...] = (v + nt(ddt[...], wdt[...])).astype(bf16)
 
 
+def weight_kernel(count, tiles, extra, core, *refs):
+    lhs, rhs, more, (keep, give) = refs[:count], refs[count : 2 * count], refs[2 * count : -2], refs[-2:]
+    v = tn(lhs[0][...], rhs[0][...])
+    for k in range(1, count):
+        v = v + tn(lhs[k][...], rhs[k][...])
+    if extra:
+        part = lhs[0].shape[0]
+        w = tn(lhs[0][...], more[0][:part, :])
+        for k in range(1, count):
+            w = w + tn(lhs[k][...], more[0][k * part : (k + 1) * part, :])
+        n, m = v.shape[1] // 2, w.shape[1] // 2
+        v = jnp.concatenate([v[:, :n], w[:, :m], v[:, n:], w[:, m:]], axis=1)
+    step = pl.program_id(0)
+
+    @pl.when(step < tiles)
+    def _():
+        keep[...] = v
+
+    @pl.when(step >= tiles)
+    def _():
+        give[...] = v
+
+
+def join_kernel(core, za, zb, xa, xb, o):
+    first = pl.program_id(0) * 2 // pl.num_programs(0) == core[0]
+    rows, lanes = za.shape
+    parts = lanes // 128
+
+    def put(z, x):
+        for k in range(parts):
+            at = slice(k * 128, k * 128 + 128)
+            o[pl.ds(2 * k, rows, stride=2 * parts), :] = z[:, at].astype(f32)
+            o[pl.ds(2 * k + 1, rows, stride=2 * parts), :] = x[:, at].astype(f32)
+
+    @pl.when(first)
+    def _():
+        put(za, xa)
+
+    @pl.when(jnp.logical_not(first))
+    def _():
+        put(zb, xb)
+
+
 def tile(width, first=0):
     return pl.BlockSpec((BLK, width), lambda i, *_: (first + i, 0))
 
@@ -405,34 +452,61 @@
     return jax.ShapeDtypeStruct(shape, dtype)
 
 
-def call(kernel, grid, in_specs, out_specs, out_shape, scratch=(), flops=0, moved=0, prefetch=0):
-    return pl.pallas_call(
-        kernel,
+def call(
+    kernel, grid, in_specs, out_specs, out_shape, scratch=(), flops=0, moved=0, prefetch=0, after=(), into=()
+):
+    first = prefetch + len(in_specs)
+    extra = len(after) + len(into)
+
+    def body(*refs):
+        kernel(*refs[:first], *refs[first + extra :])
+
+    fn = pl.pallas_call(
+        body,
         grid_spec=pltpu.PrefetchScalarGridSpec(
             num_scalar_prefetch=prefetch,
             grid=(grid,),
-            in_specs=in_specs,
+            in_specs=list(in_specs) + [pl.BlockSpec(memory_space=pl.ANY)] * extra,
             out_specs=out_specs,
             scratch_shapes=list(scratch),
         ),
         out_shape=out_shape,
+        input_output_aliases={first + len(after) + k: k for k in range(len(into))},
         compiler_params=pltpu.CompilerParams(
             dimension_semantics=("arbitrary",), vmem_limit_bytes=VMEM_LIMIT
         ),
-        cost_estimate=pl.CostEstimate(flops=flops, bytes_accessed=moved, transcendentals=0),
+        cost_estimate=pl.CostEstimate(flops=flops // COST, bytes_accessed=moved // COST, transcendentals=0),
     )
+    return lambda *args: fn(*args, *after, *into)
+
+
+def three(v):
+    high = lax.optimization_barrier(v.astype(bf16))
+    rest = v - high.astype(f32)
+    mid = lax.optimization_barrier(rest.astype(bf16))
+    return high, mid, (rest - mid.astype(f32)).astype(bf16)
 
 
 def shards(
     hidden_in, starts, cotangent, norm_gain, w_zx, w_dt, w_bc, conv_x_w, conv_x_b,
     conv_bc_w, conv_bc_b, dt_bias, a_log, d_skip, gnorm_w, w_out,
 ):
-    parts = lax.axis_size("state")
+    order = []
+
+    def ordered(*args, after=(), **kw):
+        def run(*operands):
+            outs = call(*args, after=tuple(after) + tuple(order[-1:]), **kw)(*operands)
+            order.append(jax.tree.leaves(outs)[-1])
+            return outs
+
+        return run
+
+    groups = lax.axis_size("zline")
+    parts = 2 * groups
     nrows = lax.axis_size("rows")
-    groups = parts // 2
-    me = lax.axis_index("state")
-    mine = me % 2
-    zpos = me // 2
+    zpos = lax.axis_index("zline")
+    mine = lax.axis_index("pair")
+    me = 2 * zpos + mine
     core = lax.axis_index("rows") % 2
     dim = hidden_in.shape[1]
     local_dim = cotangent.shape[1]
@@ -442,35 +516,39 @@
     docl = 2 * heads
     wide = dim // groups
 
-    pair = [(i, i ^ 1) for i in range(parts)]
-
     def swap(v):
-        return lax.ppermute(v, "state", pair)
+        return lax.ppermute(v, "pair", [(0, 1), (1, 0)])
 
     def cross(v, bit):
         return lax.ppermute(v, "rows", [(i, i ^ bit) for i in range(nrows)])
 
     def line_sum(v):
-        bit = 2
-        while bit < parts:
-            v = v + lax.ppermute(v, "state", [(i, i ^ bit) for i in range(parts)])
+        bit = 1
+        while bit < groups:
+            v = v + lax.ppermute(v, "zline", [(i, i ^ bit) for i in range(groups)])
             bit *= 2
         return v
 
     def rows_of(v, start, size):
         return lax.dynamic_slice_in_dim(v, start, size, 0)
 
-    def fetch(own):
+    def zero_after(v):
+        return (v.reshape(-1)[0].astype(f32) > 1e38).astype(jnp.int32)
+
+    def late(v, after):
+        return v + zero_after(after).astype(v.dtype)
+
+    def half_of_partner(own, after):
         half = own.shape[0] // 2
-        got = swap(rows_of(own, core * half, half))
+        return swap(rows_of(own, core * half + zero_after(after), half))
+
+    def with_other_half(got, after):
         other = cross(got, 1)
-        first = core == 0
+        first = core + zero_after(after) == 0
         return jnp.concatenate([jnp.where(first, got, other), jnp.where(first, other, got)], axis=0)
 
     w_a = w_zx.reshape(dim, 2 * lanes)
-    w_b = fetch(w_a)
     o_a = w_out
-    o_b = fetch(w_out)
     small = jnp.stack([dt_bias, a_log, d_skip]).reshape(-1)
     prm_a = jnp.concatenate(
         [
@@ -489,13 +567,44 @@
     bias_all = jnp.concatenate([dt_bias, small_b[0]])
     rate_all = -jnp.exp(jnp.concatenate([a_log, small_b[1]]))
     dtp = jnp.pad(jnp.stack([bias_all, rate_all]), ((0, 6), (0, 128 - docl)))
-    wbc = lax.all_gather(w_bc.transpose(1, 2, 0), "state", axis=1, tiled=True)
-    wbc = wbc.reshape(2 * NS, dim)
+    taps = jnp.concatenate([conv_bc_w, conv_bc_b[None]], axis=0).transpose(1, 2, 0)
+    high, mid, low = three(taps)
+    pack = jnp.concatenate([w_bc.transpose(1, 2, 0), high, mid, low], axis=2)
+    pack = jnp.pad(pack, ((0, 0), (0, 0), (0, 128 - 15)))
+
+    def grow(v, axis, bit, here):
+        got = lax.ppermute(v, axis, [(i, i ^ bit) for i in range(lax.axis_size(axis))])
+        return jnp.concatenate([jnp.where(here, got, v), jnp.where(here, v, got)], axis=1)
+
+    pack = grow(pack, "pair", 1, mine == 1)
+    is0 = mine == 0
+    c_pair = [None] * CHUNKS
+
+    def cotangent_of(j, follow, after=None):
+        c_mine = rows_of(cotangent, mine * LEN + j * CT, CT)
+        c_got = swap(rows_of(cotangent, (1 - mine) * LEN + j * CT + zero_after(follow), CT))
+        low = is0 if after is None else mine + zero_after(after) == 0
+        return c_got, jnp.concatenate(
+            [jnp.where(low, c_mine, c_got), jnp.where(low, c_got, c_mine)], axis=1
+        )
+
+    c_got, c_pair[CHUNKS - 1] = cotangent_of(CHUNKS - 1, pack)
+    w_got = half_of_partner(w_a, pack)
+    o_got = half_of_partner(w_out, w_got)
+    early = pack
+    turned = [
+        lax.ppermute(pack, "zline", [(i, (i + k) % groups) for i in range(groups)])
+        for k in range(groups - 1, 0, -1)
+    ]
+    pack = jnp.concatenate((turned + [pack]) * 2, axis=1)
+    size = 2 * w_bc.shape[2]
+    pack = lax.dynamic_slice_in_dim(pack, (groups - 1 - zpos) * size, groups * size, 1)
+    pack = pack.reshape(2 * NS, dim + 128)
+    wbc = pack[:, :dim]
+    taps = pack[:, dim : dim + 15].astype(f32).reshape(2 * NS, 3, 5).sum(axis=1)
+    kern_bc = jnp.pad(taps.T, ((0, 3), (0, 0)))
     wdt = jnp.concatenate([wdt_a, wdt_b, jnp.zeros((128 - docl, dim), bf16)], axis=0)
     wst = jnp.concatenate([wbc, wdt], axis=0)
-    kern_bc = jnp.concatenate([conv_bc_w, conv_bc_b[None]], axis=0)
-    kern_bc = lax.all_gather(kern_bc, "state", axis=2, tiled=True).reshape(5, 2 * NS)
-    kern_bc = jnp.pad(kern_bc, ((0, 3), (0, 0)))
 
     st = rows_of(starts, mine * LEN, LEN).astype(f32)
     open1 = jnp.where(jnp.arange(LEN) == 0, 0.0, 1.0 - st)
@@ -506,26 +615,35 @@
 
     tl = (BLK, lanes)
     proj_out = [tile(lanes), tile(lanes), tile(lanes), tile(lanes)]
-    proj_shape = [sds((LEN, lanes), f32)] * 3 + [sds((LEN, lanes), bf16)]
+    proj_shape = [sds((LEN, lanes), bf16)] * 4
     pf = 2 * LEN * dim * 2 * lanes
-    normed, r_wide, z_a, xp_a, a_a, xs_a = call(
-        first_kernel,
-        NBLK,
-        [
-            pl.BlockSpec((BLK, dim), lambda i, which: (which[0] * NBLK + i, 0)),
-            whole(1, dim),
-            whole(dim, 2 * lanes),
-            whole(8, lanes),
-            tile(128),
-        ],
-        [tile(dim), tile(128)] + proj_out,
-        [sds((LEN, dim), bf16), sds((LEN, 128), f32)] + proj_shape,
-        [pltpu.VMEM((BLK + 8, lanes), f32)],
-        flops=pf,
-        moved=40 << 20,
-        prefetch=1,
-    )(which, hidden_in, norm_gain.reshape(1, dim), w_a, prm_a, msk)
-    bcp, bca, bc, dtr, dt, cum, cumt = call(
+
+    def first_step(part, start, after, into=()):
+        at = part * NBLK // 2
+        return ordered(
+            first_kernel,
+            NBLK // 2,
+            [
+                pl.BlockSpec((BLK, dim), lambda i, which: (which[0] * NBLK + at + i, 0)),
+                whole(1, dim),
+                whole(dim, 2 * lanes),
+                whole(8, lanes),
+                tile(128, at),
+                whole(8, lanes),
+            ],
+            [tile(dim, at), tile(128, at)] + [tile(lanes, at)] * 4 + [whole(8, lanes)],
+            [sds((LEN, dim), bf16), sds((LEN, 128), f32)] + proj_shape + [sds((8, lanes), f32)],
+            [pltpu.VMEM((BLK + 8, lanes), f32)],
+            flops=pf // 2,
+            moved=20 << 20,
+            prefetch=1,
+            after=after,
+            into=into,
+        )(which, hidden_in, norm_gain.reshape(1, dim), w_a, prm_a, msk, start)
+
+    *begun, tail = first_step(0, jnp.zeros((8, lanes), f32), (early,))
+    normed, r_wide, z_a, xp_a, a_a, xs_a, tail = first_step(1, tail, tuple(turned), begun)
+    bcp, bca, bc, dtr, dt, cum, cumt = ordered(
         functools.partial(states_kernel, docl),
         NBLK,
         [tile(dim), whole(2 * NS + 128, dim), whole(8, 2 * NS), whole(8, 128), tile(128)],
@@ -537,10 +655,11 @@
         [pltpu.VMEM((BLK + 8, 2 * NS), f32)],
         flops=2 * LEN * dim * 512,
         moved=18 << 20,
+        after=(c_pair[CHUNKS - 1],),
     )(normed, wst, kern_bc, dtp, msk)
 
-    def scan(off, xs, z, prm):
-        return call(
+    def scan(off, xs, z, prm, after=()):
+        return ordered(
             functools.partial(scan_kernel, docl, off),
             NBLK,
             [
@@ -557,10 +676,14 @@
             [pltpu.VMEM((NS, lanes), f32)],
             flops=10 << 30,
             moved=20 << 20,
+            after=after,
         )(xs, z, bc, dt, cum, cumt, prm)
 
     y_a, gw_a, sin_a, pw_a = scan(0, xs_a, z_a, prm_a)
-    z_b, xp_b, a_b, xs_b = call(
+    for j in reversed(range(CHUNKS - 1)):
+        c_pair[j] = cotangent_of(j, cumt, pw_a)[1]
+    w_b = with_other_half(w_got, pw_a)
+    z_b, xp_b, a_b, xs_b = ordered(
         second_kernel,
         NBLK,
         [tile(dim), whole(dim, 2 * lanes), whole(8, lanes), tile(128)],
@@ -571,128 +694,85 @@
         moved=28 << 20,
     )(normed, w_b, prm_b, msk)
     y_b, gw_b, sin_b, pw_b = scan(heads, xs_b, z_b, prm_b)
-
-    c_mine = rows_of(cotangent, mine * LEN, LEN)
-    c_got = swap(rows_of(cotangent, (1 - mine) * LEN, LEN))
-    is0 = mine == 0
-    c_pair = jnp.concatenate([jnp.where(is0, c_mine, c_got), jnp.where(is0, c_got, c_mine)], axis=1)
-
-    def right(k):
-        return [(i, i + 2) for i in range(parts - 2) if i // 2 >= k - 1]
-
-    def left(k):
-        return [(i, i - 2) for i in range(2, parts) if i // 2 <= groups - k]
-
-    def gather_line(v):
-        up, down = {}, {}
-        cur_u = cur_d = v
-        for k in range(1, groups):
-            cur_u = lax.ppermute(cur_u, "state", right(k))
-            cur_d = lax.ppermute(cur_d, "state", left(k))
-            up[k], down[k] = cur_u, cur_d
-        pieces = [v]
-        for k in range(1, groups):
-            pieces.append(jnp.where(zpos >= k, up[k], down[groups - k]))
-        return jnp.concatenate(pieces, axis=1)
-
-    def relative(w):
-        return jnp.concatenate(
-            [
-                lax.dynamic_slice_in_dim(w, (zpos + groups - k) % groups * wide, wide, 1)
-                for k in range(groups)
-            ],
-            axis=1,
-        )
-
-    def scatter_line(v):
-        def own(j):
-            return lax.dynamic_slice_in_dim(v, jnp.clip(j, 0, groups - 1) * wide, wide, 1)
-
-        up = down = None
-        for d in range(groups - 1, 0, -1):
-            send_u, send_d = own(zpos + d), own(zpos - d)
-            if up is not None:
-                send_u = (send_u.astype(f32) + up.astype(f32)).astype(bf16)
-                send_d = (send_d.astype(f32) + down.astype(f32)).astype(bf16)
-            up = lax.ppermute(
-                send_u, "state", [(i, i + 2) for i in range(parts - 2) if i // 2 + d < groups]
-            )
-            down = lax.ppermute(
-                send_d, "state", [(i, i - 2) for i in range(2, parts) if i // 2 - d >= 0]
-            )
-        return own(zpos).astype(f32) + up.astype(f32) + down.astype(f32)
-
-    c_rel = [None] * CHUNKS
+    o_b = with_other_half(o_got, pw_b)
+
+    class LineSum:
+        def __init__(self, v):
+            self.v = v
+            self.left = groups - 1
+            self.up = self.down = None
+
+        def own(self, j):
+            return lax.dynamic_slice_in_dim(self.v, jnp.clip(j, 0, groups - 1) * wide, wide, 1)
+
+        def step(self, after=None):
+            d = self.left
+            if d == 0:
+                return
+            late = 0 if after is None else zero_after(after)
+            send_u, send_d = self.own(zpos + d + late), self.own(zpos - d - late)
+            if self.up is not None:
+                send_u = (send_u.astype(f32) + self.up.astype(f32)).astype(bf16)
+                send_d = (send_d.astype(f32) + self.down.astype(f32)).astype(bf16)
+            self.up = lax.ppermute(send_u, "zline", [(i, i + 1) for i in range(groups - d)])
+            self.down = lax.ppermute(send_d, "zline", [(i, i - 1) for i in range(d, groups)])
+            self.left = d - 1
+
+        def result(self):
+            while self.left:
+                self.step()
+            return self.own(zpos).astype(f32) + self.up.astype(f32) + self.down.astype(f32)
+
+    c_all = [None] * CHUNKS
     for j in reversed(range(CHUNKS)):
-        c_rel[j] = gather_line(c_pair[j * CT : (j + 1) * CT])
-    or_a, or_b = relative(o_a), relative(o_b)
-
-    partial_out = call(
-        out_kernel,
-        NBLK,
-        [tile(lanes), tile(lanes), whole(lanes, dim), whole(lanes, dim)],
-        tile(dim),
-        sds((LEN, dim), bf16),
-        flops=4 * LEN * lanes * dim,
-        moved=14 << 20,
-    )(gw_a, gw_b, o_a, o_b)
-    mixer = scatter_line(partial_out)
-
-    def dyn_call(j):
-        return call(
+        c_all[j] = lax.all_gather(c_pair[j], "zline", axis=1, tiled=True)
+
+    power = pw_a[:, 0] + pw_b[:, 0]
+    wdt_t = wdt.T
+    wbc_near = lax.dynamic_slice_in_dim(wbc, zpos * wide, wide, 1)
+
+    def dyn_step(j, after=()):
+        return ordered(
             dyn_kernel,
             CB,
             [tile(dim), whole(lanes, dim), whole(lanes, dim), tile(lanes, j * CB), tile(lanes, j * CB)],
             [tile(lanes), tile(lanes), tile(128)],
             [sds((CT, lanes), bf16)] * 2 + [sds((CT, 128), f32)],
             flops=4 * CT * lanes * dim,
-            moved=10 << 20,
-        )(c_rel[j], or_a, or_b, gw_a, gw_b)
-
-    power = pw_a[:, 0] + pw_b[:, 0]
-    dz, dy, yn, mtg, ggs, scales = ([None] * CHUNKS for _ in range(6))
-    for j in reversed(range(CHUNKS)):
-        d_a, d_b, qs = dyn_call(j)
+            moved=12 << 20,
+            after=after,
+        )(c_all[j], o_a, o_b, gw_a, gw_b)
+
+    def scales_of(j, qs):
         sums = line_sum(jnp.concatenate([power[j * CT : (j + 1) * CT], qs[:, 0]]))
         s = lax.rsqrt(sums[:CT] / inner + EPSILON)
         kq = s * s * s * (sums[CT:] / inner)
-        scales[j] = s
-        sq = jnp.pad(jnp.stack([s, kq], axis=1), ((0, 0), (0, 126)))
-        dz[j], dy[j], yn[j], mtg[j], gg = call(
+        return s, jnp.pad(jnp.stack([s, kq], axis=1), ((0, 0), (0, 126)))
+
+    def gate_step(j, sq, d_a, d_b, after=()):
+        return ordered(
             gate_kernel,
             CB,
-            [tile(128)]
-            + [tile(lanes)] * 2
-            + [tile(lanes, j * CB)] * 4
-            + [whole(8, lanes)] * 2,
+            [tile(128)] + [tile(lanes)] * 2 + [tile(lanes, j * CB)] * 4 + [whole(8, lanes)] * 2,
             [tile(2 * lanes)] * 3 + [tile(128), whole(8, 2 * lanes)],
             [sds((CT, 2 * lanes), bf16)] * 3 + [sds((CT, 128), f32), sds((8, 2 * lanes), f32)],
-            flops=100 * CT * lanes,
-            moved=12 << 20,
+            flops=4000 * CT * lanes,
+            moved=20 << 20,
+            after=after,
         )(sq, d_a, d_b, y_a, y_b, z_a, z_b, prm_a, prm_b)
-        ggs[j] = gg.sum(axis=0)
-
-    wdt_t = wdt.T
-    wbc_near = lax.dynamic_slice_in_dim(wbc, zpos * wide, wide, 1)
-    ds = jnp.zeros((2, NS, lanes), f32)
-    cda = jnp.zeros((2, 8, lanes), f32)
-    cm = jnp.zeros((8, 128), f32)
-    sda = jnp.zeros((8, 2 * NS), f32)
-    scm = cm
-    dxp, ddt, dsp, mts, near, far = ([None] * CHUNKS for _ in range(6))
-    accs, accs_dt, accs_bc = [], [], []
-    for j in reversed(range(CHUNKS)):
+
+    def back_step(j, dy, ds, cda, cm, after=()):
         last = j * CB + CB - 1
 
-        def bt(width, last=last):
+        def bt(width):
             return back_tile(width, last)
 
         def loc(width):
             return back_tile(width, CB - 1)
 
-        cols = pl.BlockSpec((128, BLK), lambda i, last=last: (0, last - i))
-        sins = pl.BlockSpec((1, NS, lanes), lambda i, last=last: (last - i, 0, 0))
-        dxp[j], ddt[j], dbc, mtb, acc, acc_dt, ds, cda, cm = call(
+        cols = pl.BlockSpec((128, BLK), lambda i: (0, last - i))
+        sins = pl.BlockSpec((1, NS, lanes), lambda i: (last - i, 0, 0))
+        return ordered(
             functools.partial(back_kernel, docl),
             CB,
             [
@@ -711,25 +791,36 @@
                 sds((2, NS, lanes), f32), sds((2, 8, lanes), f32), sds((8, 128), f32),
             ],
             [pltpu.VMEM((2, BLK + 8, lanes), f32), pltpu.VMEM((BLK + 8, 128), f32)],
-            flops=24 << 30,
-            moved=20 << 20,
+            flops=(80 << 30) // CHUNKS,
+            moved=(80 << 20) // CHUNKS,
+            after=after,
         )(
-            dy[j], bc, dt, cum, cumt, dtr, msk, dtp,
+            dy, bc, dt, cum, cumt, dtr, msk, dtp,
             y_a, y_b, xs_a, xs_b, a_a, a_b, xp_a, xp_b, sin_a, sin_b, prm_a, prm_b,
             ds, cda, cm,
         )
-        accs.append(acc)
-        accs_dt.append(acc_dt)
-
-        whole_dbc = dbc
-        bit = 2
-        while bit < parts:
-            got = lax.ppermute(
-                whole_dbc.astype(bf16), "state", [(i, i ^ bit) for i in range(parts)]
-            )
-            whole_dbc = whole_dbc.astype(f32) + got.astype(f32)
+
+    def states_sum(v, *after):
+        bit = 1
+        after = list(after)
+        while bit < groups:
+            if after:
+                v = late(v, after.pop(0))
+            got = lax.ppermute(v.astype(bf16), "zline", [(i, i ^ bit) for i in range(groups)])
+            v = v.astype(f32) + got.astype(f32)
             bit *= 2
-        dsp[j], mtc, acc_bc, sda, scm = call(
+        return v
+
+    def states_step(j, dbc, sda, scm, after=()):
+        last = j * CB + CB - 1
+
+        def bt(width):
+            return back_tile(width, last)
+
+        def loc(width):
+            return back_tile(width, CB - 1)
+
+        return ordered(
             states_back_kernel,
             CB,
             [loc(2 * NS), bt(2 * NS), bt(2 * NS), bt(128), whole(8, 2 * NS), whole(8, 2 * NS), whole(8, 128)],
@@ -739,12 +830,13 @@
                 sds((8, 2 * NS), f32), sds((8, 128), f32),
             ],
             [pltpu.VMEM((BLK + 8, 2 * NS), f32), pltpu.VMEM((BLK + 8, 128), f32)],
-            flops=100 * CT * 2 * NS,
-            moved=3 << 20,
-        )(whole_dbc, bca, bcp, msk, kern_bc, sda, scm)
-        accs_bc.append(acc_bc)
-
-        dn = call(
+            flops=CHEAP,
+            moved=CHEAP,
+            after=after,
+        )(dbc, bca, bcp, msk, kern_bc, sda, scm)
+
+    def dn_step(dz, dxp, ddt, after=()):
+        return ordered(
             dn_kernel,
             4,
             [
@@ -756,76 +848,181 @@
             pl.BlockSpec((CT, dim // 4), lambda i: (0, i)),
             sds((CT, dim), bf16),
             flops=8 * CT * lanes * dim,
-            moved=14 << 20,
-        )(dz[j], dxp[j], ddt[j], w_a, w_b, wdt_t)
-        near_sum = scatter_line(dn) + jnp.dot(dsp[j], wbc_near, preferred_element_type=f32)
-        near[j] = lax.dynamic_slice_in_dim(near_sum, mine * local_dim, local_dim, 1)
-        far[j] = swap(
-            lax.dynamic_slice_in_dim(near_sum, (1 - mine) * local_dim, local_dim, 1).astype(bf16)
-        )
-        mts[j] = line_sum(mtg[j][:, 0] + mtb[:, 0]) + mtc[:, 0]
-
-    def halves(v, bit):
-        size = v.shape[-2] // 2
-        up = (lax.axis_index("rows") // bit) % 2
-        keep = lax.dynamic_slice_in_dim(v, up * size, size, v.ndim - 2)
-        give = lax.dynamic_slice_in_dim(v, (1 - up) * size, size, v.ndim - 2)
-        return keep, give
-
-    def reduce_pair(v):
-        keep, give = halves(v, 1)
-        v = keep + cross(give, 1)
-        v = v[0] + swap(v[1].astype(bf16)).astype(f32)
-        bit = 2
-        while bit < nrows:
-            keep, give = halves(v, bit)
-            v = keep + cross(give.astype(bf16), bit).astype(f32)
-            bit *= 2
-        while bit > 1:
-            bit //= 2
-            got = cross(v, bit)
-            low = (lax.axis_index("rows") // bit) % 2 == 0
-            v = jnp.concatenate([jnp.where(low, v, got), jnp.where(low, got, v)], axis=0)
-        return v
-
-    def weight_grad(a, b):
-        return jnp.einsum("ta,tb->ab", a, b, preferred_element_type=f32)
-
-    c_all = jnp.concatenate(c_rel, axis=0)
-    yn_all = jnp.concatenate(yn, axis=0)
-    g_out = reduce_pair(weight_grad(yn_all, c_all).reshape(2, lanes, dim))
-    back = [(zpos + groups - q) % groups for q in range(groups)]
-    grad_w_out = jnp.concatenate(
-        [lax.dynamic_slice_in_dim(g_out, k * wide, wide, 1) for k in back], axis=1
+            moved=16 << 20,
+            after=after,
+        )(dz, dxp, ddt, w_a, w_b, wdt_t)
+
+    def near_sum(dn):
+        return lax.psum_scatter(dn, "zline", scatter_dimension=1, tiled=True)
+
+    def near_step(total, dsp):
+        total = total.astype(f32) + jnp.dot(dsp, wbc_near, preferred_element_type=f32)
+        keep = lax.dynamic_slice_in_dim(total, mine * local_dim, local_dim, 1)
+        give = lax.dynamic_slice_in_dim(total, (1 - mine) * local_dim, local_dim, 1)
+        return keep, swap(give.astype(bf16))
+
+    core_at = core.astype(jnp.int32).reshape(1)
+
+    def weight_grad(lhs, rhs, more=None):
+        count = len(rhs)
+        n, m = lhs[0].shape[1], rhs[0].shape[1]
+        part = LEN // count
+        more = [] if more is None else [more]
+        full = m + sum(v.shape[1] for v in more)
+        size = min(256, n // 4)
+        tiles = n // size // 2
+
+        def order(i, core):
+            return jnp.where(i < tiles, i + core[0] * tiles, i - core[0] * tiles)
+
+        return ordered(
+            functools.partial(weight_kernel, count, tiles, len(more)),
+            2 * tiles,
+            [
+                pl.BlockSpec(
+                    (part, size),
+                    lambda i, core, at=0 if v.shape[0] == part else k: (at, order(i, core)),
+                )
+                for k, v in enumerate(lhs)
+            ]
+            + [whole(part, m)] * count
+            + [whole(*v.shape) for v in more],
+            [
+                pl.BlockSpec((size, full), lambda i, core: (jnp.minimum(i, tiles - 1), 0)),
+                pl.BlockSpec((size, full), lambda i, core: (jnp.maximum(i - tiles, 0), 0)),
+            ],
+            [sds((n // 2, full), f32)] * 2,
+            flops=CHEAP,
+            moved=CHEAP,
+            prefetch=1,
+        )(core_at, *lhs, *rhs, *more)
+
+    dz, dy, yn, mtg, scales = ([None] * CHUNKS for _ in range(5))
+    dxp, ddt, dsp, near, far, dns = ([None] * CHUNKS for _ in range(6))
+    ggs, accs, accs_dt, accs_bc = [], [], [], []
+    carry = (jnp.zeros((2, NS, lanes), f32), jnp.zeros((2, 8, lanes), f32), jnp.zeros((8, 128), f32))
+    state_carry = (jnp.zeros((8, 2 * NS), f32), jnp.zeros((8, 128), f32))
+
+    def out_step(j):
+        return ordered(
+            out_kernel,
+            CB,
+            [tile(lanes, j * CB)] * 2 + [whole(lanes, dim)] * 2,
+            tile(dim),
+            sds((CT, dim), bf16),
+            flops=4 * CT * lanes * dim,
+            moved=10 << 20,
+        )(gw_a, gw_b, o_a, o_b)
+
+    top = CHUNKS - 1
+    d_a, d_b, qs = dyn_step(top)
+    scales[top], sq = scales_of(top, qs)
+    mixing = LineSum(out_step(top))
+    mixing.step(after=sq)
+
+    dz[1], dy[1], yn[1], mtg[1], gg = gate_step(1, sq, d_a, d_b)
+    ggs.append(gg)
+    dxp[1], ddt[1], dbc_1, mtb_1, acc, acc_dt, *carry = back_step(1, dy[1], *carry)
+    accs.append(acc)
+    accs_dt.append(acc_dt)
+    dns[1] = dn_step(dz[1], dxp[1], ddt[1], after=(mixing.up, mixing.down))
+    total_1 = near_sum(dns[1])
+    d_a, d_b, qs = dyn_step(0)
+    scales[0], sq = scales_of(0, qs)
+    partial_0 = out_step(0)
+    dz[0], dy[0], yn[0], mtg[0], gg = gate_step(0, sq, d_a, d_b)
+    ggs.append(gg)
+    mixing.step(after=sq)
+    g_out = weight_grad(c_all, yn)
+    g_z = weight_grad([normed] * CHUNKS, dz)
+    mixing_2 = (mixing.up, mixing.down)
+    mixing.step(after=g_z[0])
+    dxp[0], ddt[0], dbc_0, mtb_0, acc, acc_dt, *carry = back_step(
+        0, dy[0], *carry, after=mixing_2
     )
-
-    def zx_grad(v):
-        v = jnp.concatenate(v, axis=0)
-        return reduce_pair(
-            jnp.stack([weight_grad(normed, v[:, :lanes]), weight_grad(normed, v[:, lanes:])])
-        )
-
-    grad_w_zx = jnp.stack([zx_grad(dz), zx_grad(dxp)], axis=1)
+    accs.append(acc)
+    accs_dt.append(acc_dt)
+    dns[0] = dn_step(dz[0], dxp[0], ddt[0], after=(total_1,))
+    total_0 = near_sum(dns[0])
+    mixed_0 = near_sum(partial_0)
+    g_x = weight_grad([normed] * CHUNKS, dxp)
+    summed_1 = states_sum(dbc_1, dbc_0, g_x[0])
+    summed_0 = states_sum(dbc_0, dbc_0, g_x[0])
+    dsp[1], mtc_1, acc_bc, *state_carry = states_step(1, summed_1, *state_carry)
+    accs_bc.append(acc_bc)
+    dsp[0], mtc_0, acc_bc, *state_carry = states_step(0, summed_0, *state_carry)
+    accs_bc.append(acc_bc)
+
     cols = w_bc.shape[2]
-    dsp_all = jnp.concatenate(dsp, axis=0).reshape(LEN, 2, NS)
-    dsp_near = lax.dynamic_slice_in_dim(dsp_all, zpos * 2 * cols, 2 * cols, 2)
-    dsp_near = dsp_near.reshape(LEN, 2, 2, cols)
+    dsp_near = lax.dynamic_slice_in_dim(
+        jnp.concatenate(dsp, axis=0).reshape(LEN, 2, NS), zpos * 2 * cols, 2 * cols, 2
+    ).reshape(LEN, 2, 2, cols)
     ddt_all = jnp.concatenate(ddt, axis=0)
+    width = 2 * cols + heads
 
     def few(q):
         sel = lax.dynamic_index_in_dim(dsp_near, q, 2, keepdims=False).reshape(LEN, 2 * cols)
         dts = lax.dynamic_slice_in_dim(ddt_all, jnp.where(q == mine, 0, heads), heads, 1)
-        return jnp.concatenate([sel, dts], axis=1)
-
-    both = jnp.concatenate([few(mine), few(1 - mine)], axis=1)
-    g_few = weight_grad(normed, both)
-    width = 2 * cols + heads
-    g_few = reduce_pair(jnp.stack([g_few[:, :width], g_few[:, width:]]))
+        return jnp.concatenate([sel, dts, jnp.zeros((LEN, 128 - width), bf16)], axis=1)
+
+    fewer = jnp.concatenate([few(mine), few(1 - mine)], axis=1)
+    g_few = weight_grad([normed], [fewer])
+    near[1], far[1] = near_step(total_1, dsp[1])
+    near[0], far[0] = near_step(total_0, dsp[0])
+    local_sum = jnp.concatenate([mtg[j][:, 0] + m[:, 0] for j, m in ((0, mtb_0), (1, mtb_1))])
+    mean_sum = line_sum(local_sum) + jnp.concatenate([mtc_0[:, 0], mtc_1[:, 0]])
+    mixer = jnp.concatenate([mixed_0.astype(f32), mixing.result()], axis=0)
+
+    def bit_of(bit):
+        return lax.axis_index("rows") // bit % 2
+
+    def reduce_pair(keep, give):
+        n = keep.shape[1] // 2
+        v = keep + cross(give, 1)
+        v = v[:, :n] + swap(v[:, n:].astype(bf16)).astype(f32)
+        bit = 2
+        while bit < nrows:
+            size = v.shape[0] // 2
+            up = bit_of(bit)
+            give = rows_of(v, (1 - up) * size, size)
+            v = rows_of(v, up * size, size) + cross(give.astype(bf16), bit).astype(f32)
+            bit *= 2
+        v = lax.reduce_precision(v, 8, 7).astype(bf16)
+        while bit > 2:
+            bit //= 2
+            got = cross(v, bit)
+            low = bit_of(bit) == 0
+            v = jnp.concatenate([jnp.where(low, v, got), jnp.where(low, got, v)], axis=0)
+        return v
+
+    def both_cores(v):
+        got = cross(v, 1)
+        first = core == 0
+        return jnp.concatenate([jnp.where(first, v, got), jnp.where(first, got, v)], axis=0)
+
+    g_x, g_z, g_out, g_few = (reduce_pair(*g) for g in (g_x, g_z, g_out, g_few))
+    grad_w_out = both_cores(g_out).T.astype(f32)
+    g_few = both_cores(g_few).astype(f32)
     grad_w_bc = g_few[:, : 2 * cols].reshape(dim, 2, cols)
-    grad_w_dt = g_few[:, 2 * cols :]
+    grad_w_dt = g_few[:, 2 * cols : width]
+    x_far, z_far = cross(g_x, 1), cross(g_z, 1)
+    steps = 8
+    size = dim // steps
+    at = pl.BlockSpec((size, lanes), lambda i, core: (i % (steps // 2), 0))
+    grad_w_zx = ordered(
+        join_kernel,
+        steps,
+        [at] * 4,
+        pl.BlockSpec((size * 2 * lanes // 128, 128), lambda i, core: (i, 0)),
+        sds((dim * 2 * lanes // 128, 128), f32),
+        moved=24 << 20,
+        prefetch=1,
+    )(core_at, g_z, z_far, g_x, x_far)
+    grad_w_zx = grad_w_zx.reshape(dim, lanes // 128, 2, 128).transpose(0, 2, 1, 3)
+    grad_w_zx = grad_w_zx.reshape(dim, 2, lanes)
 
     acc = sum(accs).reshape(2, 6, 8, lanes).sum(axis=2)
-    gg = sum(ggs).reshape(2, 1, lanes)
+    gg = sum(ggs).sum(axis=0).reshape(2, 1, lanes)
     acc_dt = sum(accs_dt).reshape(2, 8, 128).sum(axis=1)[:, :docl].reshape(2, 2, heads)
     acc_dt = jnp.pad(acc_dt.transpose(1, 0, 2).reshape(2, 1, -1), ((0, 0), (0, 0), (0, lanes - docl)))
     vec = jnp.concatenate([acc, gg, acc_dt], axis=1)
@@ -849,7 +1046,7 @@
         lax.dynamic_slice_in_dim(out_near, (1 - mine) * local_dim, local_dim, 1).astype(bf16)
     )
     r_own = r_wide[:, 0]
-    m_own = jnp.concatenate(mts)
+    m_own = mean_sum
     r_far = swap(r_own)
     m_far = swap(m_own)
     d_own = jnp.concatenate(near, axis=0)
@@ -886,45 +1083,50 @@
     )
 
 
+STATE = ("zline", "pair")
+
+
 def solution(mesh):
     placed = (
         P("rows", None),
         P("rows"),
-        P("rows", "state"),
+        P("rows", STATE),
         P(),
-        P(None, None, "state"),
-        P(None, "state"),
-        P(None, None, "state"),
-        P(None, "state"),
-        P("state"),
-        P(None, None, "state"),
-        P(None, "state"),
-        P("state"),
-        P("state"),
-        P("state"),
-        P("state"),
-        P("state", None),
+        P(None, None, STATE),
+        P(None, STATE),
+        P(None, None, STATE),
+        P(None, STATE),
+        P(STATE),
+        P(None, None, STATE),
+        P(None, STATE),
+        P(STATE),
+        P(STATE),
+        P(STATE),
+        P(STATE),
+        P(STATE, None),
     )
+    rows, parts = mesh.devices.shape
+    split = Mesh(mesh.devices.reshape(rows, parts // 2, 2), ("rows", "zline", "pair"))
     return jax.shard_map(
         shards,
-        mesh=mesh,
+        mesh=split,
         in_specs=placed,
         out_specs=(
-            P("rows", "state"),
-            P("rows", "state"),
-            P("state"),
-            P(None, None, "state"),
-            P(None, "state"),
-            P(None, None, "state"),
-            P(None, "state"),
-            P("state"),
-            P(None, None, "state"),
-            P(None, "state"),
-            P("state"),
-            P("state"),
-            P("state"),
-            P("state"),
-            P("state", None),
+            P("rows", STATE),
+            P("rows", STATE),
+            P(STATE),
+            P(None, None, STATE),
+            P(None, STATE),
+            P(None, None, STATE),
+            P(None, STATE),
+            P(STATE),
+            P(None, None, STATE),
+            P(None, STATE),
+            P(STATE),
+            P(STATE),
+            P(STATE),
+            P(STATE),
+            P(STATE, None),
         ),
         check_vma=False,
     )

time: 1250 us -> 820 us (0.66)
  waiting for transfers between devices: 361 us -> 180 us
  starting transfers between devices: 246 us -> 114 us
  matrix products: 76.1 us -> 2.11 us
  other arithmetic: 130 us -> 88.8 us
  Pallas kernels: 273 us -> 314 us
  blocking collectives: 33.5 us -> 0 us
    ppermute x96 -> x37, waiting for transfers between devices: 289 us -> 151 us  [the longest x4 76.3 us: states_sum(): lax.ppermute(v.astype(bf16), 'zline', [(i, i ^ bit) for i in range(groups)])]
    ppermute x96 -> x37, starting transfers between devices: 232 us -> 95.7 us  [the longest x6 41.3 us: line_sum(): v = v + lax.ppermute(v, 'zline', [(i, i ^ bit) for i in range(groups)])]
    dot_general x10 -> x2, matrix products: 76.1 us -> 2.11 us  [near_step(): jnp.dot(dsp, wbc_near, preferred_element_type=f32)]
    ppermute x24, waiting for transfers between devices: 72 us -> 28.6 us  [cross(): return lax.ppermute(v, 'rows', [(i, i ^ bit) for i in range(nrows)])]
    pallas_call x26 -> x23, Pallas kernels: 273 us -> 314 us  [call(): return lambda *args: fn(*args, *after, *into)]
    all_gather x1 -> x0, blocking collectives: 33.5 us -> none  [shards(): lax.all_gather(kern_bc, 'state', axis=2, tiled=True).reshape(5, 2 * NS)]
    unnamed x287 -> x135, local copies, waits for them, and re-layouts: 40.7 us -> 35.3 us
  transfers between devices with their start and end apart: 121 -> 66, of which waited for: 43 -> 18; matrix products, arithmetic and copies ran while one was open for 16% -> 21% of each run, Pallas kernels for 11% -> 39%
where the time goes in v2:
time: 820 us; the launch traced here: 811 us
  Pallas kernels  314 us (38%)
  waiting for transfers between devices  180 us (22%)
  starting transfers between devices  114 us (14%)
  local copies, waits for them, and re-layouts  90.5 us (11%)
  other arithmetic  88.8 us (11%)
  between operations  22.3 us (3%)
    pallas_call x23, Pallas kernels, call(): return lambda *args: fn(*args, *after, *into)  314 us
    ppermute x4, waiting for transfers between devices, states_sum(): lax.ppermute(v.astype(bf16), 'zline', [(i, i ^ bit) for i in range(groups)])  76.3 us
    ppermute x17, waiting for transfers between devices, swap(): return lax.ppermute(v, 'pair', [(0, 1), (1, 0)])  66.4 us
    ppermute x6, starting transfers between devices, line_sum(): v = v + lax.ppermute(v, 'zline', [(i, i ^ bit) for i in range(groups)])  41.3 us
    unnamed x135, local copies, waits for them, and re-layouts  35.3 us
    ppermute x24, waiting for transfers between devices, cross(): return lax.ppermute(v, 'rows', [(i, i ^ bit) for i in range(nrows)])  28.6 us
    ppermute x3, starting transfers between devices, step(): lax.ppermute(send_u, 'zline', [(i, i + 1) for i in range(groups - d)])  22.8 us
    ppermute x17, starting transfers between devices, swap(): return lax.ppermute(v, 'pair', [(0, 1), (1, 0)])  20.2 us
  transfers between devices with their start and end apart: 66, of which 18 were waited for; matrix products, arithmetic and copies ran while one was open for 21% of the time, Pallas kernels for 39%

profile of v2, /device:TPU:0, one launch (start us, length us, event | category | flops | bytes accessed | tf_op | source)
XLA Modules:
  0.0 811.5 jit_solution(4139168779084330471)
XLA Ops:
  46.4 11.9 %shard_map.271 = (bf16[2048,2048]{1,0:T(8,128)(2,1)}, f32[2048,128]{1,0:T(8,128)}, bf16[2048,512]{1,0:T(8,128)(2,1)}, bf16[2048,512]{1,0:T(8,128)(2,1)}, bf16[20...) custom-call(s32[1]{0:T(128)} %bitcast.refs_0_, bf16[4096,2048]{1,0:T(8,128)(2,1)} %refs_1_.5, ...), custom_call_target="tpu_custom_call" | custom-call | flops 4294967296 | bytes 20971520 | tf_op jit(solution)/shard_map/pallas_call | solution.py:480
  73.0 11.9 %shard_map.272 = (bf16[2048,2048]{1,0:T(8,128)(2,1)}, f32[2048,128]{1,0:T(8,128)}, bf16[2048,512]{1,0:T(8,128)(2,1)}, bf16[2048,512]{1,0:T(8,128)(2,1)}, bf16[20...) custom-call(s32[1]{0:T(128)} %bitcast.refs_0_, ...), custom_call_target="tpu_custom_call", output_to_operand_aliasing={{0}: (11, {}), {1}: (12, {}), {2}: (13, {}), {3}: (14, {}),... | custom-call | flops 4294967296 | bytes 20971520 | tf_op jit(solution)/shard_map/pallas_call | solution.py:480
  86.3 10.7 %collective-permute-done.7 = bf16[1024,1024]{1,0:T(8,128)(2,1)S(1)} collective-permute-done((bf16[1024,1024]{1,0:T(8,128)(2,1)}, bf16[1024,1024]{1,0:T(8,128)(2,1)S(1)}, u32[]{:S(2)}, u32[]{:S(2)}) %collective-permute-start.7) | collective-permute-done | bytes 2097184 | tf_op jit(solution)/shard_map/ppermute | solution.py:520
  97.0 15.6 %shard_map.273 = (f32[2048,256]{1,0:T(8,128)}, f32[2048,256]{1,0:T(8,128)}, bf16[2048,256]{1,0:T(8,128)(2,1)}, f32[2048,128]{1,0:T(8,128)}, f32[2048,128]{1,0:T(...) custom-call(bf16[2048,2048]{1,0:T(8,128)(2,1)} %get-tuple-element.106.refs_0_.refs_1_.refs_2_, ...), custom_call_target="tpu_custom_call" | custom-call | flops 4294967296 | bytes 18874368 | tf_op jit(solution)/shard_map/pallas_call | solution.py:480
  123.5 16.2 %shard_map.274 = (f32[2048,512]{1,0:T(8,128)}, bf16[2048,512]{1,0:T(8,128)(2,1)}, f32[8,128,512]{2,1,0:T(8,128)}, f32[2048,128]{1,0:T(8,128)}) custom-call(bf16[2048,512]{1,0:T(8,128)(2,1)} %get-tuple-element.104.refs_0_.refs_10_, bf16[2048,512]{1,0:T(8,128)(2,1)} %get-tuple-element.105.refs_1_.refs_5_, ...), custom_call_target="tpu_custom_call" | custom-call | flops 10737418240 | bytes 20971520 | tf_op jit(solution)/shard_map/pallas_call | solution.py:480
  144.4 9.9 %collective-permute-done.9 = bf16[256,2048]{1,0:T(8,128)(2,1)S(1)} collective-permute-done((bf16[256,2048]{1,0:T(8,128)(2,1)}, bf16[256,2048]{1,0:T(8,128)(2,1)S(1)}, u32[]{:S(2)}, u32[]{:S(2)}) %collective-permute-start.9) | collective-permute-done | bytes 1048608 | tf_op jit(solution)/shard_map/ppermute | solution.py:520
  158.6 18.0 %shard_map.275 = (bf16[2048,512]{1,0:T(8,128)(2,1)}, bf16[2048,512]{1,0:T(8,128)(2,1)}, bf16[2048,512]{1,0:T(8,128)(2,1)}, bf16[2048,512]{1,0:T(8,128)(2,1)}) custom-call(bf16[2048,2048]{1,0:T(8,128)(2,1)} %get-tuple-element.106.refs_0_.refs_1_.refs_2_, bf16[2048,1024]{1,0:T(8,128)(2,1)} %pad_maximum_fusion.refs_1_.refs_4_, f32[8,512]{1,0:T(8,128)} %copy-done.51, ...), custom_call_target="tpu_custom_call" | custom-call | flops 8589934592 | bytes 29360128 | tf_op jit(solution)/shard_map/pallas_call | solution.py:480
  176.7 16.4 %shard_map.276 = (f32[2048,512]{1,0:T(8,128)}, bf16[2048,512]{1,0:T(8,128)(2,1)}, f32[8,128,512]{2,1,0:T(8,128)}, f32[2048,128]{1,0:T(8,128)}) custom-call(bf16[2048,512]{1,0:T(8,128)(2,1)} %get-tuple-element.114.refs_0_.refs_7_.refs_11_, bf16[2048,512]{1,0:T(8,128)(2,1)} %get-tuple-element.115.refs_1_.refs_6_, ...), custom_call_target="tpu_custom_call" | custom-call | flops 10737418240 | bytes 20971520 | tf_op jit(solution)/shard_map/pallas_call | solution.py:480
  199.6 9.2 %shard_map.277 = (bf16[1024,512]{1,0:T(8,128)(2,1)}, bf16[1024,512]{1,0:T(8,128)(2,1)}, f32[1024,128]{1,0:T(8,128)}) custom-call(bf16[1024,2048]{1,0:T(8,128)(2,1)} %all-gather.5.cloned.1.call-done.refs_0_.refs_2_, bf16[512,2048]{1,0:T(8,128)(2,1)} %refs_2_.3, bf16[512,2048]{1,0:T(8,128)(2,1)} %pad_maximum_fusion.2.refs_2_.refs_3_, ...), custom_call_target="tpu_custom_call" | custom-call | flops 4294967296 | bytes 12582912 | tf_op jit(solution)/shard_map/pallas_call | solution.py:480
  214.5 8.6 %shard_map.278.refs_9_ = bf16[1024,2048]{1,0:T(8,128)(2,1)} custom-call(bf16[2048,512]{1,0:T(8,128)(2,1)} %get-tuple-element.112.refs_3_.refs_0_, bf16[2048,512]{1,0:T(8,128)(2,1)} %get-tuple-element.116.refs_4_.refs_1_, bf16[512,2048]{1,0:T(8,128)(2,1)} %refs_2_.3, bf16[512,2048]{1,0:T(8,128)(2,1)} %pad_maximum_fusion.2.refs_2_.refs_3_, ...), custom_call_target="tpu_custom_call" | custom-call | flops 4294967296 | bytes 10485760 | tf_op jit(solution)/shard_map/pallas_call | solution.py:480
  230.6 8.7 %shard_map.279 = (bf16[1024,1024]{1,0:T(8,128)(2,1)}, bf16[1024,1024]{1,0:T(8,128)(2,1)}, bf16[1024,1024]{1,0:T(8,128)(2,1)}, f32[1024,128]{1,0:T(8,128)}, f32[8,1024]{1,0:T(8,128)}) custom-call(f32[1024,128]{1,0:T(8,128)} %get-tuple-element.281.refs_0_, bf16[1024,512]{1,0:T(8,128)(2,1)} %get-tuple-element.119.refs_1_, ...), custom_call_target="tpu_custom_call" | custom-call | flops 2097152000 | bytes 20971520 | tf_op jit(solution)/shard_map/pallas_call | solution.py:480
  241.4 32.4 %shard_map.280 = (bf16[1024,1024]{1,0:T(8,128)(2,1)}, bf16[1024,128]{1,0:T(8,128)(2,1)}, bf16[1024,256]{1,0:T(8,128)(2,1)}, f32[1024,128]{1,0:T(8,128)}, f32[2,4...) custom-call(bf16[1024,1024]{1,0:T(8,128)(2,1)} %get-tuple-element.12, ...), custom_call_target="tpu_custom_call" | custom-call | flops 42949672960 | bytes 41943040 | tf_op jit(solution)/shard_map/pallas_call | solution.py:480
  275.1 14.9 %shard_map.281.refs_5_ = bf16[1024,2048]{1,0:T(8,128)(2,1)} custom-call(bf16[1024,1024]{1,0:T(8,128)(2,1)} %get-tuple-element.123.refs_0_.refs_4_, bf16[1024,1024]{1,0:T(8,128)(2,1)} %get-tuple-element.133.refs_1_.refs_4_, bf16[1024,128]{1,0:T(8,128)(2,1)} %get-tuple-element.134.refs_2_, bf16[2048,1024]{1,0:T(8,128)(2,1)} %bitcast.110, ...), custom_call_target="tpu_custom_call" | custom-call | flops 8589934592 | bytes 16777216 | tf_op jit(solution)/shard_map/pallas_call | solution.py:480
  290.5 9.5 %shard_map.282 = (bf16[1024,512]{1,0:T(8,128)(2,1)}, bf16[1024,512]{1,0:T(8,128)(2,1)}, f32[1024,128]{1,0:T(8,128)}) custom-call(bf16[1024,2048]{1,0:T(8,128)(2,1)} %all-gather.3.cloned.1.call-done.refs_0_.refs_1_, bf16[512,2048]{1,0:T(8,128)(2,1)} %refs_2_.3, bf16[512,2048]{1,0:T(8,128)(2,1)} %pad_maximum_fusion.2.refs_2_.refs_3_, ...), custom_call_target="tpu_custom_call" | custom-call | flops 4294967296 | bytes 12582912 | tf_op jit(solution)/shard_map/pallas_call | solution.py:480
  318.7 8.6 %shard_map.283.refs_9_ = bf16[1024,2048]{1,0:T(8,128)(2,1)} custom-call(bf16[2048,512]{1,0:T(8,128)(2,1)} %get-tuple-element.112.refs_3_.refs_0_, bf16[2048,512]{1,0:T(8,128)(2,1)} %get-tuple-element.116.refs_4_.refs_1_, bf16[512,2048]{1,0:T(8,128)(2,1)} %refs_2_.3, bf16[512,2048]{1,0:T(8,128)(2,1)} %pad_maximum_fusion.2.refs_2_.refs_3_, ...), custom_call_target="tpu_custom_call" | custom-call | flops 4294967296 | bytes 10485760 | tf_op jit(solution)/shard_map/pallas_call | solution.py:480
  327.3 8.8 %shard_map.284 = (bf16[1024,1024]{1,0:T(8,128)(2,1)}, bf16[1024,1024]{1,0:T(8,128)(2,1)}, bf16[1024,1024]{1,0:T(8,128)(2,1)}, f32[1024,128]{1,0:T(8,128)}, f32[8,1024]{1,0:T(8,128)}) custom-call(f32[1024,128]{1,0:T(8,128)} %get-tuple-element.279.refs_0_, bf16[1024,512]{1,0:T(8,128)(2,1)} %get-tuple-element.137.refs_1_, ...), custom_call_target="tpu_custom_call" | custom-call | flops 2097152000 | bytes 20971520 | tf_op jit(solution)/shard_map/pallas_call | solution.py:480
  336.1 15.5 %shard_map.285 = (f32[1024,1024]{1,0:T(8,128)}, f32[1024,1024]{1,0:T(8,128)}) custom-call(s32[1]{0:T(128)} %bitcast.33.refs_0_, bf16[1024,2048]{1,0:T(8,128)(2,1)} %all-gather.3.cloned.1.call-done.refs_0_.refs_1_, bf16[1024,2048]{1,0:T(8,128)(2,1)} %all-gather.5.cloned.1.call-done.refs_0_.refs_2_, bf16[1024,1024]{1,0:T(8,128)(2,1)} %get-tuple-element.140.refs_3_, ...), custom_call_target="tpu_custom_call" | custom-call | flops 65536 | bytes 65536 | tf_op jit(solution)/shard_map/pallas_call | solution.py:480
  351.6 15.6 %shard_map.286 = (f32[1024,1024]{1,0:T(8,128)}, f32[1024,1024]{1,0:T(8,128)}) custom-call(s32[1]{0:T(128)} %bitcast.33.refs_0_, bf16[2048,2048]{1,0:T(8,128)(2,1)} %get-tuple-element.106.refs_0_.refs_1_.refs_2_, bf16[2048,2048]{1,0:T(8,128)(2,1)} %get-tuple-element.106.refs_0_.refs_1_.refs_2_, bf16[1024,1024]{1,0:T(8,128)(2,1)} %get-tuple-element.139.refs_3_.refs_0_, ...), custom_call_target="tpu_custom_call" | custom-call | flops 65536 | bytes 65536 | tf_op jit(solution)/shard_map/pallas_call | solution.py:480
  381.9 17.3 %collective-permute-start.19 = (bf16[1024,512]{1,0:T(8,128)(2,1)}, bf16[1024,512]{1,0:T(8,128)(2,1)}, u32[]{:S(2)}, u32[]{:S(2)}) collective-permute-start(bf16[1024,512]{1,0:T(8,128)(2,1)} %get-tuple-element.255), channel_id=1, source_target_pairs={{0,2},{2,4},{4,6},{1,3},{3,5},{5,7},{8,10},{10,12},{12,14},{9,11},... | collective-permute-start | bytes 3145736 | tf_op jit(solution)/shard_map/ppermute | solution.py:717
  400.2 32.4 %shard_map.287 = (bf16[1024,1024]{1,0:T(8,128)(2,1)}, bf16[1024,128]{1,0:T(8,128)(2,1)}, bf16[1024,256]{1,0:T(8,128)(2,1)}, f32[1024,128]{1,0:T(8,128)}, f32[2,4...) custom-call(bf16[1024,1024]{1,0:T(8,128)(2,1)} %get-tuple-element.14, ...), custom_call_target="tpu_custom_call" | custom-call | flops 42949672960 | bytes 41943040 | tf_op jit(solution)/shard_map/pallas_call | solution.py:480
  435.0 37.9 %collective-permute-start.30 = (f32[2048]{0:T(1024)S(1)}, f32[2048]{0:T(1024)S(1)}, u32[]{:S(2)}, u32[]{:S(2)}) collective-permute-start(f32[2048]{0:T(1024)S(1)} %pad_maximum_fusion.20), channel_id=1, source_target_pairs={{0,2},{2,0},{4,6},{6,4},{1,3},{3,1},{5,7},{7,5},{8,10},{10,8},{12,... | collective-permute-start | bytes 24584 | tf_op jit(solution)/shard_map/ppermute | solution.py:528
  500.3 16.6 %collective-permute-done.36 = bf16[1024,512]{1,0:T(8,128)(2,1)S(1)} collective-permute-done((bf16[1024,512]{1,0:T(8,128)(2,1)S(1)}, bf16[1024,512]{1,0:T(8,128)(2,1)S(1)}, u32[]{:S(2)}, u32[]{:S(2)}) %collective-permute-start.36) | collective-permute-done | bytes 1048608 | tf_op jit(solution)/shard_map/ppermute | solution.py:520
  520.4 14.9 %shard_map.288.refs_5_ = bf16[1024,2048]{1,0:T(8,128)(2,1)} custom-call(bf16[1024,1024]{1,0:T(8,128)(2,1)} %get-tuple-element.139.refs_3_.refs_0_, bf16[1024,1024]{1,0:T(8,128)(2,1)} %get-tuple-element.150.refs_1_.refs_3_, bf16[1024,128]{1,0:T(8,128)(2,1)} %get-tuple-element.151.refs_2_, bf16[2048,1024]{1,0:T(8,128)(2,1)} %bitcast.111, ...), custom_call_target="tpu_custom_call" | custom-call | flops 8589934592 | bytes 16777216 | tf_op jit(solution)/shard_map/pallas_call | solution.py:480
  548.4 15.6 %shard_map.289 = (f32[1024,1024]{1,0:T(8,128)}, f32[1024,1024]{1,0:T(8,128)}) custom-call(s32[1]{0:T(128)} %bitcast.33.refs_0_, bf16[2048,2048]{1,0:T(8,128)(2,1)} %get-tuple-element.106.refs_0_.refs_1_.refs_2_, bf16[2048,2048]{1,0:T(8,128)(2,1)} %get-tuple-element.106.refs_0_.refs_1_.refs_2_, bf16[1024,1024]{1,0:T(8,128)(2,1)} %get-tuple-element.150.refs_1_.refs_3_, ...), custom_call_target="tpu_custom_call" | custom-call | flops 65536 | bytes 65536 | tf_op jit(solution)/shard_map/pallas_call | solution.py:480
  586.8 11.9 %collective-permute-done.24 = bf16[1024,256]{1,0:T(8,128)(2,1)} collective-permute-done((bf16[1024,256]{1,0:T(8,128)(2,1)}, bf16[1024,256]{1,0:T(8,128)(2,1)}, u32[]{:S(2)}, u32[]{:S(2)}) %collective-permute-start.24) | collective-permute-done | bytes 524320 | tf_op jit(solution)/shard_map/ppermute | solution.py:809
  601.2 42.4 %collective-permute-done.26 = bf16[1024,256]{1,0:T(8,128)(2,1)} collective-permute-done((bf16[1024,256]{1,0:T(8,128)(2,1)}, bf16[1024,256]{1,0:T(8,128)(2,1)}, u32[]{:S(2)}, u32[]{:S(2)}) %collective-permute-start.26) | collective-permute-done | bytes 524320 | tf_op jit(solution)/shard_map/ppermute | solution.py:809
  648.8 22.0 %collective-permute-done.27 = bf16[1024,256]{1,0:T(8,128)(2,1)} collective-permute-done((bf16[1024,256]{1,0:T(8,128)(2,1)}, bf16[1024,256]{1,0:T(8,128)(2,1)}, u32[]{:S(2)}, u32[]{:S(2)}) %collective-permute-start.27) | collective-permute-done | bytes 524320 | tf_op jit(solution)/shard_map/ppermute | solution.py:809
  693.9 9.7 %shard_map.292 = (f32[1024,256]{1,0:T(8,128)}, f32[1024,256]{1,0:T(8,128)}) custom-call(s32[1]{0:T(128)} %bitcast.33.refs_0_, bf16[2048,2048]{1,0:T(8,128)(2,1)} %get-tuple-element.106.refs_0_.refs_1_.refs_2_, bf16[2048,256]{1,0:T(8,128)(2,1)} %concatenate.143.refs_2_, f32[8,128]{1,0:T(8,128)} %get-tuple-element.169.refs_3_), custom_call_target="tpu_custom_call" | custom-call | flops 65536 | bytes 65536 | tf_op jit(solution)/shard_map/pallas_call | solution.py:480
  710.4 22.8 %collective-permute-done.53 = f32[5,256]{1,0:T(8,128)S(1)} collective-permute-done((f32[5,256]{1,0:T(8,128)S(1)}, f32[5,256]{1,0:T(8,128)S(1)}, u32[]{:S(2)}, u32[]{:S(2)}) %collective-permute-start.53) | collective-permute-done | bytes 5152 | tf_op jit(solution)/shard_map/ppermute | solution.py:520
  747.4 7.6 collective-permute-done.42
  760.1 10.7 %collective-permute-done.48 = bf16[512,128]{1,0:T(8,128)(2,1)S(1)} collective-permute-done((bf16[512,128]{1,0:T(8,128)(2,1)S(1)}, bf16[512,128]{1,0:T(8,128)(2,1)S(1)}, u32[]{:S(2)}, u32[]{:S(2)}) %collective-permute-start.48) | collective-permute-done | bytes 131104 | tf_op jit(solution)/shard_map/ppermute | solution.py:523
  778.2 9.9 %shard_map.293 = f32[16384,128]{1,0:T(8,128)} custom-call(s32[1]{0:T(128)} %bitcast.33.refs_0_, bf16[1024,512]{1,0:T(8,128)(2,1)} %pad_maximum_fusion.8.refs_1_, bf16[1024,512]{1,0:T(8,128)(2,1)} %collective-permute-done.39.refs_2_, bf16[1024,512]{1,0:T(8,128)(2,1)} %pad_maximum_fusion.9.refs_3_, bf16[1024,512]{1,0:T(8,128)(2,1)} %collective-permute-done.44.refs_4_, ...), custom_call_target="tpu_custom_call" | custom-call | bytes 25165824 | tf_op jit(solution)/shard_map/pallas_call | solution.py:480
  (454 shorter events, 274.9 us)
Async XLA Ops:
  7.2 192.4 %all-gather.5.cloned.1.call-start = ((), (), s32[]{:S(2)}) async-start(), calls=%async_computation.4 | async-start | bytes 5242880 | tf_op jit(solution)/shard_map/all_gather | solution.py:728
  32.7 30.3 %collective-permute-start.3 = (bf16[2,32,2176]{2,1,0:T(8,128)(2,1)S(1)}, bf16[2,32,2176]{2,1,0:T(8,128)(2,1)S(1)}, u32[]{:S(2)}, u32[]{:S(2)}) collective-permute-start(bf16[2,32,2176]{2,1,0:T(8,128)(2,1)S(1)} %pad_maximum_fusion.12.refs_7_), channel_id=1, source_target_pairs={{0,2},{2,4},{4,6},{6,0},{1,3},{3,5},{5,7},{7,1},{8,10},{10,12},{12... | collective-permute-start | bytes 835592 | tf_op jit(solution)/shard_map/ppermute | solution.py:596
  44.3 52.7 %collective-permute-start.7 = (bf16[1024,1024]{1,0:T(8,128)(2,1)}, bf16[1024,1024]{1,0:T(8,128)(2,1)S(1)}, u32[]{:S(2)}, u32[]{:S(2)}) collective-permute-start(bf16[1024,1024]{1,0:T(8,128)(2,1)} %constant_dynamic-slice_fusion.12), channel_id=1, source_target_pairs={{0,1},{1,0},{2,3},{3,2},{4,5},{5,4},{6,7},{7,6},{8,9},{9,8},{10,11... | collective-permute-start | bytes 6291464 | tf_op jit(solution)/shard_map/ppermute | solution.py:520
  62.4 228.1 %all-gather.3.cloned.1.call-start = ((), (), s32[]{:S(2)}) async-start(), calls=%async_computation.3 | async-start | bytes 5242880 | tf_op jit(solution)/shard_map/all_gather | solution.py:728
  97.0 57.2 %collective-permute-start.8 = (bf16[1024,1024]{1,0:T(8,128)(2,1)S(1)}, bf16[1024,1024]{1,0:T(8,128)(2,1)}, u32[]{:S(2)}, u32[]{:S(2)}) collective-permute-start(bf16[1024,1024]{1,0:T(8,128)(2,1)S(1)} %collective-permute-done.7), channel_id=1, source_target_pairs={{0,8},{8,0},{16,24},{24,16},{1,9},{9,1},{17,25},{25,17},{2,10},{10... | collective-permute-start | bytes 6291464 | tf_op jit(solution)/shard_map/ppermute | solution.py:523
  122.4 31.9 %collective-permute-start.9 = (bf16[256,2048]{1,0:T(8,128)(2,1)}, bf16[256,2048]{1,0:T(8,128)(2,1)S(1)}, u32[]{:S(2)}, u32[]{:S(2)}) collective-permute-start(bf16[256,2048]{1,0:T(8,128)(2,1)} %constant_dynamic-slice_fusion.11), channel_id=1, source_target_pairs={{0,1},{1,0},{2,3},{3,2},{4,5},{5,4},{6,7},{7,6},{8,9},{9,8},{10,11... | collective-permute-start | bytes 3145736 | tf_op jit(solution)/shard_map/ppermute | solution.py:520
  144.1 376.3 %reduce-scatter.6.cloned.1.call-start = ((), (), s32[]{:S(2)}) async-start(), calls=%async_computation.6 | async-start | bytes 5242880 | tf_op jit(solution)/shard_map/reduce_scatter | solution.py:856
  154.3 42.4 %collective-permute-start.10 = (bf16[256,2048]{1,0:T(8,128)(2,1)S(1)}, bf16[256,2048]{1,0:T(8,128)(2,1)}, u32[]{:S(2)}, u32[]{:S(2)}) collective-permute-start(bf16[256,2048]{1,0:T(8,128)(2,1)S(1)} %collective-permute-done.9), channel_id=1, source_target_pairs={{0,8},{8,0},{16,24},{24,16},{1,9},{9,1},{17,25},{25,17},{2,10},{10... | collective-permute-start | bytes 3145736 | tf_op jit(solution)/shard_map/ppermute | solution.py:523
  227.2 46.6 %collective-permute-start.14 = (bf16[1024,512]{1,0:T(8,128)(2,1)S(1)}, bf16[1024,512]{1,0:T(8,128)(2,1)S(1)}, u32[]{:S(2)}, u32[]{:S(2)}) collective-permute-start(bf16[1024,512]{1,0:T(8,128)(2,1)S(1)} %get-tuple-element.257), channel_id=1, source_target_pairs={{0,2},{1,3},{8,10},{9,11},{16,18},{17,19},{24,26},{25,27}} | collective-permute-start | bytes 3145736 | tf_op jit(solution)/shard_map/ppermute | solution.py:717
  229.6 44.2 %collective-permute-start.15 = (bf16[1024,512]{1,0:T(8,128)(2,1)S(1)}, bf16[1024,512]{1,0:T(8,128)(2,1)S(1)}, u32[]{:S(2)}, u32[]{:S(2)}) collective-permute-start(bf16[1024,512]{1,0:T(8,128)(2,1)S(1)} %get-tuple-element.258), channel_id=1, source_target_pairs={{6,4},{7,5},{14,12},{15,13},{22,20},{23,21},{30,28},{31,29}} | collective-permute-start | bytes 3145736 | tf_op jit(solution)/shard_map/ppermute | solution.py:718
  290.1 355.6 %reduce-scatter.4.cloned.1.call-start = ((), (), s32[]{:S(2)}) async-start(), calls=%async_computation.5 | async-start | bytes 5242880 | tf_op jit(solution)/shard_map/reduce_scatter | solution.py:856
  314.8 56.8 %collective-permute-start.18 = (bf16[1024,512]{1,0:T(8,128)(2,1)}, bf16[1024,512]{1,0:T(8,128)(2,1)S(1)}, u32[]{:S(2)}, u32[]{:S(2)}) collective-permute-start(bf16[1024,512]{1,0:T(8,128)(2,1)} %add_convert_fusion.3), channel_id=1, source_target_pairs={{0,2},{2,4},{1,3},{3,5},{8,10},{10,12},{9,11},{11,13},{16,18},{18,... | collective-permute-start | bytes 3145736 | tf_op jit(solution)/shard_map/ppermute | solution.py:717
  318.2 62.7 %collective-permute-start.23 = (f32[2048]{0:T(1024)S(1)}, f32[2048]{0:T(1024)S(1)}, u32[]{:S(2)}, u32[]{:S(2)}) collective-permute-start(f32[2048]{0:T(1024)S(1)} %slice_reduce_fusion), channel_id=1, source_target_pairs={{0,1},{1,0},{2,3},{3,2},{4,5},{5,4},{6,7},{7,6},{8,9},{9,8},{10,11... | collective-permute-start | bytes 24584 | tf_op jit(solution)/shard_map/ppermute | solution.py:520
  381.1 391.4 %reduce-scatter.8.cloned.1.call-start = ((), (), s32[]{:S(2)}) async-start(), calls=%async_computation.7 | async-start | bytes 5242880 | tf_op jit(solution)/shard_map/reduce_scatter | solution.py:856
  381.2 95.1 %collective-permute-start.56 = (f32[1024,1024]{1,0:T(8,128)}, f32[1024,1024]{1,0:T(8,128)}, u32[]{:S(2)}, u32[]{:S(2)}) collective-permute-start(f32[1024,1024]{1,0:T(8,128)} %get-tuple-element.143.refs_5_), channel_id=1, source_target_pairs={{0,8},{8,0},{16,24},{24,16},{1,9},{9,1},{17,25},{25,17},{2,10},{10... | collective-permute-start | bytes 12582920 | tf_op jit(solution)/shard_map/ppermute | solution.py:523
  381.2 105.4 %collective-permute-start.35 = (f32[1024,1024]{1,0:T(8,128)}, f32[1024,1024]{1,0:T(8,128)}, u32[]{:S(2)}, u32[]{:S(2)}) collective-permute-start(f32[1024,1024]{1,0:T(8,128)} %get-tuple-element.149.refs_25_), channel_id=1, source_target_pairs={{0,8},{8,0},{16,24},{24,16},{1,9},{9,1},{17,25},{25,17},{2,10},{10... | collective-permute-start | bytes 12582920 | tf_op jit(solution)/shard_map/ppermute | solution.py:523
  381.9 184.1 %collective-permute-start.19 = (bf16[1024,512]{1,0:T(8,128)(2,1)}, bf16[1024,512]{1,0:T(8,128)(2,1)}, u32[]{:S(2)}, u32[]{:S(2)}) collective-permute-start(bf16[1024,512]{1,0:T(8,128)(2,1)} %get-tuple-element.255), channel_id=1, source_target_pairs={{0,2},{2,4},{4,6},{1,3},{3,5},{5,7},{8,10},{10,12},{12,14},{9,11},... | collective-permute-start | bytes 3145736 | tf_op jit(solution)/shard_map/ppermute | solution.py:717
  435.0 58.9 %collective-permute-start.30 = (f32[2048]{0:T(1024)S(1)}, f32[2048]{0:T(1024)S(1)}, u32[]{:S(2)}, u32[]{:S(2)}) collective-permute-start(f32[2048]{0:T(1024)S(1)} %pad_maximum_fusion.20), channel_id=1, source_target_pairs={{0,2},{2,0},{4,6},{6,4},{1,3},{3,1},{5,7},{7,5},{8,10},{10,8},{12,... | collective-permute-start | bytes 24584 | tf_op jit(solution)/shard_map/ppermute | solution.py:528
  490.0 26.9 %collective-permute-start.36 = (bf16[1024,512]{1,0:T(8,128)(2,1)S(1)}, bf16[1024,512]{1,0:T(8,128)(2,1)S(1)}, u32[]{:S(2)}, u32[]{:S(2)}) collective-permute-start(bf16[1024,512]{1,0:T(8,128)(2,1)S(1)} %slice.356), channel_id=1, source_target_pairs={{0,1},{1,0},{2,3},{3,2},{4,5},{5,4},{6,7},{7,6},{8,9},{9,8},{10,11... | collective-permute-start | bytes 3145736 | tf_op jit(solution)/shard_map/ppermute | solution.py:520
  492.3 73.7 %collective-permute-start.21 = (bf16[1024,512]{1,0:T(8,128)(2,1)}, bf16[1024,512]{1,0:T(8,128)(2,1)}, u32[]{:S(2)}, u32[]{:S(2)}) collective-permute-start(bf16[1024,512]{1,0:T(8,128)(2,1)} %add_convert_fusion), channel_id=1, source_target_pairs={{2,0},{4,2},{6,4},{3,1},{5,3},{7,5},{10,8},{12,10},{14,12},{11,9},... | collective-permute-start | bytes 3145736 | tf_op jit(solution)/shard_map/ppermute | solution.py:718
  518.1 26.7 %collective-permute-start.37 = (bf16[512,512]{1,0:T(8,128)(2,1)}, bf16[512,512]{1,0:T(8,128)(2,1)}, u32[]{:S(2)}, u32[]{:S(2)}) collective-permute-start(bf16[512,512]{1,0:T(8,128)(2,1)} %dynamic-slice_convert_fusion.4), channel_id=1, source_target_pairs={{0,16},{8,24},{16,0},{24,8},{1,17},{9,25},{17,1},{25,9},{2,18},{10... | collective-permute-start | bytes 1572872 | tf_op jit(solution)/shard_map/ppermute | solution.py:523
  544.8 28.0 %collective-permute-start.60 = (bf16[1024,512]{1,0:T(8,128)(2,1)}, bf16[1024,512]{1,0:T(8,128)(2,1)}, u32[]{:S(2)}, u32[]{:S(2)}) collective-permute-start(bf16[1024,512]{1,0:T(8,128)(2,1)} %pad_maximum_fusion.11), channel_id=1, source_target_pairs={{0,8},{8,0},{16,24},{24,16},{1,9},{9,1},{17,25},{25,17},{2,10},{10... | collective-permute-start | bytes 3145736 | tf_op jit(solution)/shard_map/ppermute | solution.py:523
  563.9 140.0 %collective-permute-start.40 = (f32[1024,1024]{1,0:T(8,128)}, f32[1024,1024]{1,0:T(8,128)}, u32[]{:S(2)}, u32[]{:S(2)}) collective-permute-start(f32[1024,1024]{1,0:T(8,128)} %get-tuple-element.158.refs_7_), channel_id=1, source_target_pairs={{0,8},{8,0},{16,24},{24,16},{1,9},{9,1},{17,25},{25,17},{2,10},{10... | collective-permute-start | bytes 12582920 | tf_op jit(solution)/shard_map/ppermute | solution.py:523
  566.0 32.7 %collective-permute-start.24 = (bf16[1024,256]{1,0:T(8,128)(2,1)}, bf16[1024,256]{1,0:T(8,128)(2,1)}, u32[]{:S(2)}, u32[]{:S(2)}) collective-permute-start(bf16[1024,256]{1,0:T(8,128)(2,1)} %broadcast_add_fusion.1), channel_id=1, source_target_pairs={{0,2},{2,0},{4,6},{6,4},{1,3},{3,1},{5,7},{7,5},{8,10},{10,8},{12,... | collective-permute-start | bytes 1572872 | tf_op jit(solution)/shard_map/ppermute | solution.py:809
  566.1 77.5 %collective-permute-start.26 = (bf16[1024,256]{1,0:T(8,128)(2,1)}, bf16[1024,256]{1,0:T(8,128)(2,1)}, u32[]{:S(2)}, u32[]{:S(2)}) collective-permute-start(bf16[1024,256]{1,0:T(8,128)(2,1)} %broadcast_add_fusion), channel_id=1, source_target_pairs={{0,2},{2,0},{4,6},{6,4},{1,3},{3,1},{5,7},{7,5},{8,10},{10,8},{12,... | collective-permute-start | bytes 1572872 | tf_op jit(solution)/shard_map/ppermute | solution.py:809
  570.3 137.9 %collective-permute-start.31 = (f32[2048]{0:T(1024)S(1)}, f32[2048]{0:T(1024)S(1)}, u32[]{:S(2)}, u32[]{:S(2)}) collective-permute-start(f32[2048]{0:T(1024)S(1)} %fusion.26), channel_id=1, source_target_pairs={{0,4},{2,6},{4,0},{6,2},{1,5},{3,7},{5,1},{7,3},{8,12},{10,14},{12... | collective-permute-start | bytes 24584 | tf_op jit(solution)/shard_map/ppermute | solution.py:528
  572.8 205.4 %collective-permute-start.39 = (bf16[1024,512]{1,0:T(8,128)(2,1)}, bf16[1024,512]{1,0:T(8,128)(2,1)}, u32[]{:S(2)}, u32[]{:S(2)}) collective-permute-start(bf16[1024,512]{1,0:T(8,128)(2,1)} %pad_maximum_fusion.8.refs_1_), channel_id=1, source_target_pairs={{0,8},{8,0},{16,24},{24,16},{1,9},{9,1},{17,25},{25,17},{2,10},{10... | collective-permute-start | bytes 3145736 | tf_op jit(solution)/shard_map/ppermute | solution.py:523
  600.8 79.3 %collective-permute-start.25 = (bf16[1024,256]{1,0:T(8,128)(2,1)}, bf16[1024,256]{1,0:T(8,128)(2,1)}, u32[]{:S(2)}, u32[]{:S(2)}) collective-permute-start(bf16[1024,256]{1,0:T(8,128)(2,1)} %fusion.4), channel_id=1, source_target_pairs={{0,4},{2,6},{4,0},{6,2},{1,5},{3,7},{5,1},{7,3},{8,12},{10,14},{12... | collective-permute-start | bytes 1572872 | tf_op jit(solution)/shard_map/ppermute | solution.py:809
  670.8 123.5 %collective-permute-start.22 = (bf16[2048,256]{1,0:T(8,128)(2,1)}, bf16[2048,256]{1,0:T(8,128)(2,1)}, u32[]{:S(2)}, u32[]{:S(2)}) collective-permute-start(bf16[2048,256]{1,0:T(8,128)(2,1)} %dynamic-slice_convert_fusion), channel_id=1, source_target_pairs={{0,1},{1,0},{2,3},{3,2},{4,5},{5,4},{6,7},{7,6},{8,9},{9,8},{10,11... | collective-permute-start | bytes 3145736 | tf_op jit(solution)/shard_map/ppermute | solution.py:520
  703.6 31.2 %collective-permute-start.45 = (f32[1024,256]{1,0:T(8,128)}, f32[1024,256]{1,0:T(8,128)S(1)}, u32[]{:S(2)}, u32[]{:S(2)}) collective-permute-start(f32[1024,256]{1,0:T(8,128)} %get-tuple-element.170.refs_5_), channel_id=1, source_target_pairs={{0,8},{8,0},{16,24},{24,16},{1,9},{9,1},{17,25},{25,17},{2,10},{10... | collective-permute-start | bytes 3145736 | tf_op jit(solution)/shard_map/ppermute | solution.py:523
  707.4 28.4 %collective-permute-start.41 = (bf16[1024,512]{1,0:T(8,128)(2,1)S(1)}, bf16[1024,512]{1,0:T(8,128)(2,1)S(1)}, u32[]{:S(2)}, u32[]{:S(2)}) collective-permute-start(bf16[1024,512]{1,0:T(8,128)(2,1)S(1)} %slice.355), channel_id=1, source_target_pairs={{0,1},{1,0},{2,3},{3,2},{4,5},{5,4},{6,7},{7,6},{8,9},{9,8},{10,11... | collective-permute-start | bytes 3145736 | tf_op jit(solution)/shard_map/ppermute | solution.py:520
  741.9 47.7 %collective-permute-start.29 = (bf16[1024,256]{1,0:T(8,128)(2,1)}, bf16[1024,256]{1,0:T(8,128)(2,1)}, u32[]{:S(2)}, u32[]{:S(2)}) collective-permute-start(bf16[1024,256]{1,0:T(8,128)(2,1)} %dynamic-slice_convert_fusion.5), channel_id=1, source_target_pairs={{0,1},{1,0},{2,3},{3,2},{4,5},{5,4},{6,7},{7,6},{8,9},{9,8},{10,11... | collective-permute-start | bytes 1572872 | tf_op jit(solution)/shard_map/ppermute | solution.py:520
  (92 other events, 1100.8 us)
Sparse Core Ops, SparseCore 0:
  62.5 79.9 all-gather.4
  144.3 79.4 all-gather.2
  290.2 98.0 reduce-scatter.5
  390.5 99.6 reduce-scatter.3
  535.5 108.8 reduce-scatter.7

commit v3 on v2

--- a/solution.py
+++ b/solution.py
@@ -111,8 +111,9 @@
     tail[...] = buf[0:8, :]
 
 
-def second_kernel(normed, w, kern, msk, z, xp, a, xs, buf):
-    project_tile(normed[...], w, kern, msk, z, xp, a, xs, buf)
+def second_kernel(normed, w, kern, msk, start, z, xp, a, xs, tail, buf):
+    project_tile(normed[...], w, kern, msk, z, xp, a, xs, buf, start)
+    tail[...] = buf[0:8, :]
 
 
 def states_kernel(docl, normed, ws, kern, dtp, msk, bcp, bca, bc, dtr, dt, cum, cumt, buf):
@@ -150,13 +151,13 @@
     return lead, trail, retain
 
 
-def scan_kernel(docl, off, xs, z, bc, dt, cum, cumt, prm, y, gw, sin, pw, state):
+def scan_kernel(docl, off, xs, z, bc, dt, cum, cumt, prm, start, y, gw, sin, pw, state):
     lanes = xs.shape[1]
     heads = lanes // HD
 
     @pl.when(pl.program_id(0) == 0)
     def _():
-        state[...] = jnp.zeros_like(state)
+        state[...] = start[...]
 
     s_in = state[...]
     sin[0] = s_in
@@ -370,7 +371,7 @@
     mbuf[0:BLK, :] = msk[...]
     a = bca[...]
     sa = sigmoid(a)
-    da = dbc[...] * (sa * (1.0 + a * (1.0 - sa)))
+    da = dbc[...].astype(f32) * (sa * (1.0 + a * (1.0 - sa)))
     buf[BLK : BLK + 8, :] = buf[0:8, :]
     buf[0:BLK, :] = da
     xp = bcp[...]
@@ -385,11 +386,17 @@
     cm[...] = mbuf[0:8, :]
 
 
-def dn_kernel(dz, dxp, ddt, wa, wb, wdt, o):
+def dn_kernel(dz, dxp, ddt, dbc, wa, wb, wdt, o):
     n = wa.shape[1] // 2
+    wide = wa.shape[0]
     v = nt(dz[:, :n], wa[:, :n]) + nt(dxp[:, :n], wa[:, n:])
     v = v + nt(dz[:, n:], wb[:, :n]) + nt(dxp[:, n:], wb[:, n:])
-    o[...] = (v + nt(ddt[...], wdt[...])).astype(bf16)
+    o[:, :wide] = (v + nt(ddt[...], wdt[...])).astype(bf16)
+    cols = NS // pl.num_programs(0)
+    row, lane = iota((2 * NS, 128), 0), iota((2 * NS, 128), 1)
+    source = lane // cols * NS + pl.program_id(0) * cols + lane % cols
+    pick = ((row == source) & (lane < 2 * cols)).astype(bf16)
+    o[:, wide:] = nn(dbc[...], pick).astype(bf16)
 
 
 def weight_kernel(count, tiles, extra, core, *refs):
@@ -413,6 +420,10 @@
     @pl.when(step >= tiles)
     def _():
         give[...] = v
+
+
+def few_kernel(lhs, rhs, o):
+    o[...] = tn(rhs[...], lhs[...])
 
 
 def join_kernel(core, za, zb, xa, xb, o):
@@ -538,9 +549,10 @@
     def late(v, after):
         return v + zero_after(after).astype(v.dtype)
 
-    def half_of_partner(own, after):
+    def half_of_partner(own, after=None):
         half = own.shape[0] // 2
-        return swap(rows_of(own, core * half + zero_after(after), half))
+        at = core * half if after is None else core * half + zero_after(after)
+        return swap(rows_of(own, at, half))
 
     def with_other_half(got, after):
         other = cross(got, 1)
@@ -572,33 +584,14 @@
     pack = jnp.concatenate([w_bc.transpose(1, 2, 0), high, mid, low], axis=2)
     pack = jnp.pad(pack, ((0, 0), (0, 0), (0, 128 - 15)))
 
-    def grow(v, axis, bit, here):
-        got = lax.ppermute(v, axis, [(i, i ^ bit) for i in range(lax.axis_size(axis))])
-        return jnp.concatenate([jnp.where(here, got, v), jnp.where(here, v, got)], axis=1)
-
-    pack = grow(pack, "pair", 1, mine == 1)
+    pack = lax.all_gather(pack, ("zline", "pair"), axis=1, tiled=True)
     is0 = mine == 0
-    c_pair = [None] * CHUNKS
-
-    def cotangent_of(j, follow, after=None):
-        c_mine = rows_of(cotangent, mine * LEN + j * CT, CT)
-        c_got = swap(rows_of(cotangent, (1 - mine) * LEN + j * CT + zero_after(follow), CT))
-        low = is0 if after is None else mine + zero_after(after) == 0
-        return c_got, jnp.concatenate(
-            [jnp.where(low, c_mine, c_got), jnp.where(low, c_got, c_mine)], axis=1
-        )
-
-    c_got, c_pair[CHUNKS - 1] = cotangent_of(CHUNKS - 1, pack)
-    w_got = half_of_partner(w_a, pack)
+    w_half = rows_of(w_a, core * (dim // 2), dim // 2)
+    w_got = swap(w_half)
+    c_got = swap(rows_of(cotangent, (1 - mine) * LEN + zero_after(w_got), LEN))
     o_got = half_of_partner(w_out, w_got)
-    early = pack
-    turned = [
-        lax.ppermute(pack, "zline", [(i, (i + k) % groups) for i in range(groups)])
-        for k in range(groups - 1, 0, -1)
-    ]
-    pack = jnp.concatenate((turned + [pack]) * 2, axis=1)
-    size = 2 * w_bc.shape[2]
-    pack = lax.dynamic_slice_in_dim(pack, (groups - 1 - zpos) * size, groups * size, 1)
+    c_mine = rows_of(cotangent, mine * LEN, LEN)
+    c_mine = lax.all_gather(c_mine, "zline", axis=1, tiled=True)
     pack = pack.reshape(2 * NS, dim + 128)
     wbc = pack[:, :dim]
     taps = pack[:, dim : dim + 15].astype(f32).reshape(2 * NS, 3, 5).sum(axis=1)
@@ -618,31 +611,24 @@
     proj_shape = [sds((LEN, lanes), bf16)] * 4
     pf = 2 * LEN * dim * 2 * lanes
 
-    def first_step(part, start, after, into=()):
-        at = part * NBLK // 2
-        return ordered(
-            first_kernel,
-            NBLK // 2,
-            [
-                pl.BlockSpec((BLK, dim), lambda i, which: (which[0] * NBLK + at + i, 0)),
-                whole(1, dim),
-                whole(dim, 2 * lanes),
-                whole(8, lanes),
-                tile(128, at),
-                whole(8, lanes),
-            ],
-            [tile(dim, at), tile(128, at)] + [tile(lanes, at)] * 4 + [whole(8, lanes)],
-            [sds((LEN, dim), bf16), sds((LEN, 128), f32)] + proj_shape + [sds((8, lanes), f32)],
-            [pltpu.VMEM((BLK + 8, lanes), f32)],
-            flops=pf // 2,
-            moved=20 << 20,
-            prefetch=1,
-            after=after,
-            into=into,
-        )(which, hidden_in, norm_gain.reshape(1, dim), w_a, prm_a, msk, start)
-
-    *begun, tail = first_step(0, jnp.zeros((8, lanes), f32), (early,))
-    normed, r_wide, z_a, xp_a, a_a, xs_a, tail = first_step(1, tail, tuple(turned), begun)
+    normed, r_wide, z_a, xp_a, a_a, xs_a, tail = ordered(
+        first_kernel,
+        NBLK,
+        [
+            pl.BlockSpec((BLK, dim), lambda i, which: (which[0] * NBLK + i, 0)),
+            whole(1, dim),
+            whole(dim, 2 * lanes),
+            whole(8, lanes),
+            tile(128),
+            whole(8, lanes),
+        ],
+        [tile(dim), tile(128)] + [tile(lanes)] * 4 + [whole(8, lanes)],
+        [sds((LEN, dim), bf16), sds((LEN, 128), f32)] + proj_shape + [sds((8, lanes), f32)],
+        [pltpu.VMEM((BLK + 8, lanes), f32)],
+        flops=pf,
+        moved=40 << 20,
+        prefetch=1,
+    )(which, hidden_in, norm_gain.reshape(1, dim), w_a, prm_a, msk, jnp.zeros((8, lanes), f32))
     bcp, bca, bc, dtr, dt, cum, cumt = ordered(
         functools.partial(states_kernel, docl),
         NBLK,
@@ -655,81 +641,110 @@
         [pltpu.VMEM((BLK + 8, 2 * NS), f32)],
         flops=2 * LEN * dim * 512,
         moved=18 << 20,
-        after=(c_pair[CHUNKS - 1],),
+        after=(w_got,),
     )(normed, wst, kern_bc, dtp, msk)
 
-    def scan(off, xs, z, prm, after=()):
+    def line_scatter(v, axis=1):
+        return lax.psum_scatter(v, "zline", scatter_dimension=axis, tiled=True)
+
+    no_tail = jnp.zeros((8, lanes), f32)
+    no_state = jnp.zeros((NS, lanes), f32)
+
+    def scan(off, xs, z, prm, start=no_state, at=0, blocks=NBLK, into=()):
         return ordered(
             functools.partial(scan_kernel, docl, off),
-            NBLK,
+            blocks,
             [
-                tile(lanes), tile(lanes), tile(2 * NS), tile(128), tile(128),
-                pl.BlockSpec((128, BLK), lambda i: (0, i)), whole(8, lanes),
+                tile(lanes, at), tile(lanes, at), tile(2 * NS, at), tile(128, at), tile(128, at),
+                pl.BlockSpec((128, BLK), lambda i: (0, at + i)), whole(8, lanes), whole(NS, lanes),
             ],
-            [tile(lanes), tile(lanes), pl.BlockSpec((1, NS, lanes), lambda i: (i, 0, 0)), tile(128)],
+            [
+                tile(lanes, at), tile(lanes, at),
+                pl.BlockSpec((1, NS, lanes), lambda i: (at + i, 0, 0)), tile(128, at), whole(NS, lanes),
+            ],
             [
                 sds((LEN, lanes), f32),
                 sds((LEN, lanes), bf16),
                 sds((NBLK, NS, lanes), f32),
                 sds((LEN, 128), f32),
+                sds((NS, lanes), f32),
             ],
-            [pltpu.VMEM((NS, lanes), f32)],
-            flops=10 << 30,
-            moved=20 << 20,
-            after=after,
-        )(xs, z, bc, dt, cum, cumt, prm)
-
-    y_a, gw_a, sin_a, pw_a = scan(0, xs_a, z_a, prm_a)
-    for j in reversed(range(CHUNKS - 1)):
-        c_pair[j] = cotangent_of(j, cumt, pw_a)[1]
+            flops=(10 << 30) * blocks // NBLK,
+            moved=(20 << 20) * blocks // NBLK,
+            into=into,
+        )(xs, z, bc, dt, cum, cumt, prm, start)
+
+    def second_step(start, at, blocks, into):
+        return ordered(
+            second_kernel,
+            blocks,
+            [tile(dim, at), whole(dim, 2 * lanes), whole(8, lanes), tile(128, at), whole(8, lanes)],
+            [tile(lanes, at)] * 4 + [whole(8, lanes)],
+            proj_shape + [sds((8, lanes), f32)],
+            [pltpu.VMEM((BLK + 8, lanes), f32)],
+            flops=pf * blocks // NBLK,
+            moved=(28 << 20) * blocks // NBLK,
+            into=into,
+        )(normed, w_b, prm_b, msk, start)
+
+    def out_step(j):
+        return ordered(
+            out_kernel,
+            CB,
+            [tile(lanes, j * CB)] * 2 + [whole(lanes, dim)] * 2,
+            tile(dim),
+            sds((CT, dim), bf16),
+            flops=4 * CT * lanes * dim,
+            moved=10 << 20,
+        )(gw_a, gw_b, o_a, o_b)
+
+    y_a, gw_a, sin_a, pw_a, _ = scan(0, xs_a, z_a, prm_a)
     w_b = with_other_half(w_got, pw_a)
-    z_b, xp_b, a_b, xs_b = ordered(
-        second_kernel,
-        NBLK,
-        [tile(dim), whole(dim, 2 * lanes), whole(8, lanes), tile(128)],
-        proj_out,
-        proj_shape,
-        [pltpu.VMEM((BLK + 8, lanes), f32)],
-        flops=pf,
-        moved=28 << 20,
-    )(normed, w_b, prm_b, msk)
-    y_b, gw_b, sin_b, pw_b = scan(heads, xs_b, z_b, prm_b)
-    o_b = with_other_half(o_got, pw_b)
-
-    class LineSum:
-        def __init__(self, v):
-            self.v = v
-            self.left = groups - 1
-            self.up = self.down = None
-
-        def own(self, j):
-            return lax.dynamic_slice_in_dim(self.v, jnp.clip(j, 0, groups - 1) * wide, wide, 1)
-
-        def step(self, after=None):
-            d = self.left
-            if d == 0:
-                return
-            late = 0 if after is None else zero_after(after)
-            send_u, send_d = self.own(zpos + d + late), self.own(zpos - d - late)
-            if self.up is not None:
-                send_u = (send_u.astype(f32) + self.up.astype(f32)).astype(bf16)
-                send_d = (send_d.astype(f32) + self.down.astype(f32)).astype(bf16)
-            self.up = lax.ppermute(send_u, "zline", [(i, i + 1) for i in range(groups - d)])
-            self.down = lax.ppermute(send_d, "zline", [(i, i - 1) for i in range(d, groups)])
-            self.left = d - 1
-
-        def result(self):
-            while self.left:
-                self.step()
-            return self.own(zpos).astype(f32) + self.up.astype(f32) + self.down.astype(f32)
+    c_got = lax.all_gather(late(c_got, pw_a), "zline", axis=1, tiled=True)
+    half = NBLK // 2
+    *begun, tail = second_step(no_tail, 0, half, ())
+    *done, state = scan(heads, begun[3], begun[0], prm_b, no_state, 0, half)
+    o_b = with_other_half(late(o_got, tail), state)
+    gw_b = done[1]
+    mixed_0 = line_scatter(out_step(0))
+    z_b, xp_b, a_b, xs_b, _ = second_step(tail, half, half, begun)
+    y_b, gw_b, sin_b, pw_b, _ = scan(heads, xs_b, z_b, prm_b, state, half, half, done)
 
     c_all = [None] * CHUNKS
     for j in reversed(range(CHUNKS)):
-        c_all[j] = lax.all_gather(c_pair[j], "zline", axis=1, tiled=True)
+        mine_j, got_j = (v[j * CT : (j + 1) * CT] for v in (c_mine, c_got))
+        c_all[j] = jnp.concatenate(
+            [jnp.where(is0, mine_j, got_j), jnp.where(is0, got_j, mine_j)], axis=1
+        )
+
+    def reordered(w):
+        return jnp.concatenate(
+            [
+                w[:, (2 * z + q) * local_dim : (2 * z + q + 1) * local_dim]
+                for q in range(2)
+                for z in range(groups)
+            ],
+            axis=1,
+        )
+
+    p_a, p_b = reordered(o_a), reordered(o_b)
 
     power = pw_a[:, 0] + pw_b[:, 0]
     wdt_t = wdt.T
-    wbc_near = lax.dynamic_slice_in_dim(wbc, zpos * wide, wide, 1)
+    cols = w_bc.shape[2]
+
+    def group_columns(v, group):
+        v = v.reshape(-1, 2, NS)
+        return lax.dynamic_slice_in_dim(v, group * 2 * cols, 2 * cols, 2).reshape(-1, 4 * cols)
+
+    def near_columns(v):
+        return jnp.pad(group_columns(v, zpos), ((0, 0), (0, 128 - 4 * cols)))
+
+    bca_near, bcp_near, kern_near = near_columns(bca), near_columns(bcp), near_columns(kern_bc)
+    wbc_near = lax.dynamic_slice_in_dim(wbc, zpos * wide, wide, 1).T
+    wbc_near = jnp.concatenate(
+        [group_columns(wbc_near, (zpos + groups - k) % groups) for k in range(groups)], axis=1
+    ).T
 
     def dyn_step(j, after=()):
         return ordered(
@@ -741,7 +756,7 @@
             flops=4 * CT * lanes * dim,
             moved=12 << 20,
             after=after,
-        )(c_all[j], o_a, o_b, gw_a, gw_b)
+        )(c_all[j], p_a, p_b, gw_a, gw_b)
 
     def scales_of(j, qs):
         sums = line_sum(jnp.concatenate([power[j * CT : (j + 1) * CT], qs[:, 0]]))
@@ -800,18 +815,7 @@
             ds, cda, cm,
         )
 
-    def states_sum(v, *after):
-        bit = 1
-        after = list(after)
-        while bit < groups:
-            if after:
-                v = late(v, after.pop(0))
-            got = lax.ppermute(v.astype(bf16), "zline", [(i, i ^ bit) for i in range(groups)])
-            v = v.astype(f32) + got.astype(f32)
-            bit *= 2
-        return v
-
-    def states_step(j, dbc, sda, scm, after=()):
+    def states_step(j, dbc, sda, scm):
         last = j * CB + CB - 1
 
         def bt(width):
@@ -823,47 +827,50 @@
         return ordered(
             states_back_kernel,
             CB,
-            [loc(2 * NS), bt(2 * NS), bt(2 * NS), bt(128), whole(8, 2 * NS), whole(8, 2 * NS), whole(8, 128)],
-            [loc(2 * NS), loc(128), whole(40, 2 * NS), whole(8, 2 * NS), whole(8, 128)],
             [
-                sds((CT, 2 * NS), bf16), sds((CT, 128), f32), sds((40, 2 * NS), f32),
-                sds((8, 2 * NS), f32), sds((8, 128), f32),
+                pl.BlockSpec((BLK, 128), lambda i: (CB - 1 - i, wide // 128)),
+                bt(128), bt(128), bt(128), whole(8, 128), whole(8, 128), whole(8, 128),
             ],
-            [pltpu.VMEM((BLK + 8, 2 * NS), f32), pltpu.VMEM((BLK + 8, 128), f32)],
+            [loc(128), loc(128), whole(40, 128), whole(8, 128), whole(8, 128)],
+            [
+                sds((CT, 128), bf16), sds((CT, 128), f32), sds((40, 128), f32),
+                sds((8, 128), f32), sds((8, 128), f32),
+            ],
+            [pltpu.VMEM((BLK + 8, 128), f32), pltpu.VMEM((BLK + 8, 128), f32)],
             flops=CHEAP,
             moved=CHEAP,
-            after=after,
-        )(dbc, bca, bcp, msk, kern_bc, sda, scm)
-
-    def dn_step(dz, dxp, ddt, after=()):
+        )(dbc, bca_near, bcp_near, msk, kern_near, sda, scm)
+
+    def dn_step(dz, dxp, ddt, dbc, after=()):
         return ordered(
             dn_kernel,
-            4,
+            groups,
             [
-                whole(CT, 2 * lanes), whole(CT, 2 * lanes), whole(CT, 128),
-                pl.BlockSpec((dim // 4, 2 * lanes), lambda i: (i, 0)),
-                pl.BlockSpec((dim // 4, 2 * lanes), lambda i: (i, 0)),
-                pl.BlockSpec((dim // 4, 128), lambda i: (i, 0)),
+                whole(CT, 2 * lanes), whole(CT, 2 * lanes), whole(CT, 128), whole(CT, 2 * NS),
+                pl.BlockSpec((wide, 2 * lanes), lambda i: (i, 0)),
+                pl.BlockSpec((wide, 2 * lanes), lambda i: (i, 0)),
+                pl.BlockSpec((wide, 128), lambda i: (i, 0)),
             ],
-            pl.BlockSpec((CT, dim // 4), lambda i: (0, i)),
-            sds((CT, dim), bf16),
+            pl.BlockSpec((CT, wide + 128), lambda i: (i, 0)),
+            sds((groups * CT, wide + 128), bf16),
             flops=8 * CT * lanes * dim,
             moved=16 << 20,
             after=after,
-        )(dz, dxp, ddt, w_a, w_b, wdt_t)
-
-    def near_sum(dn):
-        return lax.psum_scatter(dn, "zline", scatter_dimension=1, tiled=True)
+        )(dz, dxp, ddt, dbc, w_a, w_b, wdt_t)
 
     def near_step(total, dsp):
-        total = total.astype(f32) + jnp.dot(dsp, wbc_near, preferred_element_type=f32)
+        mine_first = [dsp[:, : 4 * cols]] + [
+            lax.ppermute(dsp[:, : 4 * cols], "zline", [(i, (i + k) % groups) for i in range(groups)])
+            for k in range(1, groups)
+        ]
+        total = total[:, :wide].astype(f32) + nn(jnp.concatenate(mine_first, axis=1), wbc_near)
         keep = lax.dynamic_slice_in_dim(total, mine * local_dim, local_dim, 1)
         give = lax.dynamic_slice_in_dim(total, (1 - mine) * local_dim, local_dim, 1)
         return keep, swap(give.astype(bf16))
 
     core_at = core.astype(jnp.int32).reshape(1)
 
-    def weight_grad(lhs, rhs, more=None):
+    def weight_grad(lhs, rhs, more=None, after=()):
         count = len(rhs)
         n, m = lhs[0].shape[1], rhs[0].shape[1]
         part = LEN // count
@@ -895,68 +902,58 @@
             flops=CHEAP,
             moved=CHEAP,
             prefetch=1,
+            after=after,
         )(core_at, *lhs, *rhs, *more)
+
+    def bit_of(bit):
+        return lax.axis_index("rows") // bit % 2
+
+    def core_sum(keep, give):
+        return keep + cross(give, 1)
+
+    def pair_sum(v):
+        n = v.shape[1] // 2
+        return v[:, :n] + swap(v[:, n:].astype(bf16)).astype(f32)
 
     dz, dy, yn, mtg, scales = ([None] * CHUNKS for _ in range(5))
     dxp, ddt, dsp, near, far, dns = ([None] * CHUNKS for _ in range(6))
     ggs, accs, accs_dt, accs_bc = [], [], [], []
     carry = (jnp.zeros((2, NS, lanes), f32), jnp.zeros((2, 8, lanes), f32), jnp.zeros((8, 128), f32))
-    state_carry = (jnp.zeros((8, 2 * NS), f32), jnp.zeros((8, 128), f32))
-
-    def out_step(j):
-        return ordered(
-            out_kernel,
-            CB,
-            [tile(lanes, j * CB)] * 2 + [whole(lanes, dim)] * 2,
-            tile(dim),
-            sds((CT, dim), bf16),
-            flops=4 * CT * lanes * dim,
-            moved=10 << 20,
-        )(gw_a, gw_b, o_a, o_b)
+    state_carry = (jnp.zeros((8, 128), f32), jnp.zeros((8, 128), f32))
 
     top = CHUNKS - 1
     d_a, d_b, qs = dyn_step(top)
     scales[top], sq = scales_of(top, qs)
-    mixing = LineSum(out_step(top))
-    mixing.step(after=sq)
 
     dz[1], dy[1], yn[1], mtg[1], gg = gate_step(1, sq, d_a, d_b)
     ggs.append(gg)
     dxp[1], ddt[1], dbc_1, mtb_1, acc, acc_dt, *carry = back_step(1, dy[1], *carry)
     accs.append(acc)
     accs_dt.append(acc_dt)
-    dns[1] = dn_step(dz[1], dxp[1], ddt[1], after=(mixing.up, mixing.down))
-    total_1 = near_sum(dns[1])
+    dns[1] = dn_step(dz[1], dxp[1], ddt[1], dbc_1, after=(mixed_0,))
+    total_1 = line_scatter(dns[1], 0)
     d_a, d_b, qs = dyn_step(0)
     scales[0], sq = scales_of(0, qs)
-    partial_0 = out_step(0)
+    mixed_1 = line_scatter(out_step(1))
     dz[0], dy[0], yn[0], mtg[0], gg = gate_step(0, sq, d_a, d_b)
     ggs.append(gg)
-    mixing.step(after=sq)
     g_out = weight_grad(c_all, yn)
     g_z = weight_grad([normed] * CHUNKS, dz)
-    mixing_2 = (mixing.up, mixing.down)
-    mixing.step(after=g_z[0])
-    dxp[0], ddt[0], dbc_0, mtb_0, acc, acc_dt, *carry = back_step(
-        0, dy[0], *carry, after=mixing_2
-    )
+    dxp[0], ddt[0], dbc_0, mtb_0, acc, acc_dt, *carry = back_step(0, dy[0], *carry)
     accs.append(acc)
     accs_dt.append(acc_dt)
-    dns[0] = dn_step(dz[0], dxp[0], ddt[0], after=(total_1,))
-    total_0 = near_sum(dns[0])
-    mixed_0 = near_sum(partial_0)
-    g_x = weight_grad([normed] * CHUNKS, dxp)
-    summed_1 = states_sum(dbc_1, dbc_0, g_x[0])
-    summed_0 = states_sum(dbc_0, dbc_0, g_x[0])
-    dsp[1], mtc_1, acc_bc, *state_carry = states_step(1, summed_1, *state_carry)
+    dsp[1], mtc_1, acc_bc, *state_carry = states_step(1, total_1, *state_carry)
     accs_bc.append(acc_bc)
-    dsp[0], mtc_0, acc_bc, *state_carry = states_step(0, summed_0, *state_carry)
+    out_sum, z_sum = core_sum(*g_out), core_sum(*g_z)
+    g_x = weight_grad([normed] * CHUNKS, dxp, after=(out_sum, z_sum))
+    x_sum = core_sum(*g_x)
+    out_sum = pair_sum(out_sum)
+    dns[0] = dn_step(dz[0], dxp[0], ddt[0], dbc_0, after=(out_sum,))
+    total_0 = line_scatter(dns[0], 0)
+    dsp[0], mtc_0, acc_bc, *state_carry = states_step(0, total_0, *state_carry)
     accs_bc.append(acc_bc)
 
-    cols = w_bc.shape[2]
-    dsp_near = lax.dynamic_slice_in_dim(
-        jnp.concatenate(dsp, axis=0).reshape(LEN, 2, NS), zpos * 2 * cols, 2 * cols, 2
-    ).reshape(LEN, 2, 2, cols)
+    dsp_near = jnp.concatenate(dsp, axis=0)[:, : 4 * cols].reshape(LEN, 2, 2, cols)
     ddt_all = jnp.concatenate(ddt, axis=0)
     width = 2 * cols + heads
 
@@ -966,20 +963,24 @@
         return jnp.concatenate([sel, dts, jnp.zeros((LEN, 128 - width), bf16)], axis=1)
 
     fewer = jnp.concatenate([few(mine), few(1 - mine)], axis=1)
-    g_few = weight_grad([normed], [fewer])
+    g_few = ordered(
+        few_kernel,
+        8,
+        [pl.BlockSpec((LEN, dim // 8), lambda i: (0, i)), whole(LEN, fewer.shape[1])],
+        pl.BlockSpec((fewer.shape[1], dim // 8), lambda i: (0, i)),
+        sds((fewer.shape[1], dim), f32),
+        flops=CHEAP,
+        moved=CHEAP,
+    )(normed, fewer)
     near[1], far[1] = near_step(total_1, dsp[1])
     near[0], far[0] = near_step(total_0, dsp[0])
-    local_sum = jnp.concatenate([mtg[j][:, 0] + m[:, 0] for j, m in ((0, mtb_0), (1, mtb_1))])
-    mean_sum = line_sum(local_sum) + jnp.concatenate([mtc_0[:, 0], mtc_1[:, 0]])
-    mixer = jnp.concatenate([mixed_0.astype(f32), mixing.result()], axis=0)
-
-    def bit_of(bit):
-        return lax.axis_index("rows") // bit % 2
-
-    def reduce_pair(keep, give):
-        n = keep.shape[1] // 2
-        v = keep + cross(give, 1)
-        v = v[:, :n] + swap(v[:, n:].astype(bf16)).astype(f32)
+    local_sum = [
+        mtg[j][:, 0] + m[:, 0] + n[:, 0] for j, m, n in ((0, mtb_0, mtc_0), (1, mtb_1, mtc_1))
+    ]
+    mean_sum = line_sum(jnp.concatenate(local_sum))
+    mixer = jnp.concatenate([mixed_0, mixed_1], axis=0).astype(f32)
+
+    def reduce_rows(v):
         bit = 2
         while bit < nrows:
             size = v.shape[0] // 2
@@ -1000,11 +1001,26 @@
         first = core == 0
         return jnp.concatenate([jnp.where(first, v, got), jnp.where(first, got, v)], axis=0)
 
-    g_x, g_z, g_out, g_few = (reduce_pair(*g) for g in (g_x, g_z, g_out, g_few))
-    grad_w_out = both_cores(g_out).T.astype(f32)
-    g_few = both_cores(g_few).astype(f32)
-    grad_w_bc = g_few[:, : 2 * cols].reshape(dim, 2, cols)
-    grad_w_dt = g_few[:, 2 * cols : width]
+    def rows_sum(v):
+        bit = 1
+        while bit < nrows:
+            v = v + cross(v, bit)
+            bit *= 2
+        return v
+
+    g_x, g_z, g_out = (reduce_rows(v) for v in (pair_sum(x_sum), pair_sum(z_sum), out_sum))
+    g_few = rows_sum(g_few[:width] + swap(g_few[128 : 128 + width].astype(bf16)).astype(f32))
+    g_out = both_cores(g_out)
+    grad_w_out = jnp.concatenate(
+        [
+            g_out[(q * groups + z) * local_dim : (q * groups + z + 1) * local_dim]
+            for z in range(groups)
+            for q in range(2)
+        ],
+        axis=0,
+    ).T.astype(f32)
+    grad_w_bc = g_few[: 2 * cols].reshape(2, cols, dim).transpose(2, 0, 1)
+    grad_w_dt = g_few[2 * cols :].T
     x_far, z_far = cross(g_x, 1), cross(g_z, 1)
     steps = 8
     size = dim // steps
@@ -1026,18 +1042,11 @@
     acc_dt = sum(accs_dt).reshape(2, 8, 128).sum(axis=1)[:, :docl].reshape(2, 2, heads)
     acc_dt = jnp.pad(acc_dt.transpose(1, 0, 2).reshape(2, 1, -1), ((0, 0), (0, 0), (0, lanes - docl)))
     vec = jnp.concatenate([acc, gg, acc_dt], axis=1)
-    acc_bc = sum(accs_bc).reshape(5, 8, 2 * NS).sum(axis=1)
-
-    def rows_sum(v):
-        bit = 1
-        while bit < nrows:
-            v = v + cross(v, bit)
-            bit *= 2
-        return v
+    acc_bc = sum(accs_bc).reshape(5, 8, 128).sum(axis=1)[:, : 4 * cols]
 
     vec = rows_sum(vec[0] + swap(vec[1]))
-    acc_bc = rows_sum(acc_bc + swap(acc_bc)).reshape(5, 2, NS)
-    acc_bc = lax.dynamic_slice_in_dim(acc_bc, me * cols, cols, 2)
+    acc_bc = rows_sum(acc_bc + swap(acc_bc)).reshape(5, 2, 2, cols)
+    acc_bc = lax.dynamic_index_in_dim(acc_bc, mine, 2, keepdims=False)
 
     s_all = jnp.concatenate(scales)
     out_near = mixer * s_all[:, None]

time: 820 us -> 764 us (0.932)
  starting transfers between devices: 114 us -> 48.5 us
  Pallas kernels: 314 us -> 328 us
  waiting for transfers between devices: 180 us -> 193 us
  local copies, waits for them, and re-layouts: 90.5 us -> 78.9 us
    ppermute x14 -> x6, waiting for transfers between devices: 76.4 us -> 12.2 us  [near_step(): lax.ppermute(dsp[:, :4 * cols], 'zline', [(i, (i + k) % groups) for i in...]
    ppermute x17 -> x16, waiting for transfers between devices: 66.4 us -> 114 us  [swap(): return lax.ppermute(v, 'pair', [(0, 1), (1, 0)])]
    ppermute x6, starting transfers between devices: 41.3 us -> 6.11 us  [line_sum(): v = v + lax.ppermute(v, 'zline', [(i, i ^ bit) for i in range(groups)])]
    ppermute x14 -> x6, starting transfers between devices: 34.2 us -> 9.04 us  [near_step(): lax.ppermute(dsp[:, :4 * cols], 'zline', [(i, (i + k) % groups) for i in...]
    convert_element_type x12 -> x4, other arithmetic: 20.5 us -> 4.13 us  [the longest x1 2.57 us: shards(): grad_w_out = jnp.concatenate([g_out[(q * groups + z) * local_dim:(q * gro...]
    pallas_call x23 -> x24, Pallas kernels: 314 us -> 328 us  [call(): return lambda *args: fn(*args, *after, *into)]
    ppermute x6, waiting for transfers between devices: 8.53 us -> 18.8 us  [line_sum(): v = v + lax.ppermute(v, 'zline', [(i, i ^ bit) for i in range(groups)])]
    unnamed x135 -> x144, local copies, waits for them, and re-layouts: 35.3 us -> 25.2 us
  transfers between devices with their start and end apart: 66 -> 57, of which waited for: 18 -> 21; matrix products, arithmetic and copies ran while one was open for 21% -> 21% of each run, Pallas kernels for 39% -> 41%
where the time goes in v3:
time: 764 us; the launch traced here: 758 us
  Pallas kernels  328 us (43%)
  waiting for transfers between devices  193 us (25%)
  other arithmetic  89.3 us (12%)
  local copies, waits for them, and re-layouts  78.9 us (10%)
  starting transfers between devices  48.5 us (6%)
  between operations  18.3 us (2%)
    pallas_call x24, Pallas kernels, call(): return lambda *args: fn(*args, *after, *into)  328 us
    ppermute x16, waiting for transfers between devices, swap(): return lax.ppermute(v, 'pair', [(0, 1), (1, 0)])  114 us
    ppermute x22, waiting for transfers between devices, cross(): return lax.ppermute(v, 'rows', [(i, i ^ bit) for i in range(nrows)])  35.8 us
    unnamed x144, local copies, waits for them, and re-layouts  25.2 us
    ppermute x6, waiting for transfers between devices, line_sum(): v = v + lax.ppermute(v, 'zline', [(i, i ^ bit) for i in range(groups)])  18.8 us
    ppermute x16, starting transfers between devices, swap(): return lax.ppermute(v, 'pair', [(0, 1), (1, 0)])  18.5 us
  transfers between devices with their start and end apart: 57, of which 21 were waited for; matrix products, arithmetic and copies ran while one was open for 21% of the time, Pallas kernels for 41%

profile of v3, /device:TPU:0, one launch (start us, length us, event | category | flops | bytes accessed | tf_op | source)
XLA Modules:
  0.0 758.2 jit_solution(18021886990855545517)
XLA Ops:
  18.7 52.0 %collective-permute-done.2.refs_5_ = bf16[1024,1024]{1,0:T(8,128)(2,1)} collective-permute-done((bf16[1024,1024]{1,0:T(8,128)(2,1)S(1)}, bf16[1024,1024]{1,0:T(8,128)(2,1)}, u32[]{:S(2)}, u32[]{:S(2)}) %collective-permute-start.2) | collective-permute-done | bytes 2097184 | tf_op jit(solution)/shard_map/ppermute | solution.py:531
  80.6 20.3 %shard_map.271 = (bf16[2048,2048]{1,0:T(8,128)(2,1)}, f32[2048,128]{1,0:T(8,128)}, bf16[2048,512]{1,0:T(8,128)(2,1)}, bf16[2048,512]{1,0:T(8,128)(2,1)}, bf16[20...) custom-call(s32[1]{0:T(128)} %bitcast.refs_0_, bf16[4096,2048]{1,0:T(8,128)(2,1)} %refs_1_.1, ...), custom_call_target="tpu_custom_call" | custom-call | flops 8589934592 | bytes 41943040 | tf_op jit(solution)/shard_map/pallas_call | solution.py:491
  108.2 15.6 %shard_map.272 = (f32[2048,256]{1,0:T(8,128)}, f32[2048,256]{1,0:T(8,128)}, bf16[2048,256]{1,0:T(8,128)(2,1)}, f32[2048,128]{1,0:T(8,128)}, f32[2048,128]{1,0:T(...) custom-call(bf16[2048,2048]{1,0:T(8,128)(2,1)} %get-tuple-element.103.refs_0_.refs_1_.refs_2_, ...), custom_call_target="tpu_custom_call" | custom-call | flops 4294967296 | bytes 18874368 | tf_op jit(solution)/shard_map/pallas_call | solution.py:491
  124.5 16.6 %shard_map.273 = (f32[2048,512]{1,0:T(8,128)}, bf16[2048,512]{1,0:T(8,128)(2,1)}, f32[8,128,512]{2,1,0:T(8,128)}, f32[2048,128]{1,0:T(8,128)}, f32[128,512]{1,0:T(8,128)}) custom-call(bf16[2048,512]{1,0:T(8,128)(2,1)} %get-tuple-element.101.refs_0_.refs_10_, bf16[2048,512]{1,0:T(8,128)(2,1)} %get-tuple-element.102.refs_1_.refs_5_, ...), custom_call_target="tpu_custom_call" | custom-call | flops 10737418240 | bytes 20971520 | tf_op jit(solution)/shard_map/pallas_call | solution.py:491
  156.1 10.7 %shard_map.274 = (bf16[2048,512]{1,0:T(8,128)(2,1)}, bf16[2048,512]{1,0:T(8,128)(2,1)}, bf16[2048,512]{1,0:T(8,128)(2,1)}, bf16[2048,512]{1,0:T(8,128)(2,1)}, f32[8,512]{1,0:T(8,128)}) custom-call(bf16[2048,2048]{1,0:T(8,128)(2,1)} %get-tuple-element.103.refs_0_.refs_1_.refs_2_, bf16[2048,1024]{1,0:T(8,128)(2,1)} %pad_maximum_fusion.1.refs_1_.refs_5_, ...), custom_call_target="tpu_custom_call" | custom-call | flops 4294967296 | bytes 14680064 | tf_op jit(solution)/shard_map/pallas_call | solution.py:491
  168.7 7.9 %collective-permute-done.4 = bf16[256,2048]{1,0:T(8,128)(2,1)S(1)} collective-permute-done((bf16[256,2048]{1,0:T(8,128)(2,1)}, bf16[256,2048]{1,0:T(8,128)(2,1)S(1)}, u32[]{:S(2)}, u32[]{:S(2)}) %collective-permute-start.4) | collective-permute-done | bytes 1048608 | tf_op jit(solution)/shard_map/ppermute | solution.py:531
  180.0 9.5 %shard_map.275 = (f32[2048,512]{1,0:T(8,128)}, bf16[2048,512]{1,0:T(8,128)(2,1)}, f32[8,128,512]{2,1,0:T(8,128)}, f32[2048,128]{1,0:T(8,128)}, f32[128,512]{1,0:T(8,128)}) custom-call(bf16[2048,512]{1,0:T(8,128)(2,1)} %get-tuple-element.112.refs_0_.refs_9_, bf16[2048,512]{1,0:T(8,128)(2,1)} %get-tuple-element.113.refs_1_.refs_6_, ...), custom_call_target="tpu_custom_call" | custom-call | flops 5368709120 | bytes 10485760 | tf_op jit(solution)/shard_map/pallas_call | solution.py:491
  199.9 8.6 %shard_map.276.refs_5_ = bf16[1024,2048]{1,0:T(8,128)(2,1)} custom-call(bf16[2048,512]{1,0:T(8,128)(2,1)} %get-tuple-element.109.refs_0_.refs_3_, bf16[2048,512]{1,0:T(8,128)(2,1)} %get-tuple-element.115.refs_1_.refs_10_, bf16[512,2048]{1,0:T(8,128)(2,1)} %refs_2_.3, bf16[512,2048]{1,0:T(8,128)(2,1)} %pad_maximum_fusion.refs_3_, ...), custom_call_target="tpu_custom_call" | custom-call | flops 4294967296 | bytes 10485760 | tf_op jit(solution)/shard_map/pallas_call | solution.py:491
  209.6 10.8 %shard_map.277 = (bf16[2048,512]{1,0:T(8,128)(2,1)}, bf16[2048,512]{1,0:T(8,128)(2,1)}, bf16[2048,512]{1,0:T(8,128)(2,1)}, bf16[2048,512]{1,0:T(8,128)(2,1)}, f32[8,512]{1,0:T(8,128)}) custom-call(bf16[2048,2048]{1,0:T(8,128)(2,1)} %get-tuple-element.103.refs_0_.refs_1_.refs_2_, ...), custom_call_target="tpu_custom_call", output_to_operand_aliasing={{0}: (6, {}), {1}: (7, {}), {2}: (8, {}), {3}: (9, {})} | custom-call | flops 4294967296 | bytes 14680064 | tf_op jit(solution)/shard_map/pallas_call | solution.py:491
  220.3 9.6 %shard_map.278 = (f32[2048,512]{1,0:T(8,128)}, bf16[2048,512]{1,0:T(8,128)(2,1)}, f32[8,128,512]{2,1,0:T(8,128)}, f32[2048,128]{1,0:T(8,128)}, f32[128,512]{1,0:T(8,128)}) custom-call(bf16[2048,512]{1,0:T(8,128)(2,1)} %get-tuple-element.119.refs_0_.refs_11_, ...), custom_call_target="tpu_custom_call", output_to_operand_aliasing={{0}: (9, {}), {1}: (10, {}), {2}: (11, {}), {3}: (12, {})} | custom-call | flops 5368709120 | bytes 10485760 | tf_op jit(solution)/shard_map/pallas_call | solution.py:491
  245.4 9.2 %shard_map.279 = (bf16[1024,512]{1,0:T(8,128)(2,1)}, bf16[1024,512]{1,0:T(8,128)(2,1)}, f32[1024,128]{1,0:T(8,128)}) custom-call(bf16[1024,2048]{1,0:T(8,128)(2,1)} %pad_maximum_fusion.3.refs_0_.refs_2_, bf16[512,2048]{1,0:T(8,128)(2,1)} %slice_dynamic-update-slice_fusion.8.refs_1_, bf16[512,2048]{1,0:T(8,128)(2,1)} %fusion.36.refs_2_, ...), custom_call_target="tpu_custom_call" | custom-call | flops 4294967296 | bytes 12582912 | tf_op jit(solution)/shard_map/pallas_call | solution.py:491
  266.7 8.7 %shard_map.280 = (bf16[1024,1024]{1,0:T(8,128)(2,1)}, bf16[1024,1024]{1,0:T(8,128)(2,1)}, bf16[1024,1024]{1,0:T(8,128)(2,1)}, f32[1024,128]{1,0:T(8,128)}, f32[8,1024]{1,0:T(8,128)}) custom-call(f32[1024,128]{1,0:T(8,128)} %pad.48.refs_0_, bf16[1024,512]{1,0:T(8,128)(2,1)} %get-tuple-element.129.refs_1_, bf16[1024,512]{1,0:T(8,128)(2,1)} %get-tuple-element.130.refs_2_, ...), custom_call_target="tpu_custom_call" | custom-call | flops 2097152000 | bytes 20971520 | tf_op jit(solution)/shard_map/pallas_call | solution.py:491
  277.5 32.8 %shard_map.281 = (bf16[1024,1024]{1,0:T(8,128)(2,1)}, bf16[1024,128]{1,0:T(8,128)(2,1)}, bf16[1024,256]{1,0:T(8,128)(2,1)}, f32[1024,128]{1,0:T(8,128)}, f32[2,4...) custom-call(bf16[1024,1024]{1,0:T(8,128)(2,1)} %get-tuple-element.13, ...), custom_call_target="tpu_custom_call" | custom-call | flops 42949672960 | bytes 41943040 | tf_op jit(solution)/shard_map/pallas_call | solution.py:491
  315.6 15.6 %shard_map.282.refs_5_ = bf16[4096,640]{1,0:T(8,128)(2,1)} custom-call(bf16[1024,1024]{1,0:T(8,128)(2,1)} %get-tuple-element.133.refs_0_.refs_4_, bf16[1024,1024]{1,0:T(8,128)(2,1)} %get-tuple-element.143.refs_1_.refs_4_, bf16[1024,128]{1,0:T(8,128)(2,1)} %get-tuple-element.144.refs_2_, bf16[1024,256]{1,0:T(8,128)(2,1)} %get-tuple-element.145.refs_3_, ...), custom_call_target="tpu_custom_call" | custom-call | flops 8589934592 | bytes 16777216 | tf_op jit(solution)/shard_map/pallas_call | solution.py:491
  335.2 20.1 %shard_map.283 = (bf16[1024,512]{1,0:T(8,128)(2,1)}, bf16[1024,512]{1,0:T(8,128)(2,1)}, f32[1024,128]{1,0:T(8,128)}) custom-call(bf16[1024,2048]{1,0:T(8,128)(2,1)} %pad_maximum_fusion.2.refs_0_.refs_1_, bf16[512,2048]{1,0:T(8,128)(2,1)} %slice_dynamic-update-slice_fusion.8.refs_1_, bf16[512,2048]{1,0:T(8,128)(2,1)} %fusion.36.refs_2_, ...), custom_call_target="tpu_custom_call" | custom-call | flops 4294967296 | bytes 12582912 | tf_op jit(solution)/shard_map/pallas_call | solution.py:491
  363.5 8.6 %shard_map.284.refs_9_ = bf16[1024,2048]{1,0:T(8,128)(2,1)} custom-call(bf16[2048,512]{1,0:T(8,128)(2,1)} %get-tuple-element.109.refs_0_.refs_3_, bf16[2048,512]{1,0:T(8,128)(2,1)} %get-tuple-element.125.refs_4_.refs_1_, bf16[512,2048]{1,0:T(8,128)(2,1)} %refs_2_.3, bf16[512,2048]{1,0:T(8,128)(2,1)} %pad_maximum_fusion.refs_3_, ...), custom_call_target="tpu_custom_call" | custom-call | flops 4294967296 | bytes 10485760 | tf_op jit(solution)/shard_map/pallas_call | solution.py:491
  373.2 8.8 %shard_map.285 = (bf16[1024,1024]{1,0:T(8,128)(2,1)}, bf16[1024,1024]{1,0:T(8,128)(2,1)}, bf16[1024,1024]{1,0:T(8,128)(2,1)}, f32[1024,128]{1,0:T(8,128)}, f32[8,1024]{1,0:T(8,128)}) custom-call(f32[1024,128]{1,0:T(8,128)} %pad.49.refs_0_, bf16[1024,512]{1,0:T(8,128)(2,1)} %get-tuple-element.149.refs_1_, bf16[1024,512]{1,0:T(8,128)(2,1)} %get-tuple-element.150.refs_2_, ...), custom_call_target="tpu_custom_call" | custom-call | flops 2097152000 | bytes 20971520 | tf_op jit(solution)/shard_map/pallas_call | solution.py:491
  382.0 15.6 %shard_map.286 = (f32[1024,1024]{1,0:T(8,128)}, f32[1024,1024]{1,0:T(8,128)}) custom-call(s32[1]{0:T(128)} %bitcast.31.refs_0_, bf16[1024,2048]{1,0:T(8,128)(2,1)} %pad_maximum_fusion.2.refs_0_.refs_1_, bf16[1024,2048]{1,0:T(8,128)(2,1)} %pad_maximum_fusion.3.refs_0_.refs_2_, bf16[1024,1024]{1,0:T(8,128)(2,1)} %get-tuple-element.155.refs_3_, ...), custom_call_target="tpu_custom_call" | custom-call | flops 65536 | bytes 65536 | tf_op jit(solution)/shard_map/pallas_call | solution.py:491
  406.2 15.5 %shard_map.287 = (f32[1024,1024]{1,0:T(8,128)}, f32[1024,1024]{1,0:T(8,128)}) custom-call(s32[1]{0:T(128)} %bitcast.31.refs_0_, bf16[2048,2048]{1,0:T(8,128)(2,1)} %get-tuple-element.103.refs_0_.refs_1_.refs_2_, bf16[2048,2048]{1,0:T(8,128)(2,1)} %get-tuple-element.103.refs_0_.refs_1_.refs_2_, bf16[1024,1024]{1,0:T(8,128)(2,1)} %get-tuple-element.151.refs_3_.refs_0_, ...), custom_call_target="tpu_custom_call" | custom-call | flops 65536 | bytes 65536 | tf_op jit(solution)/shard_map/pallas_call | solution.py:491
  431.4 33.2 %shard_map.288 = (bf16[1024,1024]{1,0:T(8,128)(2,1)}, bf16[1024,128]{1,0:T(8,128)(2,1)}, bf16[1024,256]{1,0:T(8,128)(2,1)}, f32[1024,128]{1,0:T(8,128)}, f32[2,4...) custom-call(bf16[1024,1024]{1,0:T(8,128)(2,1)} %get-tuple-element.15, ...), custom_call_target="tpu_custom_call" | custom-call | flops 42949672960 | bytes 41943040 | tf_op jit(solution)/shard_map/pallas_call | solution.py:491
  464.6 6.8 add.337.refs_6_
  477.3 15.6 %shard_map.290 = (f32[1024,1024]{1,0:T(8,128)}, f32[1024,1024]{1,0:T(8,128)}) custom-call(s32[1]{0:T(128)} %bitcast.31.refs_0_, bf16[2048,2048]{1,0:T(8,128)(2,1)} %get-tuple-element.103.refs_0_.refs_1_.refs_2_, bf16[2048,2048]{1,0:T(8,128)(2,1)} %get-tuple-element.103.refs_0_.refs_1_.refs_2_, bf16[1024,1024]{1,0:T(8,128)(2,1)} %get-tuple-element.160.refs_3_.refs_1_, ...), custom_call_target="tpu_custom_call" | custom-call | flops 65536 | bytes 65536 | tf_op jit(solution)/shard_map/pallas_call | solution.py:491
  492.8 15.7 %shard_map.291.refs_7_ = bf16[4096,640]{1,0:T(8,128)(2,1)} custom-call(bf16[1024,1024]{1,0:T(8,128)(2,1)} %get-tuple-element.151.refs_3_.refs_0_, bf16[1024,1024]{1,0:T(8,128)(2,1)} %get-tuple-element.160.refs_3_.refs_1_, bf16[1024,128]{1,0:T(8,128)(2,1)} %get-tuple-element.161.refs_2_, bf16[1024,256]{1,0:T(8,128)(2,1)} %get-tuple-element.162.refs_3_, ...), custom_call_target="tpu_custom_call" | custom-call | flops 8589934592 | bytes 16777216 | tf_op jit(solution)/shard_map/pallas_call | solution.py:491
  522.6 22.0 %collective-permute-done.41 = f32[8,512]{1,0:T(8,128)S(1)} collective-permute-done((f32[8,512]{1,0:T(8,128)S(1)}, f32[8,512]{1,0:T(8,128)S(1)}, u32[]{:S(2)}, u32[]{:S(2)}) %collective-permute-start.41) | collective-permute-done | bytes 16416 | tf_op jit(solution)/shard_map/ppermute | solution.py:531
  550.7 9.9 %collective-permute-done.48 = bf16[512,512]{1,0:T(8,128)(2,1)S(1)} collective-permute-done((bf16[512,512]{1,0:T(8,128)(2,1)S(1)}, bf16[512,512]{1,0:T(8,128)(2,1)S(1)}, u32[]{:S(2)}, u32[]{:S(2)}) %collective-permute-start.48) | collective-permute-done | bytes 524320 | tf_op jit(solution)/shard_map/ppermute | solution.py:534
  561.7 9.4 %collective-permute-done.30 = bf16[512,512]{1,0:T(8,128)(2,1)S(1)} collective-permute-done((bf16[512,512]{1,0:T(8,128)(2,1)S(1)}, bf16[512,512]{1,0:T(8,128)(2,1)S(1)}, u32[]{:S(2)}, u32[]{:S(2)}) %collective-permute-start.30) | collective-permute-done | bytes 524320 | tf_op jit(solution)/shard_map/ppermute | solution.py:534
  575.3 9.0 %collective-permute-done.31 = bf16[512,512]{1,0:T(8,128)(2,1)S(1)} collective-permute-done((bf16[512,512]{1,0:T(8,128)(2,1)S(1)}, bf16[512,512]{1,0:T(8,128)(2,1)S(1)}, u32[]{:S(2)}, u32[]{:S(2)}) %collective-permute-start.31) | collective-permute-done | bytes 524320 | tf_op jit(solution)/shard_map/ppermute | solution.py:534
  601.4 16.7 %collective-permute-done.34 = bf16[1024,512]{1,0:T(8,128)(2,1)} collective-permute-done((bf16[1024,512]{1,0:T(8,128)(2,1)S(1)}, bf16[1024,512]{1,0:T(8,128)(2,1)}, u32[]{:S(2)}, u32[]{:S(2)}) %collective-permute-start.34) | collective-permute-done | bytes 1048608 | tf_op jit(solution)/shard_map/ppermute | solution.py:531
  638.7 12.2 %collective-permute-done.20 = bf16[1024,64]{1,0:T(8,128)(2,1)S(1)} collective-permute-done((bf16[1024,64]{1,0:T(8,128)(2,1)S(1)}, bf16[1024,64]{1,0:T(8,128)(2,1)S(1)}, u32[]{:S(2)}, u32[]{:S(2)}) %collective-permute-start.20) | collective-permute-done | bytes 131104 | tf_op jit(solution)/shard_map/ppermute | solution.py:863
  672.3 9.1 %shard_map.293.refs_5_ = f32[256,2048]{1,0:T(8,128)} custom-call(bf16[2048,2048]{1,0:T(8,128)(2,1)} %get-tuple-element.103.refs_0_.refs_1_.refs_2_, bf16[2048,256]{1,0:T(8,128)(2,1)} %concatenate.144.refs_1_, f32[8,128]{1,0:T(8,128)} %get-tuple-element.180.refs_2_), custom_call_target="tpu_custom_call" | custom-call | flops 65536 | bytes 65536 | tf_op jit(solution)/shard_map/pallas_call | solution.py:491
  688.2 9.5 %shard_map.294 = f32[16384,128]{1,0:T(8,128)} custom-call(s32[1]{0:T(128)} %bitcast.31.refs_0_, bf16[1024,512]{1,0:T(8,128)(2,1)} %copy-done.12, bf16[1024,512]{1,0:T(8,128)(2,1)} %collective-permute-done.32.refs_2_, bf16[1024,512]{1,0:T(8,128)(2,1)} %pad_maximum_fusion.9.refs_3_, bf16[1024,512]{1,0:T(8,128)(2,1)} %collective-permute-done.37.refs_4_, ...), custom_call_target="tpu_custom_call" | custom-call | bytes 25165824 | tf_op jit(solution)/shard_map/pallas_call | solution.py:491
  716.3 12.2 %collective-permute-done.38 = bf16[40,2048]{1,0:T(8,128)(2,1)S(1)} collective-permute-done((bf16[40,2048]{1,0:T(8,128)(2,1)S(1)}, bf16[40,2048]{1,0:T(8,128)(2,1)S(1)}, u32[]{:S(2)}, u32[]{:S(2)}) %collective-permute-start.38) | collective-permute-done | bytes 163872 | tf_op jit(solution)/shard_map/ppermute | solution.py:531
  (439 shorter events, 262.5 us)
Async XLA Ops:
  7.2 94.8 %all-gather.4.cloned.1.call-start = ((), (), s32[]{:S(2)}) async-start(), calls=%async_computation.4 | async-start | bytes 1253376 | tf_op jit(solution)/shard_map/all_gather | solution.py:587
  14.4 56.2 %collective-permute-start.2 = (bf16[1024,1024]{1,0:T(8,128)(2,1)S(1)}, bf16[1024,1024]{1,0:T(8,128)(2,1)}, u32[]{:S(2)}, u32[]{:S(2)}) collective-permute-start(bf16[1024,1024]{1,0:T(8,128)(2,1)S(1)} %constant_dynamic-slice_fusion.18), channel_id=1, source_target_pairs={{0,1},{1,0},{2,3},{3,2},{4,5},{5,4},{6,7},{7,6},{8,9},{9,8},{10,11... | collective-permute-start | bytes 6291464 | tf_op jit(solution)/shard_map/ppermute | solution.py:531
  18.6 212.7 %all-gather.6.cloned.1.call-start = ((), (), s32[]{:S(2)}) async-start(), calls=%async_computation.6 | async-start | bytes 5242880 | tf_op jit(solution)/shard_map/all_gather | solution.py:594
  75.5 162.5 %all-gather.8.cloned.1.call-start = ((), (), s32[]{:S(2)}) async-start(), calls=%async_computation.7 | async-start | bytes 5242880 | tf_op jit(solution)/shard_map/all_gather | solution.py:703
  75.9 25.1 %collective-permute-start.1 = (f32[8,512]{1,0:T(8,128)S(1)}, f32[8,512]{1,0:T(8,128)S(1)}, u32[]{:S(2)}, u32[]{:S(2)}) collective-permute-start(f32[8,512]{1,0:T(8,128)S(1)} %concatenate.113.refs_4_.refs_6_.refs_7_.refs_18_), channel_id=1, source_target_pairs={{0,1},{1,0},{2,3},{3,2},{4,5},{5,4},{6,7},{7,6},{8,9},{9,8},{10,11... | collective-permute-start | bytes 49160 | tf_op jit(solution)/shard_map/ppermute | solution.py:531
  78.0 23.8 %collective-permute-start = (bf16[8,2048]{0,1:T(8,128)(2,1)S(1)}, bf16[8,2048]{0,1:T(8,128)(2,1)S(1)}, u32[]{:S(2)}, u32[]{:S(2)}) collective-permute-start(bf16[8,2048]{0,1:T(8,128)(2,1)S(1)} %bitcast.120), channel_id=1, source_target_pairs={{0,1},{1,0},{2,3},{3,2},{4,5},{5,4},{6,7},{7,6},{8,9},{9,8},{10,11... | collective-permute-start | bytes 98312 | tf_op jit(solution)/shard_map/ppermute | solution.py:531
  106.4 36.7 %collective-permute-start.6 = (bf16[2048,256]{1,0:T(8,128)(2,1)S(1)}, bf16[2048,256]{1,0:T(8,128)(2,1)}, u32[]{:S(2)}, u32[]{:S(2)}) collective-permute-start(bf16[2048,256]{1,0:T(8,128)(2,1)S(1)} %get-tuple-element.272), channel_id=1, source_target_pairs={{0,1},{1,0},{2,3},{3,2},{4,5},{5,4},{6,7},{7,6},{8,9},{9,8},{10,11... | collective-permute-start | bytes 3145736 | tf_op jit(solution)/shard_map/ppermute | solution.py:531
  108.2 42.9 %collective-permute-start.3 = (bf16[1024,1024]{1,0:T(8,128)(2,1)}, bf16[1024,1024]{1,0:T(8,128)(2,1)}, u32[]{:S(2)}, u32[]{:S(2)}) collective-permute-start(bf16[1024,1024]{1,0:T(8,128)(2,1)} %collective-permute-done.2.refs_5_), channel_id=1, source_target_pairs={{0,8},{8,0},{16,24},{24,16},{1,9},{9,1},{17,25},{25,17},{2,10},{10... | collective-permute-start | bytes 6291464 | tf_op jit(solution)/shard_map/ppermute | solution.py:534
  145.4 170.1 %reduce-scatter.5.cloned.1.call-start = ((), (), s32[]{:S(2)}) async-start(), calls=%async_computation.5 | async-start | bytes 5242880 | tf_op jit(solution)/shard_map/reduce_scatter | solution.py:648
  150.8 25.8 %collective-permute-start.4 = (bf16[256,2048]{1,0:T(8,128)(2,1)}, bf16[256,2048]{1,0:T(8,128)(2,1)S(1)}, u32[]{:S(2)}, u32[]{:S(2)}) collective-permute-start(bf16[256,2048]{1,0:T(8,128)(2,1)} %constant_dynamic-slice_fusion.17), channel_id=1, source_target_pairs={{0,1},{1,0},{2,3},{3,2},{4,5},{5,4},{6,7},{7,6},{8,9},{9,8},{10,11... | collective-permute-start | bytes 3145736 | tf_op jit(solution)/shard_map/ppermute | solution.py:531
  208.6 264.7 %reduce-scatter.9.cloned.1.call-start = ((), (), s32[]{:S(2)}) async-start(), calls=%async_computation.9 | async-start | bytes 6553600 | tf_op jit(solution)/shard_map/reduce_scatter | solution.py:648
  331.2 291.4 %reduce-scatter.7.cloned.1.call-start = ((), (), s32[]{:S(2)}) async-start(), calls=%async_computation.8 | async-start | bytes 5242880 | tf_op jit(solution)/shard_map/reduce_scatter | solution.py:648
  397.6 28.0 %collective-permute-start.13 = (f32[1024,1024]{1,0:T(8,128)}, f32[1024,1024]{1,0:T(8,128)}, u32[]{:S(2)}, u32[]{:S(2)}) collective-permute-start(f32[1024,1024]{1,0:T(8,128)} %get-tuple-element.158.refs_5_), channel_id=1, source_target_pairs={{0,8},{8,0},{16,24},{24,16},{1,9},{9,1},{17,25},{25,17},{2,10},{10... | collective-permute-start | bytes 12582920 | tf_op jit(solution)/shard_map/ppermute | solution.py:534
  397.7 256.0 %reduce-scatter.11.cloned.1.call-start = ((), (), s32[]{:S(2)}) async-start(), calls=%async_computation.10 | async-start | bytes 6553600 | tf_op jit(solution)/shard_map/reduce_scatter | solution.py:648
  399.1 115.0 %collective-permute-start.12 = (f32[2048]{0:T(1024)S(1)}, f32[2048]{0:T(1024)S(1)}, u32[]{:S(2)}, u32[]{:S(2)}) collective-permute-start(f32[2048]{0:T(1024)S(1)} %slice_reduce_fusion), channel_id=1, source_target_pairs={{0,1},{1,0},{2,3},{3,2},{4,5},{5,4},{6,7},{7,6},{8,9},{9,8},{10,11... | collective-permute-start | bytes 24584 | tf_op jit(solution)/shard_map/ppermute | solution.py:531
  421.7 42.9 %collective-permute-start.15 = (f32[1024,1024]{1,0:T(8,128)}, f32[1024,1024]{1,0:T(8,128)}, u32[]{:S(2)}, u32[]{:S(2)}) collective-permute-start(f32[1024,1024]{1,0:T(8,128)} %get-tuple-element.159.refs_23_), channel_id=1, source_target_pairs={{0,8},{8,0},{16,24},{24,16},{1,9},{9,1},{17,25},{25,17},{2,10},{10... | collective-permute-start | bytes 12582920 | tf_op jit(solution)/shard_map/ppermute | solution.py:534
  430.6 40.8 %collective-permute-start.14 = (bf16[1024,512]{1,0:T(8,128)(2,1)S(1)}, bf16[1024,512]{1,0:T(8,128)(2,1)S(1)}, u32[]{:S(2)}, u32[]{:S(2)}) collective-permute-start(bf16[1024,512]{1,0:T(8,128)(2,1)S(1)} %slice.609), channel_id=1, source_target_pairs={{0,1},{1,0},{2,3},{3,2},{4,5},{5,4},{6,7},{7,6},{8,9},{9,8},{10,11... | collective-permute-start | bytes 3145736 | tf_op jit(solution)/shard_map/ppermute | solution.py:531
  518.6 26.0 %collective-permute-start.29 = (bf16[1024,512]{1,0:T(8,128)(2,1)S(1)}, bf16[1024,512]{1,0:T(8,128)(2,1)S(1)}, u32[]{:S(2)}, u32[]{:S(2)}) collective-permute-start(bf16[1024,512]{1,0:T(8,128)(2,1)S(1)} %slice.608), channel_id=1, source_target_pairs={{0,1},{1,0},{2,3},{3,2},{4,5},{5,4},{6,7},{7,6},{8,9},{9,8},{10,11... | collective-permute-start | bytes 3145736 | tf_op jit(solution)/shard_map/ppermute | solution.py:531
  519.7 24.8 %collective-permute-start.41 = (f32[8,512]{1,0:T(8,128)S(1)}, f32[8,512]{1,0:T(8,128)S(1)}, u32[]{:S(2)}, u32[]{:S(2)}) collective-permute-start(f32[8,512]{1,0:T(8,128)S(1)} %slice_bitcast_fusion.1), channel_id=1, source_target_pairs={{0,1},{1,0},{2,3},{3,2},{4,5},{5,4},{6,7},{7,6},{8,9},{9,8},{10,11... | collective-permute-start | bytes 49160 | tf_op jit(solution)/shard_map/ppermute | solution.py:531
  521.0 24.5 %collective-permute-start.47 = (bf16[512,512]{1,0:T(8,128)(2,1)S(1)}, bf16[512,512]{1,0:T(8,128)(2,1)S(1)}, u32[]{:S(2)}, u32[]{:S(2)}) collective-permute-start(bf16[512,512]{1,0:T(8,128)(2,1)S(1)} %dynamic-slice_convert_fusion.2), channel_id=1, source_target_pairs={{0,16},{8,24},{16,0},{24,8},{1,17},{9,25},{17,1},{25,9},{2,18},{10... | collective-permute-start | bytes 1572872 | tf_op jit(solution)/shard_map/ppermute | solution.py:534
  545.0 41.7 %collective-permute-start.33 = (f32[1024,1024]{1,0:T(8,128)}, f32[1024,1024]{1,0:T(8,128)}, u32[]{:S(2)}, u32[]{:S(2)}) collective-permute-start(f32[1024,1024]{1,0:T(8,128)} %get-tuple-element.169.refs_8_), channel_id=1, source_target_pairs={{0,8},{8,0},{16,24},{24,16},{1,9},{9,1},{17,25},{25,17},{2,10},{10... | collective-permute-start | bytes 12582920 | tf_op jit(solution)/shard_map/ppermute | solution.py:534
  547.3 23.7 %collective-permute-start.30 = (bf16[512,512]{1,0:T(8,128)(2,1)S(1)}, bf16[512,512]{1,0:T(8,128)(2,1)S(1)}, u32[]{:S(2)}, u32[]{:S(2)}) collective-permute-start(bf16[512,512]{1,0:T(8,128)(2,1)S(1)} %dynamic-slice_convert_fusion.4), channel_id=1, source_target_pairs={{0,16},{8,24},{16,0},{24,8},{1,17},{9,25},{17,1},{25,9},{2,18},{10... | collective-permute-start | bytes 1572872 | tf_op jit(solution)/shard_map/ppermute | solution.py:534
  549.1 23.7 %collective-permute-start.43 = (f32[8,512]{1,0:T(8,128)S(1)}, f32[8,512]{1,0:T(8,128)S(1)}, u32[]{:S(2)}, u32[]{:S(2)}) collective-permute-start(f32[8,512]{1,0:T(8,128)S(1)} %add.381), channel_id=1, source_target_pairs={{0,16},{8,24},{16,0},{24,8},{1,17},{9,25},{17,1},{25,9},{2,18},{10... | collective-permute-start | bytes 49160 | tf_op jit(solution)/shard_map/ppermute | solution.py:534
  561.7 22.8 %collective-permute-start.49 = (bf16[1024,512]{1,0:T(8,128)(2,1)}, bf16[1024,512]{1,0:T(8,128)(2,1)}, u32[]{:S(2)}, u32[]{:S(2)}) collective-permute-start(bf16[1024,512]{1,0:T(8,128)(2,1)} %pad_maximum_fusion.10), channel_id=1, source_target_pairs={{0,8},{8,0},{16,24},{24,16},{1,9},{9,1},{17,25},{25,17},{2,10},{10... | collective-permute-start | bytes 3145736 | tf_op jit(solution)/shard_map/ppermute | solution.py:534
  584.4 98.6 %collective-permute-start.32 = (bf16[1024,512]{1,0:T(8,128)(2,1)S(1)}, bf16[1024,512]{1,0:T(8,128)(2,1)}, u32[]{:S(2)}, u32[]{:S(2)}) collective-permute-start(bf16[1024,512]{1,0:T(8,128)(2,1)S(1)} %pad_maximum_fusion.8.refs_1_), channel_id=1, source_target_pairs={{0,8},{8,0},{16,24},{24,16},{1,9},{9,1},{17,25},{25,17},{2,10},{10... | collective-permute-start | bytes 3145736 | tf_op jit(solution)/shard_map/ppermute | solution.py:534
  592.7 25.4 %collective-permute-start.34 = (bf16[1024,512]{1,0:T(8,128)(2,1)S(1)}, bf16[1024,512]{1,0:T(8,128)(2,1)}, u32[]{:S(2)}, u32[]{:S(2)}) collective-permute-start(bf16[1024,512]{1,0:T(8,128)(2,1)S(1)} %slice.607), channel_id=1, source_target_pairs={{0,1},{1,0},{2,3},{3,2},{4,5},{5,4},{6,7},{7,6},{8,9},{9,8},{10,11... | collective-permute-start | bytes 3145736 | tf_op jit(solution)/shard_map/ppermute | solution.py:531
  625.7 113.3 %collective-permute-start.11 = (bf16[2048,256]{1,0:T(8,128)(2,1)}, bf16[2048,256]{1,0:T(8,128)(2,1)}, u32[]{:S(2)}, u32[]{:S(2)}) collective-permute-start(bf16[2048,256]{1,0:T(8,128)(2,1)} %dynamic-slice_convert_fusion), channel_id=1, source_target_pairs={{0,1},{1,0},{2,3},{3,2},{4,5},{5,4},{6,7},{7,6},{8,9},{9,8},{10,11... | collective-permute-start | bytes 3145736 | tf_op jit(solution)/shard_map/ppermute | solution.py:531
  653.7 34.6 %collective-permute-start.37 = (bf16[1024,512]{1,0:T(8,128)(2,1)}, bf16[1024,512]{1,0:T(8,128)(2,1)}, u32[]{:S(2)}, u32[]{:S(2)}) collective-permute-start(bf16[1024,512]{1,0:T(8,128)(2,1)} %pad_maximum_fusion.9.refs_3_), channel_id=1, source_target_pairs={{0,8},{8,0},{16,24},{24,16},{1,9},{9,1},{17,25},{25,17},{2,10},{10... | collective-permute-start | bytes 3145736 | tf_op jit(solution)/shard_map/ppermute | solution.py:534
  660.9 49.9 %collective-permute-start.18 = (bf16[1024,64]{1,0:T(8,128)(2,1)}, bf16[1024,64]{1,0:T(8,128)(2,1)}, u32[]{:S(2)}, u32[]{:S(2)}) collective-permute-start(bf16[1024,64]{1,0:T(8,128)(2,1)} %bitcast.136), channel_id=1, source_target_pairs={{0,6},{2,0},{4,2},{6,4},{1,7},{3,1},{5,3},{7,5},{8,14},{10,8},{12,... | collective-permute-start | bytes 393224 | tf_op jit(solution)/shard_map/ppermute | solution.py:863
  665.1 32.6 %collective-permute-start.46 = (f32[5,64]{1,0:T(8,128)}, f32[5,64]{1,0:T(8,128)}, u32[]{:S(2)}, u32[]{:S(2)}) collective-permute-start(f32[5,64]{1,0:T(8,128)} %add.385), channel_id=1, source_target_pairs={{0,16},{8,24},{16,0},{24,8},{1,17},{9,25},{17,1},{25,9},{2,18},{10... | collective-permute-start | bytes 3848 | tf_op jit(solution)/shard_map/ppermute | solution.py:534
  683.1 29.1 %collective-permute-start.17 = (bf16[1024,64]{1,0:T(8,128)(2,1)S(1)}, bf16[1024,64]{1,0:T(8,128)(2,1)}, u32[]{:S(2)}, u32[]{:S(2)}) collective-permute-start(bf16[1024,64]{1,0:T(8,128)(2,1)S(1)} %bitcast.137), channel_id=1, source_target_pairs={{0,4},{2,6},{4,0},{6,2},{1,5},{3,7},{5,1},{7,3},{8,12},{10,14},{12... | collective-permute-start | bytes 393224 | tf_op jit(solution)/shard_map/ppermute | solution.py:863
  688.2 24.6 %collective-permute-start.16 = (bf16[1024,64]{1,0:T(8,128)(2,1)S(1)}, bf16[1024,64]{1,0:T(8,128)(2,1)}, u32[]{:S(2)}, u32[]{:S(2)}) collective-permute-start(bf16[1024,64]{1,0:T(8,128)(2,1)S(1)} %bitcast.138), channel_id=1, source_target_pairs={{0,2},{2,4},{4,6},{6,0},{1,3},{3,5},{5,7},{7,1},{8,10},{10,12},{12... | collective-permute-start | bytes 393224 | tf_op jit(solution)/shard_map/ppermute | solution.py:863
  (86 other events, 930.3 us)
Sparse Core Ops, SparseCore 0:
  18.8 47.1 all-gather.3
  75.7 82.0 all-gather.5
  159.3 78.7 all-gather.7
  240.2 75.2 reduce-scatter.4
  331.3 94.5 reduce-scatter.8
  428.2 77.2 reduce-scatter.6
  508.6 93.4 reduce-scatter.10

commit v4 on v3

--- a/solution.py
+++ b/solution.py
@@ -422,8 +422,19 @@
         give[...] = v
 
 
-def few_kernel(lhs, rhs, o):
-    o[...] = tn(rhs[...], lhs[...])
+def few_kernel(cols, heads, mine, lhs, dsp_0, dsp_1, ddt_0, ddt_1, o, few):
+    @pl.when(pl.program_id(0) == 0)
+    def _():
+        row, lane = iota((128, 256), 0), iota((128, 256), 1)
+        side, c = lane // 128, lane % 128
+        pair = jnp.where(side == 0, mine[0], 1 - mine[0])
+        state = (row == c // cols * 2 * cols + pair * cols + c % cols) & (c < 2 * cols)
+        step = (row == side * heads + c - 2 * cols) & (c >= 2 * cols) & (c < 2 * cols + heads)
+        for k, (dsp, ddt) in enumerate(((dsp_0, ddt_0), (dsp_1, ddt_1))):
+            v = nn(dsp[...], state.astype(bf16)) + nn(ddt[...], step.astype(bf16))
+            few[k * CT : k * CT + CT, :] = v.astype(bf16)
+
+    o[...] = tn(few[...], lhs[...])
 
 
 def join_kernel(core, za, zb, xa, xb, o):
@@ -586,10 +597,9 @@
 
     pack = lax.all_gather(pack, ("zline", "pair"), axis=1, tiled=True)
     is0 = mine == 0
-    w_half = rows_of(w_a, core * (dim // 2), dim // 2)
-    w_got = swap(w_half)
-    c_got = swap(rows_of(cotangent, (1 - mine) * LEN + zero_after(w_got), LEN))
-    o_got = half_of_partner(w_out, w_got)
+    c_got = swap(rows_of(cotangent, (1 - mine) * LEN, LEN))
+    w_got = half_of_partner(w_a)
+    o_got = half_of_partner(w_out)
     c_mine = rows_of(cotangent, mine * LEN, LEN)
     c_mine = lax.all_gather(c_mine, "zline", axis=1, tiled=True)
     pack = pack.reshape(2 * NS, dim + 128)
@@ -628,6 +638,7 @@
         flops=pf,
         moved=40 << 20,
         prefetch=1,
+        after=(prm_b, wdt_b),
     )(which, hidden_in, norm_gain.reshape(1, dim), w_a, prm_a, msk, jnp.zeros((8, lanes), f32))
     bcp, bca, bc, dtr, dt, cum, cumt = ordered(
         functools.partial(states_kernel, docl),
@@ -641,7 +652,6 @@
         [pltpu.VMEM((BLK + 8, 2 * NS), f32)],
         flops=2 * LEN * dim * 512,
         moved=18 << 20,
-        after=(w_got,),
     )(normed, wst, kern_bc, dtp, msk)
 
     def line_scatter(v, axis=1):
@@ -650,7 +660,7 @@
     no_tail = jnp.zeros((8, lanes), f32)
     no_state = jnp.zeros((NS, lanes), f32)
 
-    def scan(off, xs, z, prm, start=no_state, at=0, blocks=NBLK, into=()):
+    def scan(off, xs, z, prm, start=no_state, at=0, blocks=NBLK, into=(), after=()):
         return ordered(
             functools.partial(scan_kernel, docl, off),
             blocks,
@@ -672,6 +682,7 @@
             flops=(10 << 30) * blocks // NBLK,
             moved=(20 << 20) * blocks // NBLK,
             into=into,
+            after=after,
         )(xs, z, bc, dt, cum, cumt, prm, start)
 
     def second_step(start, at, blocks, into):
@@ -698,7 +709,7 @@
             moved=10 << 20,
         )(gw_a, gw_b, o_a, o_b)
 
-    y_a, gw_a, sin_a, pw_a, _ = scan(0, xs_a, z_a, prm_a)
+    y_a, gw_a, sin_a, pw_a, _ = scan(0, xs_a, z_a, prm_a, after=(w_got,))
     w_b = with_other_half(w_got, pw_a)
     c_got = lax.all_gather(late(c_got, pw_a), "zline", axis=1, tiled=True)
     half = NBLK // 2
@@ -815,7 +826,7 @@
             ds, cda, cm,
         )
 
-    def states_step(j, dbc, sda, scm):
+    def states_step(j, dbc, sda, scm, after=()):
         last = j * CB + CB - 1
 
         def bt(width):
@@ -839,6 +850,7 @@
             [pltpu.VMEM((BLK + 8, 128), f32), pltpu.VMEM((BLK + 8, 128), f32)],
             flops=CHEAP,
             moved=CHEAP,
+            after=after,
         )(dbc, bca_near, bcp_near, msk, kern_near, sda, scm)
 
     def dn_step(dz, dxp, ddt, dbc, after=()):
@@ -858,12 +870,12 @@
             after=after,
         )(dz, dxp, ddt, dbc, w_a, w_b, wdt_t)
 
-    def near_step(total, dsp):
+    def near_step(total, dsp, after):
         mine_first = [dsp[:, : 4 * cols]] + [
             lax.ppermute(dsp[:, : 4 * cols], "zline", [(i, (i + k) % groups) for i in range(groups)])
             for k in range(1, groups)
         ]
-        total = total[:, :wide].astype(f32) + nn(jnp.concatenate(mine_first, axis=1), wbc_near)
+        total = late(total[:, :wide].astype(f32), after) + nn(jnp.concatenate(mine_first, axis=1), wbc_near)
         keep = lax.dynamic_slice_in_dim(total, mine * local_dim, local_dim, 1)
         give = lax.dynamic_slice_in_dim(total, (1 - mine) * local_dim, local_dim, 1)
         return keep, swap(give.astype(bf16))
@@ -911,9 +923,28 @@
     def core_sum(keep, give):
         return keep + cross(give, 1)
 
-    def pair_sum(v):
+    def pair_sum(v, after):
         n = v.shape[1] // 2
-        return v[:, :n] + swap(v[:, n:].astype(bf16)).astype(f32)
+        return late(v[:, :n], after) + swap(v[:, n:].astype(bf16)).astype(f32)
+
+    def chip_sum(v):
+        bit = 2
+        while bit < nrows:
+            size = v.shape[0] // 2
+            up = bit_of(bit)
+            give = rows_of(v, (1 - up) * size, size)
+            v = rows_of(v, up * size, size) + cross(give.astype(bf16), bit).astype(f32)
+            bit *= 2
+        return lax.reduce_precision(v, 8, 7).astype(bf16)
+
+    def chip_parts(v):
+        bit = nrows
+        while bit > 2:
+            bit //= 2
+            got = cross(v, bit)
+            low = bit_of(bit) == 0
+            v = jnp.concatenate([jnp.where(low, v, got), jnp.where(low, got, v)], axis=0)
+        return v
 
     dz, dy, yn, mtg, scales = ([None] * CHUNKS for _ in range(5))
     dxp, ddt, dsp, near, far, dns = ([None] * CHUNKS for _ in range(6))
@@ -939,62 +970,41 @@
     ggs.append(gg)
     g_out = weight_grad(c_all, yn)
     g_z = weight_grad([normed] * CHUNKS, dz)
+    dsp[1], mtc_1, acc_bc, *state_carry = states_step(1, total_1, *state_carry)
+    accs_bc.append(acc_bc)
     dxp[0], ddt[0], dbc_0, mtb_0, acc, acc_dt, *carry = back_step(0, dy[0], *carry)
     accs.append(acc)
     accs_dt.append(acc_dt)
-    dsp[1], mtc_1, acc_bc, *state_carry = states_step(1, total_1, *state_carry)
-    accs_bc.append(acc_bc)
+    near[1], far[1] = near_step(total_1, dsp[1], dbc_0)
     out_sum, z_sum = core_sum(*g_out), core_sum(*g_z)
     g_x = weight_grad([normed] * CHUNKS, dxp, after=(out_sum, z_sum))
     x_sum = core_sum(*g_x)
-    out_sum = pair_sum(out_sum)
-    dns[0] = dn_step(dz[0], dxp[0], ddt[0], dbc_0, after=(out_sum,))
+    out_sum, z_sum = pair_sum(out_sum, dbc_0), pair_sum(z_sum, dbc_0)
+    dns[0] = dn_step(dz[0], dxp[0], ddt[0], dbc_0, after=(out_sum, z_sum, near[1]))
     total_0 = line_scatter(dns[0], 0)
+    x_part = chip_sum(pair_sum(x_sum, total_0))
     dsp[0], mtc_0, acc_bc, *state_carry = states_step(0, total_0, *state_carry)
+    g_x = chip_parts(x_part)
     accs_bc.append(acc_bc)
 
-    dsp_near = jnp.concatenate(dsp, axis=0)[:, : 4 * cols].reshape(LEN, 2, 2, cols)
-    ddt_all = jnp.concatenate(ddt, axis=0)
     width = 2 * cols + heads
-
-    def few(q):
-        sel = lax.dynamic_index_in_dim(dsp_near, q, 2, keepdims=False).reshape(LEN, 2 * cols)
-        dts = lax.dynamic_slice_in_dim(ddt_all, jnp.where(q == mine, 0, heads), heads, 1)
-        return jnp.concatenate([sel, dts, jnp.zeros((LEN, 128 - width), bf16)], axis=1)
-
-    fewer = jnp.concatenate([few(mine), few(1 - mine)], axis=1)
     g_few = ordered(
-        few_kernel,
+        functools.partial(few_kernel, cols, heads),
         8,
-        [pl.BlockSpec((LEN, dim // 8), lambda i: (0, i)), whole(LEN, fewer.shape[1])],
-        pl.BlockSpec((fewer.shape[1], dim // 8), lambda i: (0, i)),
-        sds((fewer.shape[1], dim), f32),
+        [pl.BlockSpec((LEN, dim // 8), lambda i, mine: (0, i))] + [whole(CT, 128)] * 4,
+        pl.BlockSpec((256, dim // 8), lambda i, mine: (0, i)),
+        sds((256, dim), f32),
+        [pltpu.VMEM((LEN, 256), bf16)],
         flops=CHEAP,
         moved=CHEAP,
-    )(normed, fewer)
-    near[1], far[1] = near_step(total_1, dsp[1])
-    near[0], far[0] = near_step(total_0, dsp[0])
+        prefetch=1,
+    )(which, normed, dsp[0], dsp[1], ddt[0], ddt[1])
+    near[0], far[0] = near_step(total_0, dsp[0], total_0)
     local_sum = [
         mtg[j][:, 0] + m[:, 0] + n[:, 0] for j, m, n in ((0, mtb_0, mtc_0), (1, mtb_1, mtc_1))
     ]
     mean_sum = line_sum(jnp.concatenate(local_sum))
     mixer = jnp.concatenate([mixed_0, mixed_1], axis=0).astype(f32)
-
-    def reduce_rows(v):
-        bit = 2
-        while bit < nrows:
-            size = v.shape[0] // 2
-            up = bit_of(bit)
-            give = rows_of(v, (1 - up) * size, size)
-            v = rows_of(v, up * size, size) + cross(give.astype(bf16), bit).astype(f32)
-            bit *= 2
-        v = lax.reduce_precision(v, 8, 7).astype(bf16)
-        while bit > 2:
-            bit //= 2
-            got = cross(v, bit)
-            low = bit_of(bit) == 0
-            v = jnp.concatenate([jnp.where(low, v, got), jnp.where(low, got, v)], axis=0)
-        return v
 
     def both_cores(v):
         got = cross(v, 1)
@@ -1008,7 +1018,7 @@
             bit *= 2
         return v
 
-    g_x, g_z, g_out = (reduce_rows(v) for v in (pair_sum(x_sum), pair_sum(z_sum), out_sum))
+    g_z, g_out = (chip_parts(chip_sum(v)) for v in (z_sum, out_sum))
     g_few = rows_sum(g_few[:width] + swap(g_few[128 : 128 + width].astype(bf16)).astype(f32))
     g_out = both_cores(g_out)
     grad_w_out = jnp.concatenate(

time: 764 us -> 724 us (0.948)
  waiting for transfers between devices: 193 us -> 151 us
  local copies, waits for them, and re-layouts: 78.9 us -> 89.3 us
  Pallas kernels: 328 us -> 318 us
    ppermute x16, waiting for transfers between devices: 114 us -> 50.7 us  [swap(): return lax.ppermute(v, 'pair', [(0, 1), (1, 0)])]
    reduce_scatter x4, waiting for transfers between devices: 5.27 us -> 26.2 us  [line_scatter(): return lax.psum_scatter(v, 'zline', scatter_dimension=axis, tiled=True)]
    ppermute x6, waiting for transfers between devices: 12.2 us -> 0.02 us  [near_step(): lax.ppermute(dsp[:, :4 * cols], 'zline', [(i, (i + k) % groups) for i in...]
    ppermute x22, waiting for transfers between devices: 35.8 us -> 47.6 us  [cross(): return lax.ppermute(v, 'rows', [(i, i ^ bit) for i in range(nrows)])]
    pallas_call x24, Pallas kernels: 328 us -> 318 us  [call(): return lambda *args: fn(*args, *after, *into)]
    unnamed x144 -> x149, local copies, waits for them, and re-layouts: 25.2 us -> 32.8 us
  transfers between devices with their start and end apart: 57 -> 57, of which waited for: 21 -> 21; matrix products, arithmetic and copies ran while one was open for 21% -> 23% of each run, Pallas kernels for 41% -> 41%
where the time goes in v4:
time: 724 us; the launch traced here: 714 us
  Pallas kernels  318 us (44%)
  waiting for transfers between devices  151 us (21%)
  local copies, waits for them, and re-layouts  89.3 us (12%)
  other arithmetic  87.6 us (12%)
  starting transfers between devices  44.8 us (6%)
  between operations  19.1 us (3%)
    pallas_call x24, Pallas kernels, call(): return lambda *args: fn(*args, *after, *into)  318 us
    ppermute x16, waiting for transfers between devices, swap(): return lax.ppermute(v, 'pair', [(0, 1), (1, 0)])  50.7 us
    ppermute x22, waiting for transfers between devices, cross(): return lax.ppermute(v, 'rows', [(i, i ^ bit) for i in range(nrows)])  47.6 us
    unnamed x149, local copies, waits for them, and re-layouts  32.8 us
    reduce_scatter x4, waiting for transfers between devices, line_scatter(): return lax.psum_scatter(v, 'zline', scatter_dimension=axis, tiled=True)  26.2 us
    ppermute x16, starting transfers between devices, swap(): return lax.ppermute(v, 'pair', [(0, 1), (1, 0)])  17.8 us
  transfers between devices with their start and end apart: 57, of which 21 were waited for; matrix products, arithmetic and copies ran while one was open for 23% of the time, Pallas kernels for 41%

profile of v4, /device:TPU:0, one launch (start us, length us, event | category | flops | bytes accessed | tf_op | source)
XLA Modules:
  0.0 714.2 jit_solution(12102664027971811310)
XLA Ops:
  21.0 5.5 copy.126
  38.0 20.3 %shard_map.271 = (bf16[2048,2048]{1,0:T(8,128)(2,1)}, f32[2048,128]{1,0:T(8,128)}, bf16[2048,512]{1,0:T(8,128)(2,1)}, bf16[2048,512]{1,0:T(8,128)(2,1)}, bf16[20...) custom-call(s32[1]{0:T(128)} %bitcast.refs_0_, bf16[4096,2048]{1,0:T(8,128)(2,1)} %refs_1_.1, ...), custom_call_target="tpu_custom_call" | custom-call | flops 8589934592 | bytes 41943040 | tf_op jit(solution)/shard_map/pallas_call | solution.py:502
  65.5 15.6 %shard_map.272 = (f32[2048,256]{1,0:T(8,128)}, f32[2048,256]{1,0:T(8,128)}, bf16[2048,256]{1,0:T(8,128)(2,1)}, f32[2048,128]{1,0:T(8,128)}, f32[2048,128]{1,0:T(...) custom-call(bf16[2048,2048]{1,0:T(8,128)(2,1)} %get-tuple-element.103.refs_0_.refs_1_.refs_2_, ...), custom_call_target="tpu_custom_call" | custom-call | flops 4294967296 | bytes 18874368 | tf_op jit(solution)/shard_map/pallas_call | solution.py:502
  81.1 26.4 %collective-permute-done.2.refs_8_ = bf16[1024,1024]{1,0:T(8,128)(2,1)} collective-permute-done((bf16[1024,1024]{1,0:T(8,128)(2,1)S(1)}, bf16[1024,1024]{1,0:T(8,128)(2,1)}, u32[]{:S(2)}, u32[]{:S(2)}) %collective-permute-start.2) | collective-permute-done | bytes 2097184 | tf_op jit(solution)/shard_map/ppermute | solution.py:542
  108.2 16.6 %shard_map.273 = (f32[2048,512]{1,0:T(8,128)}, bf16[2048,512]{1,0:T(8,128)(2,1)}, f32[8,128,512]{2,1,0:T(8,128)}, f32[2048,128]{1,0:T(8,128)}, f32[128,512]{1,0:T(8,128)}) custom-call(bf16[2048,512]{1,0:T(8,128)(2,1)} %get-tuple-element.101.refs_0_.refs_10_, bf16[2048,512]{1,0:T(8,128)(2,1)} %get-tuple-element.102.refs_1_.refs_5_, ...), custom_call_target="tpu_custom_call" | custom-call | flops 10737418240 | bytes 20971520 | tf_op jit(solution)/shard_map/pallas_call | solution.py:502
  140.0 10.7 %shard_map.274 = (bf16[2048,512]{1,0:T(8,128)(2,1)}, bf16[2048,512]{1,0:T(8,128)(2,1)}, bf16[2048,512]{1,0:T(8,128)(2,1)}, bf16[2048,512]{1,0:T(8,128)(2,1)}, f32[8,512]{1,0:T(8,128)}) custom-call(bf16[2048,2048]{1,0:T(8,128)(2,1)} %get-tuple-element.103.refs_0_.refs_1_.refs_2_, bf16[2048,1024]{1,0:T(8,128)(2,1)} %pad_maximum_fusion.1.refs_1_.refs_5_, ...), custom_call_target="tpu_custom_call" | custom-call | flops 4294967296 | bytes 14680064 | tf_op jit(solution)/shard_map/pallas_call | solution.py:502
  159.9 9.5 %shard_map.275 = (f32[2048,512]{1,0:T(8,128)}, bf16[2048,512]{1,0:T(8,128)(2,1)}, f32[8,128,512]{2,1,0:T(8,128)}, f32[2048,128]{1,0:T(8,128)}, f32[128,512]{1,0:T(8,128)}) custom-call(bf16[2048,512]{1,0:T(8,128)(2,1)} %get-tuple-element.112.refs_0_.refs_9_, bf16[2048,512]{1,0:T(8,128)(2,1)} %get-tuple-element.113.refs_1_.refs_6_, ...), custom_call_target="tpu_custom_call" | custom-call | flops 5368709120 | bytes 10485760 | tf_op jit(solution)/shard_map/pallas_call | solution.py:502
  179.8 8.7 %shard_map.276.refs_5_ = bf16[1024,2048]{1,0:T(8,128)(2,1)} custom-call(bf16[2048,512]{1,0:T(8,128)(2,1)} %get-tuple-element.109.refs_0_.refs_3_, bf16[2048,512]{1,0:T(8,128)(2,1)} %get-tuple-element.115.refs_1_.refs_10_, bf16[512,2048]{1,0:T(8,128)(2,1)} %refs_2_.3, bf16[512,2048]{1,0:T(8,128)(2,1)} %pad_maximum_fusion.refs_3_, ...), custom_call_target="tpu_custom_call" | custom-call | flops 4294967296 | bytes 10485760 | tf_op jit(solution)/shard_map/pallas_call | solution.py:502
  189.5 10.7 %shard_map.277 = (bf16[2048,512]{1,0:T(8,128)(2,1)}, bf16[2048,512]{1,0:T(8,128)(2,1)}, bf16[2048,512]{1,0:T(8,128)(2,1)}, bf16[2048,512]{1,0:T(8,128)(2,1)}, f32[8,512]{1,0:T(8,128)}) custom-call(bf16[2048,2048]{1,0:T(8,128)(2,1)} %get-tuple-element.103.refs_0_.refs_1_.refs_2_, ...), custom_call_target="tpu_custom_call", output_to_operand_aliasing={{0}: (6, {}), {1}: (7, {}), {2}: (8, {}), {3}: (9, {})} | custom-call | flops 4294967296 | bytes 14680064 | tf_op jit(solution)/shard_map/pallas_call | solution.py:502
  200.2 9.6 %shard_map.278 = (f32[2048,512]{1,0:T(8,128)}, bf16[2048,512]{1,0:T(8,128)(2,1)}, f32[8,128,512]{2,1,0:T(8,128)}, f32[2048,128]{1,0:T(8,128)}, f32[128,512]{1,0:T(8,128)}) custom-call(bf16[2048,512]{1,0:T(8,128)(2,1)} %get-tuple-element.119.refs_0_.refs_11_, ...), custom_call_target="tpu_custom_call", output_to_operand_aliasing={{0}: (9, {}), {1}: (10, {}), {2}: (11, {}), {3}: (12, {})} | custom-call | flops 5368709120 | bytes 10485760 | tf_op jit(solution)/shard_map/pallas_call | solution.py:502
  211.2 11.5 %all-gather.8.cloned.1.call-done = bf16[2048,1024]{1,0:T(8,128)(2,1)} async-done(((bf16[2048,256]{1,0:T(8,128)(2,1)}), bf16[2048,1024]{1,0:T(8,128)(2,1)}) %all-gather.8.cloned.1.call-update) | async-done | bytes 4194320 | tf_op jit(solution)/shard_map/all_gather | solution.py:714
  230.0 9.1 %shard_map.279 = (bf16[1024,512]{1,0:T(8,128)(2,1)}, bf16[1024,512]{1,0:T(8,128)(2,1)}, f32[1024,128]{1,0:T(8,128)}) custom-call(bf16[1024,2048]{1,0:T(8,128)(2,1)} %pad_maximum_fusion.3.refs_0_.refs_2_, bf16[512,2048]{1,0:T(8,128)(2,1)} %slice_dynamic-update-slice_fusion.8.refs_1_, bf16[512,2048]{1,0:T(8,128)(2,1)} %fusion.39.refs_2_, ...), custom_call_target="tpu_custom_call" | custom-call | flops 4294967296 | bytes 12582912 | tf_op jit(solution)/shard_map/pallas_call | solution.py:502
  251.3 8.7 %shard_map.280 = (bf16[1024,1024]{1,0:T(8,128)(2,1)}, bf16[1024,1024]{1,0:T(8,128)(2,1)}, bf16[1024,1024]{1,0:T(8,128)(2,1)}, f32[1024,128]{1,0:T(8,128)}, f32[8,1024]{1,0:T(8,128)}) custom-call(f32[1024,128]{1,0:T(8,128)} %pad.48.refs_0_, bf16[1024,512]{1,0:T(8,128)(2,1)} %get-tuple-element.129.refs_1_, bf16[1024,512]{1,0:T(8,128)(2,1)} %get-tuple-element.130.refs_2_, ...), custom_call_target="tpu_custom_call" | custom-call | flops 2097152000 | bytes 20971520 | tf_op jit(solution)/shard_map/pallas_call | solution.py:502
  262.1 32.7 %shard_map.281 = (bf16[1024,1024]{1,0:T(8,128)(2,1)}, bf16[1024,128]{1,0:T(8,128)(2,1)}, bf16[1024,256]{1,0:T(8,128)(2,1)}, f32[1024,128]{1,0:T(8,128)}, f32[2,4...) custom-call(bf16[1024,1024]{1,0:T(8,128)(2,1)} %get-tuple-element.13, ...), custom_call_target="tpu_custom_call" | custom-call | flops 42949672960 | bytes 41943040 | tf_op jit(solution)/shard_map/pallas_call | solution.py:502
  294.8 5.3 reduce-scatter.5.cloned.1.call-done.refs_7_
  300.1 15.6 %shard_map.282.refs_5_ = bf16[4096,640]{1,0:T(8,128)(2,1)} custom-call(bf16[1024,1024]{1,0:T(8,128)(2,1)} %get-tuple-element.133.refs_0_.refs_4_, bf16[1024,1024]{1,0:T(8,128)(2,1)} %get-tuple-element.143.refs_1_.refs_4_, bf16[1024,128]{1,0:T(8,128)(2,1)} %get-tuple-element.144.refs_2_.refs_5_, bf16[1024,256]{1,0:T(8,128)(2,1)} %get-tuple-element.145.refs_3_, ...), custom_call_target="tpu_custom_call" | custom-call | flops 8589934592 | bytes 16777216 | tf_op jit(solution)/shard_map/pallas_call | solution.py:502
  319.8 10.1 %shard_map.283 = (bf16[1024,512]{1,0:T(8,128)(2,1)}, bf16[1024,512]{1,0:T(8,128)(2,1)}, f32[1024,128]{1,0:T(8,128)}) custom-call(bf16[1024,2048]{1,0:T(8,128)(2,1)} %pad_maximum_fusion.2.refs_0_.refs_1_, bf16[512,2048]{1,0:T(8,128)(2,1)} %slice_dynamic-update-slice_fusion.8.refs_1_, bf16[512,2048]{1,0:T(8,128)(2,1)} %fusion.39.refs_2_, ...), custom_call_target="tpu_custom_call" | custom-call | flops 4294967296 | bytes 12582912 | tf_op jit(solution)/shard_map/pallas_call | solution.py:502
  337.9 8.6 %shard_map.284.refs_9_ = bf16[1024,2048]{1,0:T(8,128)(2,1)} custom-call(bf16[2048,512]{1,0:T(8,128)(2,1)} %get-tuple-element.109.refs_0_.refs_3_, bf16[2048,512]{1,0:T(8,128)(2,1)} %get-tuple-element.125.refs_4_.refs_1_, bf16[512,2048]{1,0:T(8,128)(2,1)} %refs_2_.3, bf16[512,2048]{1,0:T(8,128)(2,1)} %pad_maximum_fusion.refs_3_, ...), custom_call_target="tpu_custom_call" | custom-call | flops 4294967296 | bytes 10485760 | tf_op jit(solution)/shard_map/pallas_call | solution.py:502
  347.6 9.0 %shard_map.285 = (bf16[1024,1024]{1,0:T(8,128)(2,1)}, bf16[1024,1024]{1,0:T(8,128)(2,1)}, bf16[1024,1024]{1,0:T(8,128)(2,1)}, f32[1024,128]{1,0:T(8,128)}, f32[8,1024]{1,0:T(8,128)}) custom-call(f32[1024,128]{1,0:T(8,128)} %pad.49.refs_0_, bf16[1024,512]{1,0:T(8,128)(2,1)} %get-tuple-element.149.refs_1_, bf16[1024,512]{1,0:T(8,128)(2,1)} %get-tuple-element.150.refs_2_, ...), custom_call_target="tpu_custom_call" | custom-call | flops 2097152000 | bytes 20971520 | tf_op jit(solution)/shard_map/pallas_call | solution.py:502
  356.6 15.6 %shard_map.286 = (f32[1024,1024]{1,0:T(8,128)}, f32[1024,1024]{1,0:T(8,128)}) custom-call(s32[1]{0:T(128)} %bitcast.35.refs_0_, bf16[1024,2048]{1,0:T(8,128)(2,1)} %pad_maximum_fusion.2.refs_0_.refs_1_, bf16[1024,2048]{1,0:T(8,128)(2,1)} %pad_maximum_fusion.3.refs_0_.refs_2_, bf16[1024,1024]{1,0:T(8,128)(2,1)} %get-tuple-element.157.refs_3_, ...), custom_call_target="tpu_custom_call" | custom-call | flops 65536 | bytes 65536 | tf_op jit(solution)/shard_map/pallas_call | solution.py:502
  372.2 15.6 %shard_map.287 = (f32[1024,1024]{1,0:T(8,128)}, f32[1024,1024]{1,0:T(8,128)}) custom-call(s32[1]{0:T(128)} %bitcast.35.refs_0_, bf16[2048,2048]{1,0:T(8,128)(2,1)} %get-tuple-element.103.refs_0_.refs_1_.refs_2_, bf16[2048,2048]{1,0:T(8,128)(2,1)} %get-tuple-element.103.refs_0_.refs_1_.refs_2_, bf16[1024,1024]{1,0:T(8,128)(2,1)} %get-tuple-element.151.refs_3_.refs_0_, ...), custom_call_target="tpu_custom_call" | custom-call | flops 65536 | bytes 65536 | tf_op jit(solution)/shard_map/pallas_call | solution.py:502
  420.2 32.7 %shard_map.289 = (bf16[1024,1024]{1,0:T(8,128)(2,1)}, bf16[1024,128]{1,0:T(8,128)(2,1)}, bf16[1024,256]{1,0:T(8,128)(2,1)}, f32[1024,128]{1,0:T(8,128)}, f32[2,4...) custom-call(bf16[1024,1024]{1,0:T(8,128)(2,1)} %get-tuple-element.15, ...), custom_call_target="tpu_custom_call" | custom-call | flops 42949672960 | bytes 41943040 | tf_op jit(solution)/shard_map/pallas_call | solution.py:502
  461.3 15.6 %shard_map.290 = (f32[1024,1024]{1,0:T(8,128)}, f32[1024,1024]{1,0:T(8,128)}) custom-call(s32[1]{0:T(128)} %bitcast.35.refs_0_, bf16[2048,2048]{1,0:T(8,128)(2,1)} %get-tuple-element.103.refs_0_.refs_1_.refs_2_, bf16[2048,2048]{1,0:T(8,128)(2,1)} %get-tuple-element.103.refs_0_.refs_1_.refs_2_, bf16[1024,1024]{1,0:T(8,128)(2,1)} %get-tuple-element.163.refs_3_.refs_1_, ...), custom_call_target="tpu_custom_call" | custom-call | flops 65536 | bytes 65536 | tf_op jit(solution)/shard_map/pallas_call | solution.py:502
  481.1 15.8 %shard_map.291.refs_7_ = bf16[4096,640]{1,0:T(8,128)(2,1)} custom-call(bf16[1024,1024]{1,0:T(8,128)(2,1)} %get-tuple-element.151.refs_3_.refs_0_, bf16[1024,1024]{1,0:T(8,128)(2,1)} %get-tuple-element.163.refs_3_.refs_1_, bf16[1024,128]{1,0:T(8,128)(2,1)} %get-tuple-element.164.refs_2_.refs_4_, bf16[1024,256]{1,0:T(8,128)(2,1)} %get-tuple-element.165.refs_3_, ...), custom_call_target="tpu_custom_call" | custom-call | flops 8589934592 | bytes 16777216 | tf_op jit(solution)/shard_map/pallas_call | solution.py:502
  513.6 11.2 %collective-permute-done.47 = bf16[512,512]{1,0:T(8,128)(2,1)S(1)} collective-permute-done((bf16[512,512]{1,0:T(8,128)(2,1)S(1)}, bf16[512,512]{1,0:T(8,128)(2,1)S(1)}, u32[]{:S(2)}, u32[]{:S(2)}) %collective-permute-start.47) | collective-permute-done | bytes 524320 | tf_op jit(solution)/shard_map/ppermute | solution.py:545
  532.3 17.9 %collective-permute-done.43 = f32[8,512]{1,0:T(8,128)S(1)} collective-permute-done((f32[8,512]{1,0:T(8,128)S(1)}, f32[8,512]{1,0:T(8,128)S(1)}, u32[]{:S(2)}, u32[]{:S(2)}) %collective-permute-start.43) | collective-permute-done | bytes 16416 | tf_op jit(solution)/shard_map/ppermute | solution.py:545
  557.3 9.2 %collective-permute-done.31 = bf16[512,512]{1,0:T(8,128)(2,1)S(1)} collective-permute-done((bf16[512,512]{1,0:T(8,128)(2,1)S(1)}, bf16[512,512]{1,0:T(8,128)(2,1)S(1)}, u32[]{:S(2)}, u32[]{:S(2)}) %collective-permute-start.31) | collective-permute-done | bytes 524320 | tf_op jit(solution)/shard_map/ppermute | solution.py:545
  584.9 20.8 %reduce-scatter.11.cloned.1.call-done.refs_0_ = bf16[1024,640]{1,0:T(8,128)(2,1)} async-done(((bf16[4096,640]{1,0:T(8,128)(2,1)}), bf16[1024,640]{1,0:T(8,128)(2,1)}) %reduce-scatter.11.cloned.1.call-update) | async-done | bytes 1310736 | tf_op jit(solution)/shard_map/reduce_scatter | solution.py:658
  624.5 10.0 %shard_map.293.refs_5_ = f32[256,2048]{1,0:T(8,128)} custom-call(s32[1]{0:T(128)} %bitcast.refs_0_, bf16[2048,2048]{1,0:T(8,128)(2,1)} %get-tuple-element.103.refs_0_.refs_1_.refs_2_, bf16[1024,128]{1,0:T(8,128)(2,1)} %get-tuple-element.172.refs_2_, bf16[1024,128]{1,0:T(8,128)(2,1)} %get-tuple-element.168.refs_3_, ...), custom_call_target="tpu_custom_call" | custom-call | flops 65536 | bytes 65536 | tf_op jit(solution)/shard_map/pallas_call | solution.py:502
  651.7 10.5 %collective-permute-done.38 = bf16[40,2048]{1,0:T(8,128)(2,1)S(1)} collective-permute-done((bf16[40,2048]{1,0:T(8,128)(2,1)}, bf16[40,2048]{1,0:T(8,128)(2,1)S(1)}, u32[]{:S(2)}, u32[]{:S(2)}) %collective-permute-start.38) | collective-permute-done | bytes 163872 | tf_op jit(solution)/shard_map/ppermute | solution.py:542
  681.9 5.6 collective-permute-done.36
  697.6 9.5 %shard_map.294 = f32[16384,128]{1,0:T(8,128)} custom-call(s32[1]{0:T(128)} %bitcast.35.refs_0_, bf16[1024,512]{1,0:T(8,128)(2,1)} %pad_maximum_fusion.8.refs_1_, bf16[1024,512]{1,0:T(8,128)(2,1)} %copy-done.21, bf16[1024,512]{1,0:T(8,128)(2,1)} %copy-done.17, bf16[1024,512]{1,0:T(8,128)(2,1)} %copy-done.22, f32[256,2048]{1,0:T(8,128)} %shard_map.293.refs_5_), custom_call_target="tpu_custom_call" | custom-call | bytes 25165824 | tf_op jit(solution)/shard_map/pallas_call | solution.py:502
  (437 shorter events, 260.9 us)
Async XLA Ops:
  7.2 53.9 %all-gather.4.cloned.1.call-start = ((), (), s32[]{:S(2)}) async-start(), calls=%async_computation.4 | async-start | bytes 1253376 | tf_op jit(solution)/shard_map/all_gather | solution.py:598
  11.4 199.8 %all-gather.6.cloned.1.call-start = ((), (), s32[]{:S(2)}) async-start(), calls=%async_computation.6 | async-start | bytes 5242880 | tf_op jit(solution)/shard_map/all_gather | solution.py:604
  14.5 208.2 %all-gather.8.cloned.1.call-start = ((), (), s32[]{:S(2)}) async-start(), calls=%async_computation.7 | async-start | bytes 5242880 | tf_op jit(solution)/shard_map/all_gather | solution.py:714
  19.0 107.9 %collective-permute-start.6 = (bf16[2048,256]{1,0:T(8,128)(2,1)}, bf16[2048,256]{1,0:T(8,128)(2,1)}, u32[]{:S(2)}, u32[]{:S(2)}) collective-permute-start(bf16[2048,256]{1,0:T(8,128)(2,1)} %get-tuple-element.272), channel_id=1, source_target_pairs={{0,1},{1,0},{2,3},{3,2},{4,5},{5,4},{6,7},{7,6},{8,9},{9,8},{10,11... | collective-permute-start | bytes 3145736 | tf_op jit(solution)/shard_map/ppermute | solution.py:542
  28.2 79.3 %collective-permute-start.2 = (bf16[1024,1024]{1,0:T(8,128)(2,1)S(1)}, bf16[1024,1024]{1,0:T(8,128)(2,1)}, u32[]{:S(2)}, u32[]{:S(2)}) collective-permute-start(bf16[1024,1024]{1,0:T(8,128)(2,1)S(1)} %constant_dynamic-slice_fusion.15), channel_id=1, source_target_pairs={{0,1},{1,0},{2,3},{3,2},{4,5},{5,4},{6,7},{7,6},{8,9},{9,8},{10,11... | collective-permute-start | bytes 6291464 | tf_op jit(solution)/shard_map/ppermute | solution.py:542
  107.5 27.5 %collective-permute-start.3 = (bf16[1024,1024]{1,0:T(8,128)(2,1)}, bf16[1024,1024]{1,0:T(8,128)(2,1)}, u32[]{:S(2)}, u32[]{:S(2)}) collective-permute-start(bf16[1024,1024]{1,0:T(8,128)(2,1)} %collective-permute-done.2.refs_8_), channel_id=1, source_target_pairs={{0,8},{8,0},{16,24},{24,16},{1,9},{9,1},{17,25},{25,17},{2,10},{10... | collective-permute-start | bytes 6291464 | tf_op jit(solution)/shard_map/ppermute | solution.py:545
  129.2 170.9 %reduce-scatter.5.cloned.1.call-start = ((), (), s32[]{:S(2)}) async-start(), calls=%async_computation.5 | async-start | bytes 5242880 | tf_op jit(solution)/shard_map/reduce_scatter | solution.py:658
  130.8 25.8 %collective-permute-start.4 = (bf16[256,2048]{1,0:T(8,128)(2,1)}, bf16[256,2048]{1,0:T(8,128)(2,1)S(1)}, u32[]{:S(2)}, u32[]{:S(2)}) collective-permute-start(bf16[256,2048]{1,0:T(8,128)(2,1)} %constant_dynamic-slice_fusion.14), channel_id=1, source_target_pairs={{0,1},{1,0},{2,3},{3,2},{4,5},{5,4},{6,7},{7,6},{8,9},{9,8},{10,11... | collective-permute-start | bytes 3145736 | tf_op jit(solution)/shard_map/ppermute | solution.py:542
  188.5 223.2 %reduce-scatter.9.cloned.1.call-start = ((), (), s32[]{:S(2)}) async-start(), calls=%async_computation.9 | async-start | bytes 6553600 | tf_op jit(solution)/shard_map/reduce_scatter | solution.py:658
  315.7 190.8 %reduce-scatter.7.cloned.1.call-start = ((), (), s32[]{:S(2)}) async-start(), calls=%async_computation.8 | async-start | bytes 5242880 | tf_op jit(solution)/shard_map/reduce_scatter | solution.py:658
  372.2 26.9 %collective-permute-start.13 = (f32[1024,1024]{1,0:T(8,128)}, f32[1024,1024]{1,0:T(8,128)}, u32[]{:S(2)}, u32[]{:S(2)}) collective-permute-start(f32[1024,1024]{1,0:T(8,128)} %get-tuple-element.160.refs_5_), channel_id=1, source_target_pairs={{0,8},{8,0},{16,24},{24,16},{1,9},{9,1},{17,25},{25,17},{2,10},{10... | collective-permute-start | bytes 12582920 | tf_op jit(solution)/shard_map/ppermute | solution.py:545
  387.8 17.6 %collective-permute-start.15 = (f32[1024,1024]{1,0:T(8,128)}, f32[1024,1024]{1,0:T(8,128)}, u32[]{:S(2)}, u32[]{:S(2)}) collective-permute-start(f32[1024,1024]{1,0:T(8,128)} %get-tuple-element.161.refs_7_), channel_id=1, source_target_pairs={{0,8},{8,0},{16,24},{24,16},{1,9},{9,1},{17,25},{25,17},{2,10},{10... | collective-permute-start | bytes 12582920 | tf_op jit(solution)/shard_map/ppermute | solution.py:545
  388.2 217.6 %reduce-scatter.11.cloned.1.call-start = ((), (), s32[]{:S(2)}) async-start(), calls=%async_computation.10 | async-start | bytes 6553600 | tf_op jit(solution)/shard_map/reduce_scatter | solution.py:658
  403.8 51.7 %collective-permute-start.14 = (bf16[1024,512]{1,0:T(8,128)(2,1)S(1)}, bf16[1024,512]{1,0:T(8,128)(2,1)S(1)}, u32[]{:S(2)}, u32[]{:S(2)}) collective-permute-start(bf16[1024,512]{1,0:T(8,128)(2,1)S(1)} %slice.617), channel_id=1, source_target_pairs={{0,1},{1,0},{2,3},{3,2},{4,5},{5,4},{6,7},{7,6},{8,9},{9,8},{10,11... | collective-permute-start | bytes 3145736 | tf_op jit(solution)/shard_map/ppermute | solution.py:542
  410.6 46.7 %collective-permute-start.16 = (bf16[1024,512]{1,0:T(8,128)(2,1)S(1)}, bf16[1024,512]{1,0:T(8,128)(2,1)}, u32[]{:S(2)}, u32[]{:S(2)}) collective-permute-start(bf16[1024,512]{1,0:T(8,128)(2,1)S(1)} %slice.616), channel_id=1, source_target_pairs={{0,1},{1,0},{2,3},{3,2},{4,5},{5,4},{6,7},{7,6},{8,9},{9,8},{10,11... | collective-permute-start | bytes 3145736 | tf_op jit(solution)/shard_map/ppermute | solution.py:542
  415.8 61.2 %collective-permute-start.19 = (bf16[1024,64]{1,0:T(8,128)(2,1)}, bf16[1024,64]{1,0:T(8,128)(2,1)}, u32[]{:S(2)}, u32[]{:S(2)}) collective-permute-start(bf16[1024,64]{1,0:T(8,128)(2,1)} %bitcast.123), channel_id=1, source_target_pairs={{0,6},{2,0},{4,2},{6,4},{1,7},{3,1},{5,3},{7,5},{8,14},{10,8},{12,... | collective-permute-start | bytes 393224 | tf_op jit(solution)/shard_map/ppermute | solution.py:875
  418.1 58.8 %collective-permute-start.18 = (bf16[1024,64]{1,0:T(8,128)(2,1)}, bf16[1024,64]{1,0:T(8,128)(2,1)}, u32[]{:S(2)}, u32[]{:S(2)}) collective-permute-start(bf16[1024,64]{1,0:T(8,128)(2,1)} %bitcast.124), channel_id=1, source_target_pairs={{0,4},{2,6},{4,0},{6,2},{1,5},{3,7},{5,1},{7,3},{8,12},{10,14},{12... | collective-permute-start | bytes 393224 | tf_op jit(solution)/shard_map/ppermute | solution.py:875
  420.2 56.7 %collective-permute-start.17 = (bf16[1024,64]{1,0:T(8,128)(2,1)}, bf16[1024,64]{1,0:T(8,128)(2,1)}, u32[]{:S(2)}, u32[]{:S(2)}) collective-permute-start(bf16[1024,64]{1,0:T(8,128)(2,1)} %bitcast.125), channel_id=1, source_target_pairs={{0,2},{2,4},{4,6},{6,0},{1,3},{3,5},{5,7},{7,1},{8,10},{10,12},{12... | collective-permute-start | bytes 393224 | tf_op jit(solution)/shard_map/ppermute | solution.py:875
  510.2 58.0 %collective-permute-start.33 = (f32[1024,1024]{1,0:T(8,128)}, f32[1024,1024]{1,0:T(8,128)}, u32[]{:S(2)}, u32[]{:S(2)}) collective-permute-start(f32[1024,1024]{1,0:T(8,128)} %get-tuple-element.170.refs_10_), channel_id=1, source_target_pairs={{0,8},{8,0},{16,24},{24,16},{1,9},{9,1},{17,25},{25,17},{2,10},{10... | collective-permute-start | bytes 12582920 | tf_op jit(solution)/shard_map/ppermute | solution.py:545
  524.9 25.9 %collective-permute-start.48 = (bf16[512,512]{1,0:T(8,128)(2,1)S(1)}, bf16[512,512]{1,0:T(8,128)(2,1)S(1)}, u32[]{:S(2)}, u32[]{:S(2)}) collective-permute-start(bf16[512,512]{1,0:T(8,128)(2,1)S(1)} %reduce-precision_convert_fusion), channel_id=1, source_target_pairs={{0,16},{8,24},{16,0},{24,8},{1,17},{9,25},{17,1},{25,9},{2,18},{10... | collective-permute-start | bytes 1572872 | tf_op jit(solution)/shard_map/ppermute | solution.py:545
  528.8 148.7 %collective-permute-start.11 = (bf16[2048,256]{1,0:T(8,128)(2,1)}, bf16[2048,256]{1,0:T(8,128)(2,1)}, u32[]{:S(2)}, u32[]{:S(2)}) collective-permute-start(bf16[2048,256]{1,0:T(8,128)(2,1)} %dynamic-slice_convert_fusion), channel_id=1, source_target_pairs={{0,1},{1,0},{2,3},{3,2},{4,5},{5,4},{6,7},{7,6},{8,9},{9,8},{10,11... | collective-permute-start | bytes 3145736 | tf_op jit(solution)/shard_map/ppermute | solution.py:542
  529.9 22.0 %collective-permute-start.30 = (bf16[512,512]{1,0:T(8,128)(2,1)S(1)}, bf16[512,512]{1,0:T(8,128)(2,1)S(1)}, u32[]{:S(2)}, u32[]{:S(2)}) collective-permute-start(bf16[512,512]{1,0:T(8,128)(2,1)S(1)} %dynamic-slice_convert_fusion.4), channel_id=1, source_target_pairs={{0,16},{8,24},{16,0},{24,8},{1,17},{9,25},{17,1},{25,9},{2,18},{10... | collective-permute-start | bytes 1572872 | tf_op jit(solution)/shard_map/ppermute | solution.py:545
  531.0 19.2 %collective-permute-start.43 = (f32[8,512]{1,0:T(8,128)S(1)}, f32[8,512]{1,0:T(8,128)S(1)}, u32[]{:S(2)}, u32[]{:S(2)}) collective-permute-start(f32[8,512]{1,0:T(8,128)S(1)} %add.394), channel_id=1, source_target_pairs={{0,16},{8,24},{16,0},{24,8},{1,17},{9,25},{17,1},{25,9},{2,18},{10... | collective-permute-start | bytes 49160 | tf_op jit(solution)/shard_map/ppermute | solution.py:545
  576.3 40.7 %collective-permute-start.34 = (bf16[1024,512]{1,0:T(8,128)(2,1)}, bf16[1024,512]{1,0:T(8,128)(2,1)}, u32[]{:S(2)}, u32[]{:S(2)}) collective-permute-start(bf16[1024,512]{1,0:T(8,128)(2,1)} %slice.615), channel_id=1, source_target_pairs={{0,1},{1,0},{2,3},{3,2},{4,5},{5,4},{6,7},{7,6},{8,9},{9,8},{10,11... | collective-permute-start | bytes 3145736 | tf_op jit(solution)/shard_map/ppermute | solution.py:542
  609.9 37.1 %collective-permute-start.22 = (bf16[1024,64]{1,0:T(8,128)(2,1)}, bf16[1024,64]{1,0:T(8,128)(2,1)}, u32[]{:S(2)}, u32[]{:S(2)}) collective-permute-start(bf16[1024,64]{1,0:T(8,128)(2,1)} %bitcast.127), channel_id=1, source_target_pairs={{0,6},{2,0},{4,2},{6,4},{1,7},{3,1},{5,3},{7,5},{8,14},{10,8},{12,... | collective-permute-start | bytes 393224 | tf_op jit(solution)/shard_map/ppermute | solution.py:875
  612.5 35.6 %collective-permute-start.21 = (bf16[1024,64]{1,0:T(8,128)(2,1)}, bf16[1024,64]{1,0:T(8,128)(2,1)}, u32[]{:S(2)}, u32[]{:S(2)}) collective-permute-start(bf16[1024,64]{1,0:T(8,128)(2,1)} %bitcast.128), channel_id=1, source_target_pairs={{0,4},{2,6},{4,0},{6,2},{1,5},{3,7},{5,1},{7,3},{8,12},{10,14},{12... | collective-permute-start | bytes 393224 | tf_op jit(solution)/shard_map/ppermute | solution.py:875
  613.0 35.7 %collective-permute-start.20 = (bf16[1024,64]{1,0:T(8,128)(2,1)}, bf16[1024,64]{1,0:T(8,128)(2,1)}, u32[]{:S(2)}, u32[]{:S(2)}) collective-permute-start(bf16[1024,64]{1,0:T(8,128)(2,1)} %bitcast.129), channel_id=1, source_target_pairs={{0,2},{2,4},{4,6},{6,0},{1,3},{3,5},{5,7},{7,1},{8,10},{10,12},{12... | collective-permute-start | bytes 393224 | tf_op jit(solution)/shard_map/ppermute | solution.py:875
  646.1 20.9 %collective-permute-start.24 = (bf16[1024,256]{1,0:T(8,128)(2,1)}, bf16[1024,256]{1,0:T(8,128)(2,1)S(1)}, u32[]{:S(2)}, u32[]{:S(2)}) collective-permute-start(bf16[1024,256]{1,0:T(8,128)(2,1)} %dynamic-slice_convert_fusion.5), channel_id=1, source_target_pairs={{0,1},{1,0},{2,3},{3,2},{4,5},{5,4},{6,7},{7,6},{8,9},{9,8},{10,11... | collective-permute-start | bytes 1572872 | tf_op jit(solution)/shard_map/ppermute | solution.py:542
  648.1 18.0 %collective-permute-start.35 = (bf16[512,512]{1,0:T(8,128)(2,1)}, bf16[512,512]{1,0:T(8,128)(2,1)S(1)}, u32[]{:S(2)}, u32[]{:S(2)}) collective-permute-start(bf16[512,512]{1,0:T(8,128)(2,1)} %dynamic-slice_convert_fusion.3), channel_id=1, source_target_pairs={{0,16},{8,24},{16,0},{24,8},{1,17},{9,25},{17,1},{25,9},{2,18},{10... | collective-permute-start | bytes 1572872 | tf_op jit(solution)/shard_map/ppermute | solution.py:545
  666.0 29.6 %collective-permute-start.32 = (bf16[1024,512]{1,0:T(8,128)(2,1)S(1)}, bf16[1024,512]{1,0:T(8,128)(2,1)S(1)}, u32[]{:S(2)}, u32[]{:S(2)}) collective-permute-start(bf16[1024,512]{1,0:T(8,128)(2,1)S(1)} %copy-done.16), channel_id=1, source_target_pairs={{0,8},{8,0},{16,24},{24,16},{1,9},{9,1},{17,25},{25,17},{2,10},{10... | collective-permute-start | bytes 3145736 | tf_op jit(solution)/shard_map/ppermute | solution.py:545
  666.2 28.0 %collective-permute-start.40 = (f32[40,2048]{1,0:T(8,128)S(1)}, f32[40,2048]{1,0:T(8,128)S(1)}, u32[]{:S(2)}, u32[]{:S(2)}) collective-permute-start(f32[40,2048]{1,0:T(8,128)S(1)} %add.388), channel_id=1, source_target_pairs={{0,16},{8,24},{16,0},{24,8},{1,17},{9,25},{17,1},{25,9},{2,18},{10... | collective-permute-start | bytes 983048 | tf_op jit(solution)/shard_map/ppermute | solution.py:545
  667.0 20.5 %collective-permute-start.36 = (bf16[512,512]{1,0:T(8,128)(2,1)S(1)}, bf16[512,512]{1,0:T(8,128)(2,1)S(1)}, u32[]{:S(2)}, u32[]{:S(2)}) collective-permute-start(bf16[512,512]{1,0:T(8,128)(2,1)S(1)} %reduce-precision_convert_fusion.1), channel_id=1, source_target_pairs={{0,16},{8,24},{16,0},{24,8},{1,17},{9,25},{17,1},{25,9},{2,18},{10... | collective-permute-start | bytes 1572872 | tf_op jit(solution)/shard_map/ppermute | solution.py:545
  (89 other events, 996.8 us)
Sparse Core Ops, SparseCore 0:
  11.5 49.5 all-gather.3
  62.7 79.5 all-gather.5
  143.9 78.7 all-gather.7
  224.8 75.2 reduce-scatter.4
  315.8 94.5 reduce-scatter.8
  412.7 92.8 reduce-scatter.6
  507.9 97.8 reduce-scatter.10

commit v5 on v4

--- a/solution.py
+++ b/solution.py
@@ -955,6 +955,7 @@
     top = CHUNKS - 1
     d_a, d_b, qs = dyn_step(top)
     scales[top], sq = scales_of(top, qs)
+    mixed_1 = line_scatter(out_step(1))
 
     dz[1], dy[1], yn[1], mtg[1], gg = gate_step(1, sq, d_a, d_b)
     ggs.append(gg)
@@ -965,24 +966,23 @@
     total_1 = line_scatter(dns[1], 0)
     d_a, d_b, qs = dyn_step(0)
     scales[0], sq = scales_of(0, qs)
-    mixed_1 = line_scatter(out_step(1))
     dz[0], dy[0], yn[0], mtg[0], gg = gate_step(0, sq, d_a, d_b)
     ggs.append(gg)
     g_out = weight_grad(c_all, yn)
     g_z = weight_grad([normed] * CHUNKS, dz)
-    dsp[1], mtc_1, acc_bc, *state_carry = states_step(1, total_1, *state_carry)
-    accs_bc.append(acc_bc)
     dxp[0], ddt[0], dbc_0, mtb_0, acc, acc_dt, *carry = back_step(0, dy[0], *carry)
     accs.append(acc)
     accs_dt.append(acc_dt)
-    near[1], far[1] = near_step(total_1, dsp[1], dbc_0)
     out_sum, z_sum = core_sum(*g_out), core_sum(*g_z)
     g_x = weight_grad([normed] * CHUNKS, dxp, after=(out_sum, z_sum))
     x_sum = core_sum(*g_x)
     out_sum, z_sum = pair_sum(out_sum, dbc_0), pair_sum(z_sum, dbc_0)
-    dns[0] = dn_step(dz[0], dxp[0], ddt[0], dbc_0, after=(out_sum, z_sum, near[1]))
+    dns[0] = dn_step(dz[0], dxp[0], ddt[0], dbc_0, after=(out_sum, z_sum))
     total_0 = line_scatter(dns[0], 0)
     x_part = chip_sum(pair_sum(x_sum, total_0))
+    dsp[1], mtc_1, acc_bc, *state_carry = states_step(1, total_1, *state_carry)
+    accs_bc.append(acc_bc)
+    near[1], far[1] = near_step(total_1, dsp[1], dns[0])
     dsp[0], mtc_0, acc_bc, *state_carry = states_step(0, total_0, *state_carry)
     g_x = chip_parts(x_part)
     accs_bc.append(acc_bc)

time: 724 us -> 718 us (level)
  local copies, waits for them, and re-layouts: 89.3 us -> 112 us
  waiting for transfers between devices: 151 us -> 133 us
  other arithmetic: 87.6 us -> 79.8 us
    reduce_scatter x4, waiting for transfers between devices: 26.2 us -> 0.06 us  [line_scatter(): return lax.psum_scatter(v, 'zline', scatter_dimension=axis, tiled=True)]
    ppermute x6, waiting for transfers between devices: 0.02 us -> 20.6 us  [near_step(): lax.ppermute(dsp[:, :4 * cols], 'zline', [(i, (i + k) % groups) for i in...]
    reshape x1 -> x2, local copies, waits for them, and re-layouts: 0.93 us -> 11.4 us  [zero_after(): return (v.reshape(-1)[0].astype(f32) > 1e+38).astype(jnp.int32)]
    unnamed x149 -> x141, local copies, waits for them, and re-layouts: 32.8 us -> 42.4 us
    ppermute x22, waiting for transfers between devices: 47.6 us -> 38.5 us  [cross(): return lax.ppermute(v, 'rows', [(i, i ^ bit) for i in range(nrows)])]
  transfers between devices with their start and end apart: 57 -> 57, of which waited for: 21 -> 25; matrix products, arithmetic and copies ran while one was open for 23% -> 25% of each run, Pallas kernels for 41% -> 43%
where the time goes in v5:
time: 718 us; the launch traced here: 708 us
  Pallas kernels  317 us (44%)
  waiting for transfers between devices  133 us (19%)
  local copies, waits for them, and re-layouts  112 us (16%)
  other arithmetic  79.8 us (11%)
  starting transfers between devices  42.8 us (6%)
  between operations  19.6 us (3%)
    pallas_call x24, Pallas kernels, call(): return lambda *args: fn(*args, *after, *into)  317 us
    ppermute x16, waiting for transfers between devices, swap(): return lax.ppermute(v, 'pair', [(0, 1), (1, 0)])  51.4 us
    unnamed x141, local copies, waits for them, and re-layouts  42.4 us
    ppermute x22, waiting for transfers between devices, cross(): return lax.ppermute(v, 'rows', [(i, i ^ bit) for i in range(nrows)])  38.5 us
    ppermute x6, waiting for transfers between devices, near_step(): lax.ppermute(dsp[:, :4 * cols], 'zline', [(i, (i + k) % groups) for i in...  20.6 us
    ppermute x16, starting transfers between devices, swap(): return lax.ppermute(v, 'pair', [(0, 1), (1, 0)])  17.5 us
  transfers between devices with their start and end apart: 57, of which 25 were waited for; matrix products, arithmetic and copies ran while one was open for 25% of the time, Pallas kernels for 43%

profile of v5, /device:TPU:0, one launch (start us, length us, event | category | flops | bytes accessed | tf_op | source)
XLA Modules:
  0.0 707.9 jit_solution(10092976280044635243)
XLA Ops:
  21.1 5.5 copy.126
  38.2 20.4 %shard_map.271 = (bf16[2048,2048]{1,0:T(8,128)(2,1)}, f32[2048,128]{1,0:T(8,128)}, bf16[2048,512]{1,0:T(8,128)(2,1)}, bf16[2048,512]{1,0:T(8,128)(2,1)}, bf16[20...) custom-call(s32[1]{0:T(128)} %bitcast.refs_0_, bf16[4096,2048]{1,0:T(8,128)(2,1)} %refs_1_.1, ...), custom_call_target="tpu_custom_call" | custom-call | flops 8589934592 | bytes 41943040 | tf_op jit(solution)/shard_map/pallas_call | solution.py:502
  65.5 15.7 %shard_map.272 = (f32[2048,256]{1,0:T(8,128)}, f32[2048,256]{1,0:T(8,128)}, bf16[2048,256]{1,0:T(8,128)(2,1)}, f32[2048,128]{1,0:T(8,128)}, f32[2048,128]{1,0:T(...) custom-call(bf16[2048,2048]{1,0:T(8,128)(2,1)} %get-tuple-element.103.refs_0_.refs_1_.refs_2_, ...), custom_call_target="tpu_custom_call" | custom-call | flops 4294967296 | bytes 18874368 | tf_op jit(solution)/shard_map/pallas_call | solution.py:502
  81.1 26.5 %collective-permute-done.2.refs_8_ = bf16[1024,1024]{1,0:T(8,128)(2,1)} collective-permute-done((bf16[1024,1024]{1,0:T(8,128)(2,1)S(1)}, bf16[1024,1024]{1,0:T(8,128)(2,1)}, u32[]{:S(2)}, u32[]{:S(2)}) %collective-permute-start.2) | collective-permute-done | bytes 2097184 | tf_op jit(solution)/shard_map/ppermute | solution.py:542
  108.4 16.6 %shard_map.273 = (f32[2048,512]{1,0:T(8,128)}, bf16[2048,512]{1,0:T(8,128)(2,1)}, f32[8,128,512]{2,1,0:T(8,128)}, f32[2048,128]{1,0:T(8,128)}, f32[128,512]{1,0:T(8,128)}) custom-call(bf16[2048,512]{1,0:T(8,128)(2,1)} %get-tuple-element.101.refs_0_.refs_10_, bf16[2048,512]{1,0:T(8,128)(2,1)} %get-tuple-element.102.refs_1_.refs_5_, ...), custom_call_target="tpu_custom_call" | custom-call | flops 10737418240 | bytes 20971520 | tf_op jit(solution)/shard_map/pallas_call | solution.py:502
  139.3 10.7 %shard_map.274 = (bf16[2048,512]{1,0:T(8,128)(2,1)}, bf16[2048,512]{1,0:T(8,128)(2,1)}, bf16[2048,512]{1,0:T(8,128)(2,1)}, bf16[2048,512]{1,0:T(8,128)(2,1)}, f32[8,512]{1,0:T(8,128)}) custom-call(bf16[2048,2048]{1,0:T(8,128)(2,1)} %get-tuple-element.103.refs_0_.refs_1_.refs_2_, bf16[2048,1024]{1,0:T(8,128)(2,1)} %pad_maximum_fusion.1.refs_1_.refs_5_, ...), custom_call_target="tpu_custom_call" | custom-call | flops 4294967296 | bytes 14680064 | tf_op jit(solution)/shard_map/pallas_call | solution.py:502
  157.0 9.5 %shard_map.275 = (f32[2048,512]{1,0:T(8,128)}, bf16[2048,512]{1,0:T(8,128)(2,1)}, f32[8,128,512]{2,1,0:T(8,128)}, f32[2048,128]{1,0:T(8,128)}, f32[128,512]{1,0:T(8,128)}) custom-call(bf16[2048,512]{1,0:T(8,128)(2,1)} %get-tuple-element.112.refs_0_.refs_9_, bf16[2048,512]{1,0:T(8,128)(2,1)} %get-tuple-element.113.refs_1_.refs_6_, ...), custom_call_target="tpu_custom_call" | custom-call | flops 5368709120 | bytes 10485760 | tf_op jit(solution)/shard_map/pallas_call | solution.py:502
  171.6 8.6 %shard_map.276.refs_5_ = bf16[1024,2048]{1,0:T(8,128)(2,1)} custom-call(bf16[2048,512]{1,0:T(8,128)(2,1)} %get-tuple-element.109.refs_0_.refs_3_, bf16[2048,512]{1,0:T(8,128)(2,1)} %get-tuple-element.115.refs_1_.refs_10_, bf16[512,2048]{1,0:T(8,128)(2,1)} %refs_2_.3, bf16[512,2048]{1,0:T(8,128)(2,1)} %pad_maximum_fusion.refs_3_, ...), custom_call_target="tpu_custom_call" | custom-call | flops 4294967296 | bytes 10485760 | tf_op jit(solution)/shard_map/pallas_call | solution.py:502
  195.7 10.7 %shard_map.277 = (bf16[2048,512]{1,0:T(8,128)(2,1)}, bf16[2048,512]{1,0:T(8,128)(2,1)}, bf16[2048,512]{1,0:T(8,128)(2,1)}, bf16[2048,512]{1,0:T(8,128)(2,1)}, f32[8,512]{1,0:T(8,128)}) custom-call(bf16[2048,2048]{1,0:T(8,128)(2,1)} %get-tuple-element.103.refs_0_.refs_1_.refs_2_, ...), custom_call_target="tpu_custom_call", output_to_operand_aliasing={{0}: (6, {}), {1}: (7, {}), {2}: (8, {}), {3}: (9, {})} | custom-call | flops 4294967296 | bytes 14680064 | tf_op jit(solution)/shard_map/pallas_call | solution.py:502
  206.5 9.5 %shard_map.278 = (f32[2048,512]{1,0:T(8,128)}, bf16[2048,512]{1,0:T(8,128)(2,1)}, f32[8,128,512]{2,1,0:T(8,128)}, f32[2048,128]{1,0:T(8,128)}, f32[128,512]{1,0:T(8,128)}) custom-call(bf16[2048,512]{1,0:T(8,128)(2,1)} %get-tuple-element.119.refs_0_.refs_11_, ...), custom_call_target="tpu_custom_call", output_to_operand_aliasing={{0}: (9, {}), {1}: (10, {}), {2}: (11, {}), {3}: (12, {})} | custom-call | flops 5368709120 | bytes 10485760 | tf_op jit(solution)/shard_map/pallas_call | solution.py:502
  216.0 6.7 all-gather.8.cloned.1.call-done
  230.0 9.1 %shard_map.279 = (bf16[1024,512]{1,0:T(8,128)(2,1)}, bf16[1024,512]{1,0:T(8,128)(2,1)}, f32[1024,128]{1,0:T(8,128)}) custom-call(bf16[1024,2048]{1,0:T(8,128)(2,1)} %pad_maximum_fusion.2.refs_0_.refs_2_, bf16[512,2048]{1,0:T(8,128)(2,1)} %slice_dynamic-update-slice_fusion.8.refs_1_, bf16[512,2048]{1,0:T(8,128)(2,1)} %copy-done.20, ...), custom_call_target="tpu_custom_call" | custom-call | flops 4294967296 | bytes 12582912 | tf_op jit(solution)/shard_map/pallas_call | solution.py:502
  239.0 8.6 %shard_map.280.refs_9_ = bf16[1024,2048]{1,0:T(8,128)(2,1)} custom-call(bf16[2048,512]{1,0:T(8,128)(2,1)} %get-tuple-element.109.refs_0_.refs_3_, bf16[2048,512]{1,0:T(8,128)(2,1)} %get-tuple-element.125.refs_4_.refs_1_, bf16[512,2048]{1,0:T(8,128)(2,1)} %refs_2_.3, bf16[512,2048]{1,0:T(8,128)(2,1)} %pad_maximum_fusion.refs_3_, ...), custom_call_target="tpu_custom_call" | custom-call | flops 4294967296 | bytes 10485760 | tf_op jit(solution)/shard_map/pallas_call | solution.py:502
  261.6 9.1 %shard_map.281 = (bf16[1024,1024]{1,0:T(8,128)(2,1)}, bf16[1024,1024]{1,0:T(8,128)(2,1)}, bf16[1024,1024]{1,0:T(8,128)(2,1)}, f32[1024,128]{1,0:T(8,128)}, f32[8,1024]{1,0:T(8,128)}) custom-call(f32[1024,128]{1,0:T(8,128)} %pad.48.refs_0_, bf16[1024,512]{1,0:T(8,128)(2,1)} %get-tuple-element.129.refs_1_, bf16[1024,512]{1,0:T(8,128)(2,1)} %get-tuple-element.130.refs_2_, ...), custom_call_target="tpu_custom_call" | custom-call | flops 2097152000 | bytes 20971520 | tf_op jit(solution)/shard_map/pallas_call | solution.py:502
  272.8 32.4 %shard_map.282 = (bf16[1024,1024]{1,0:T(8,128)(2,1)}, bf16[1024,128]{1,0:T(8,128)(2,1)}, bf16[1024,256]{1,0:T(8,128)(2,1)}, f32[1024,128]{1,0:T(8,128)}, f32[2,4...) custom-call(bf16[1024,1024]{1,0:T(8,128)(2,1)} %get-tuple-element.13, ...), custom_call_target="tpu_custom_call" | custom-call | flops 42949672960 | bytes 41943040 | tf_op jit(solution)/shard_map/pallas_call | solution.py:502
  305.2 15.6 %shard_map.283.refs_5_ = bf16[4096,640]{1,0:T(8,128)(2,1)} custom-call(bf16[1024,1024]{1,0:T(8,128)(2,1)} %get-tuple-element.133.refs_0_.refs_4_, bf16[1024,1024]{1,0:T(8,128)(2,1)} %get-tuple-element.143.refs_1_.refs_4_, bf16[1024,128]{1,0:T(8,128)(2,1)} %get-tuple-element.144.refs_2_.refs_5_, bf16[1024,256]{1,0:T(8,128)(2,1)} %get-tuple-element.145.refs_3_, ...), custom_call_target="tpu_custom_call" | custom-call | flops 8589934592 | bytes 16777216 | tf_op jit(solution)/shard_map/pallas_call | solution.py:502
  320.8 9.0 %shard_map.284 = (bf16[1024,512]{1,0:T(8,128)(2,1)}, bf16[1024,512]{1,0:T(8,128)(2,1)}, f32[1024,128]{1,0:T(8,128)}) custom-call(bf16[1024,2048]{1,0:T(8,128)(2,1)} %pad_maximum_fusion.3.refs_0_.refs_1_, bf16[512,2048]{1,0:T(8,128)(2,1)} %slice_dynamic-update-slice_fusion.8.refs_1_, bf16[512,2048]{1,0:T(8,128)(2,1)} %copy-done.20, ...), custom_call_target="tpu_custom_call" | custom-call | flops 4294967296 | bytes 12582912 | tf_op jit(solution)/shard_map/pallas_call | solution.py:502
  341.3 8.8 %shard_map.285 = (bf16[1024,1024]{1,0:T(8,128)(2,1)}, bf16[1024,1024]{1,0:T(8,128)(2,1)}, bf16[1024,1024]{1,0:T(8,128)(2,1)}, f32[1024,128]{1,0:T(8,128)}, f32[8,1024]{1,0:T(8,128)}) custom-call(f32[1024,128]{1,0:T(8,128)} %pad.49.refs_0_, bf16[1024,512]{1,0:T(8,128)(2,1)} %get-tuple-element.149.refs_1_, bf16[1024,512]{1,0:T(8,128)(2,1)} %get-tuple-element.150.refs_2_, ...), custom_call_target="tpu_custom_call" | custom-call | flops 2097152000 | bytes 20971520 | tf_op jit(solution)/shard_map/pallas_call | solution.py:502
  350.1 15.5 %shard_map.286 = (f32[1024,1024]{1,0:T(8,128)}, f32[1024,1024]{1,0:T(8,128)}) custom-call(s32[1]{0:T(128)} %bitcast.30.refs_0_, bf16[1024,2048]{1,0:T(8,128)(2,1)} %pad_maximum_fusion.3.refs_0_.refs_1_, bf16[1024,2048]{1,0:T(8,128)(2,1)} %pad_maximum_fusion.2.refs_0_.refs_2_, bf16[1024,1024]{1,0:T(8,128)(2,1)} %get-tuple-element.155.refs_3_, ...), custom_call_target="tpu_custom_call" | custom-call | flops 65536 | bytes 65536 | tf_op jit(solution)/shard_map/pallas_call | solution.py:502
  365.6 15.7 %shard_map.287 = (f32[1024,1024]{1,0:T(8,128)}, f32[1024,1024]{1,0:T(8,128)}) custom-call(s32[1]{0:T(128)} %bitcast.30.refs_0_, bf16[2048,2048]{1,0:T(8,128)(2,1)} %get-tuple-element.103.refs_0_.refs_1_.refs_2_, bf16[2048,2048]{1,0:T(8,128)(2,1)} %get-tuple-element.103.refs_0_.refs_1_.refs_2_, bf16[1024,1024]{1,0:T(8,128)(2,1)} %get-tuple-element.151.refs_3_.refs_0_, ...), custom_call_target="tpu_custom_call" | custom-call | flops 65536 | bytes 65536 | tf_op jit(solution)/shard_map/pallas_call | solution.py:502
  393.8 32.4 %shard_map.288 = (bf16[1024,1024]{1,0:T(8,128)(2,1)}, bf16[1024,128]{1,0:T(8,128)(2,1)}, bf16[1024,256]{1,0:T(8,128)(2,1)}, f32[1024,128]{1,0:T(8,128)}, f32[2,4...) custom-call(bf16[1024,1024]{1,0:T(8,128)(2,1)} %get-tuple-element.15, ...), custom_call_target="tpu_custom_call" | custom-call | flops 42949672960 | bytes 41943040 | tf_op jit(solution)/shard_map/pallas_call | solution.py:502
  428.8 15.6 %shard_map.289 = (f32[1024,1024]{1,0:T(8,128)}, f32[1024,1024]{1,0:T(8,128)}) custom-call(s32[1]{0:T(128)} %bitcast.30.refs_0_, bf16[2048,2048]{1,0:T(8,128)(2,1)} %get-tuple-element.103.refs_0_.refs_1_.refs_2_, bf16[2048,2048]{1,0:T(8,128)(2,1)} %get-tuple-element.103.refs_0_.refs_1_.refs_2_, bf16[1024,1024]{1,0:T(8,128)(2,1)} %get-tuple-element.160.refs_3_.refs_1_, ...), custom_call_target="tpu_custom_call" | custom-call | flops 65536 | bytes 65536 | tf_op jit(solution)/shard_map/pallas_call | solution.py:502
  450.3 16.0 %shard_map.290.refs_7_ = bf16[4096,640]{1,0:T(8,128)(2,1)} custom-call(bf16[1024,1024]{1,0:T(8,128)(2,1)} %get-tuple-element.151.refs_3_.refs_0_, bf16[1024,1024]{1,0:T(8,128)(2,1)} %get-tuple-element.160.refs_3_.refs_1_, bf16[1024,128]{1,0:T(8,128)(2,1)} %get-tuple-element.161.refs_2_.refs_4_, bf16[1024,256]{1,0:T(8,128)(2,1)} %get-tuple-element.162.refs_3_, ...), custom_call_target="tpu_custom_call" | custom-call | flops 8589934592 | bytes 16777216 | tf_op jit(solution)/shard_map/pallas_call | solution.py:502
  494.0 6.7 collective-permute-done.43
  506.6 9.2 %collective-permute-done.30 = bf16[512,512]{1,0:T(8,128)(2,1)} collective-permute-done((bf16[512,512]{1,0:T(8,128)(2,1)S(1)}, bf16[512,512]{1,0:T(8,128)(2,1)}, u32[]{:S(2)}, u32[]{:S(2)}) %collective-permute-start.30) | collective-permute-done | bytes 524320 | tf_op jit(solution)/shard_map/ppermute | solution.py:545
  518.6 8.5 %collective-permute-done.48 = bf16[512,512]{1,0:T(8,128)(2,1)} collective-permute-done((bf16[512,512]{1,0:T(8,128)(2,1)S(1)}, bf16[512,512]{1,0:T(8,128)(2,1)}, u32[]{:S(2)}, u32[]{:S(2)}) %collective-permute-start.48) | collective-permute-done | bytes 524320 | tf_op jit(solution)/shard_map/ppermute | solution.py:545
  534.5 9.5 %reshape.248 = bf16[2621440]{0:T(1024)(128)(2,1)} reshape(bf16[4096,640]{1,0:T(8,128)(2,1)} %shard_map.290.refs_7_) | data formatting | bytes 10485760 | tf_op jit(solution)/shard_map/reshape | solution.py:558
  580.4 15.4 %collective-permute-done.21 = bf16[1024,64]{1,0:T(8,128)(2,1)S(1)} collective-permute-done((bf16[1024,64]{1,0:T(8,128)(2,1)}, bf16[1024,64]{1,0:T(8,128)(2,1)S(1)}, u32[]{:S(2)}, u32[]{:S(2)}) %collective-permute-start.21) | collective-permute-done | bytes 131104 | tf_op jit(solution)/shard_map/ppermute | solution.py:875
  619.1 10.0 %shard_map.293.refs_5_ = f32[256,2048]{1,0:T(8,128)} custom-call(s32[1]{0:T(128)} %bitcast.refs_0_, bf16[2048,2048]{1,0:T(8,128)(2,1)} %get-tuple-element.103.refs_0_.refs_1_.refs_2_, bf16[1024,128]{1,0:T(8,128)(2,1)} %get-tuple-element.171.refs_2_, bf16[1024,128]{1,0:T(8,128)(2,1)} %get-tuple-element.172.refs_3_, ...), custom_call_target="tpu_custom_call" | custom-call | flops 65536 | bytes 65536 | tf_op jit(solution)/shard_map/pallas_call | solution.py:502
  646.0 10.0 %collective-permute-done.38 = bf16[40,2048]{1,0:T(8,128)(2,1)S(1)} collective-permute-done((bf16[40,2048]{1,0:T(8,128)(2,1)}, bf16[40,2048]{1,0:T(8,128)(2,1)S(1)}, u32[]{:S(2)}, u32[]{:S(2)}) %collective-permute-start.38) | collective-permute-done | bytes 163872 | tf_op jit(solution)/shard_map/ppermute | solution.py:542
  675.3 5.9 collective-permute-done.36
  691.3 9.5 %shard_map.294 = f32[16384,128]{1,0:T(8,128)} custom-call(s32[1]{0:T(128)} %bitcast.30.refs_0_, bf16[1024,512]{1,0:T(8,128)(2,1)} %pad_maximum_fusion.8.refs_1_, bf16[1024,512]{1,0:T(8,128)(2,1)} %copy-done.23, bf16[1024,512]{1,0:T(8,128)(2,1)} %copy-done.19, bf16[1024,512]{1,0:T(8,128)(2,1)} %copy-done.24, f32[256,2048]{1,0:T(8,128)} %shard_map.293.refs_5_), custom_call_target="tpu_custom_call" | custom-call | bytes 25165824 | tf_op jit(solution)/shard_map/pallas_call | solution.py:502
  (432 shorter events, 275.7 us)
Async XLA Ops:
  7.2 53.9 %all-gather.4.cloned.1.call-start = ((), (), s32[]{:S(2)}) async-start(), calls=%async_computation.4 | async-start | bytes 1253376 | tf_op jit(solution)/shard_map/all_gather | solution.py:598
  11.4 204.6 %all-gather.6.cloned.1.call-start = ((), (), s32[]{:S(2)}) async-start(), calls=%async_computation.6 | async-start | bytes 5242880 | tf_op jit(solution)/shard_map/all_gather | solution.py:604
  14.7 208.0 %all-gather.8.cloned.1.call-start = ((), (), s32[]{:S(2)}) async-start(), calls=%async_computation.7 | async-start | bytes 5242880 | tf_op jit(solution)/shard_map/all_gather | solution.py:714
  19.1 16.7 %collective-permute-start.1 = (bf16[8,2048]{0,1:T(8,128)(2,1)}, bf16[8,2048]{0,1:T(8,128)(2,1)}, u32[]{:S(2)}, u32[]{:S(2)}) collective-permute-start(bf16[8,2048]{0,1:T(8,128)(2,1)} %bitcast.12), channel_id=1, source_target_pairs={{0,1},{1,0},{2,3},{3,2},{4,5},{5,4},{6,7},{7,6},{8,9},{9,8},{10,11... | collective-permute-start | bytes 98312 | tf_op jit(solution)/shard_map/ppermute | solution.py:542
  19.1 107.9 %collective-permute-start.6 = (bf16[2048,256]{1,0:T(8,128)(2,1)}, bf16[2048,256]{1,0:T(8,128)(2,1)}, u32[]{:S(2)}, u32[]{:S(2)}) collective-permute-start(bf16[2048,256]{1,0:T(8,128)(2,1)} %get-tuple-element.272), channel_id=1, source_target_pairs={{0,1},{1,0},{2,3},{3,2},{4,5},{5,4},{6,7},{7,6},{8,9},{9,8},{10,11... | collective-permute-start | bytes 3145736 | tf_op jit(solution)/shard_map/ppermute | solution.py:542
  28.4 79.3 %collective-permute-start.2 = (bf16[1024,1024]{1,0:T(8,128)(2,1)S(1)}, bf16[1024,1024]{1,0:T(8,128)(2,1)}, u32[]{:S(2)}, u32[]{:S(2)}) collective-permute-start(bf16[1024,1024]{1,0:T(8,128)(2,1)S(1)} %constant_dynamic-slice_fusion.15), channel_id=1, source_target_pairs={{0,1},{1,0},{2,3},{3,2},{4,5},{5,4},{6,7},{7,6},{8,9},{9,8},{10,11... | collective-permute-start | bytes 6291464 | tf_op jit(solution)/shard_map/ppermute | solution.py:542
  129.3 175.9 %reduce-scatter.5.cloned.1.call-start = ((), (), s32[]{:S(2)}) async-start(), calls=%async_computation.5 | async-start | bytes 5242880 | tf_op jit(solution)/shard_map/reduce_scatter | solution.py:658
  131.1 25.7 %collective-permute-start.4 = (bf16[256,2048]{1,0:T(8,128)(2,1)}, bf16[256,2048]{1,0:T(8,128)(2,1)S(1)}, u32[]{:S(2)}, u32[]{:S(2)}) collective-permute-start(bf16[256,2048]{1,0:T(8,128)(2,1)} %constant_dynamic-slice_fusion.14), channel_id=1, source_target_pairs={{0,1},{1,0},{2,3},{3,2},{4,5},{5,4},{6,7},{7,6},{8,9},{9,8},{10,11... | collective-permute-start | bytes 3145736 | tf_op jit(solution)/shard_map/ppermute | solution.py:542
  180.2 349.0 %reduce-scatter.7.cloned.1.call-start = ((), (), s32[]{:S(2)}) async-start(), calls=%async_computation.8 | async-start | bytes 5242880 | tf_op jit(solution)/shard_map/reduce_scatter | solution.py:658
  247.7 318.8 %reduce-scatter.11.cloned.1.call-start = ((), (), s32[]{:S(2)}) async-start(), calls=%async_computation.10 | async-start | bytes 6553600 | tf_op jit(solution)/shard_map/reduce_scatter | solution.py:658
  331.6 266.8 %reduce-scatter.9.cloned.1.call-start = ((), (), s32[]{:S(2)}) async-start(), calls=%async_computation.9 | async-start | bytes 6553600 | tf_op jit(solution)/shard_map/reduce_scatter | solution.py:658
  365.6 16.2 %collective-permute-start.13 = (f32[1024,1024]{1,0:T(8,128)}, f32[1024,1024]{1,0:T(8,128)}, u32[]{:S(2)}, u32[]{:S(2)}) collective-permute-start(f32[1024,1024]{1,0:T(8,128)} %get-tuple-element.158.refs_5_), channel_id=1, source_target_pairs={{0,8},{8,0},{16,24},{24,16},{1,9},{9,1},{17,25},{25,17},{2,10},{10... | collective-permute-start | bytes 12582920 | tf_op jit(solution)/shard_map/ppermute | solution.py:545
  385.3 59.1 %collective-permute-start.14 = (bf16[1024,512]{1,0:T(8,128)(2,1)S(1)}, bf16[1024,512]{1,0:T(8,128)(2,1)S(1)}, u32[]{:S(2)}, u32[]{:S(2)}) collective-permute-start(bf16[1024,512]{1,0:T(8,128)(2,1)S(1)} %slice.621), channel_id=1, source_target_pairs={{0,1},{1,0},{2,3},{3,2},{4,5},{5,4},{6,7},{7,6},{8,9},{9,8},{10,11... | collective-permute-start | bytes 3145736 | tf_op jit(solution)/shard_map/ppermute | solution.py:542
  392.3 53.9 %collective-permute-start.16 = (bf16[1024,512]{1,0:T(8,128)(2,1)S(1)}, bf16[1024,512]{1,0:T(8,128)(2,1)}, u32[]{:S(2)}, u32[]{:S(2)}) collective-permute-start(bf16[1024,512]{1,0:T(8,128)(2,1)S(1)} %slice.620), channel_id=1, source_target_pairs={{0,1},{1,0},{2,3},{3,2},{4,5},{5,4},{6,7},{7,6},{8,9},{9,8},{10,11... | collective-permute-start | bytes 3145736 | tf_op jit(solution)/shard_map/ppermute | solution.py:542
  487.1 15.3 %collective-permute-start.47 = (bf16[512,512]{1,0:T(8,128)(2,1)}, bf16[512,512]{1,0:T(8,128)(2,1)}, u32[]{:S(2)}, u32[]{:S(2)}) collective-permute-start(bf16[512,512]{1,0:T(8,128)(2,1)} %dynamic-slice_convert_fusion.2), channel_id=1, source_target_pairs={{0,16},{8,24},{16,0},{24,8},{1,17},{9,25},{17,1},{25,9},{2,18},{10... | collective-permute-start | bytes 1572872 | tf_op jit(solution)/shard_map/ppermute | solution.py:545
  503.6 23.5 %collective-permute-start.48 = (bf16[512,512]{1,0:T(8,128)(2,1)S(1)}, bf16[512,512]{1,0:T(8,128)(2,1)}, u32[]{:S(2)}, u32[]{:S(2)}) collective-permute-start(bf16[512,512]{1,0:T(8,128)(2,1)S(1)} %reduce-precision_convert_fusion), channel_id=1, source_target_pairs={{0,16},{8,24},{16,0},{24,8},{1,17},{9,25},{17,1},{25,9},{2,18},{10... | collective-permute-start | bytes 1572872 | tf_op jit(solution)/shard_map/ppermute | solution.py:545
  504.7 45.1 %collective-permute-start.33 = (f32[1024,1024]{1,0:T(8,128)}, f32[1024,1024]{1,0:T(8,128)}, u32[]{:S(2)}, u32[]{:S(2)}) collective-permute-start(f32[1024,1024]{1,0:T(8,128)} %get-tuple-element.166.refs_9_), channel_id=1, source_target_pairs={{0,8},{8,0},{16,24},{24,16},{1,9},{9,1},{17,25},{25,17},{2,10},{10... | collective-permute-start | bytes 12582920 | tf_op jit(solution)/shard_map/ppermute | solution.py:545
  517.0 28.8 %collective-permute-start.31 = (bf16[512,512]{1,0:T(8,128)(2,1)S(1)}, bf16[512,512]{1,0:T(8,128)(2,1)}, u32[]{:S(2)}, u32[]{:S(2)}) collective-permute-start(bf16[512,512]{1,0:T(8,128)(2,1)S(1)} %reduce-precision_convert_fusion.2), channel_id=1, source_target_pairs={{0,16},{8,24},{16,0},{24,8},{1,17},{9,25},{17,1},{25,9},{2,18},{10... | collective-permute-start | bytes 1572872 | tf_op jit(solution)/shard_map/ppermute | solution.py:545
  529.2 18.8 %collective-permute-start.49 = (bf16[1024,512]{1,0:T(8,128)(2,1)}, bf16[1024,512]{1,0:T(8,128)(2,1)}, u32[]{:S(2)}, u32[]{:S(2)}) collective-permute-start(bf16[1024,512]{1,0:T(8,128)(2,1)} %pad_maximum_fusion.10), channel_id=1, source_target_pairs={{0,8},{8,0},{16,24},{24,16},{1,9},{9,1},{17,25},{25,17},{2,10},{10... | collective-permute-start | bytes 3145736 | tf_op jit(solution)/shard_map/ppermute | solution.py:545
  534.0 137.0 %collective-permute-start.11 = (bf16[2048,256]{1,0:T(8,128)(2,1)}, bf16[2048,256]{1,0:T(8,128)(2,1)}, u32[]{:S(2)}, u32[]{:S(2)}) collective-permute-start(bf16[2048,256]{1,0:T(8,128)(2,1)} %dynamic-slice_convert_fusion), channel_id=1, source_target_pairs={{0,1},{1,0},{2,3},{3,2},{4,5},{5,4},{6,7},{7,6},{8,9},{9,8},{10,11... | collective-permute-start | bytes 3145736 | tf_op jit(solution)/shard_map/ppermute | solution.py:542
  557.1 55.1 %collective-permute-start.34 = (bf16[1024,512]{1,0:T(8,128)(2,1)S(1)}, bf16[1024,512]{1,0:T(8,128)(2,1)}, u32[]{:S(2)}, u32[]{:S(2)}) collective-permute-start(bf16[1024,512]{1,0:T(8,128)(2,1)S(1)} %slice.619), channel_id=1, source_target_pairs={{0,1},{1,0},{2,3},{3,2},{4,5},{5,4},{6,7},{7,6},{8,9},{9,8},{10,11... | collective-permute-start | bytes 3145736 | tf_op jit(solution)/shard_map/ppermute | solution.py:542
  573.4 22.5 %collective-permute-start.21 = (bf16[1024,64]{1,0:T(8,128)(2,1)}, bf16[1024,64]{1,0:T(8,128)(2,1)S(1)}, u32[]{:S(2)}, u32[]{:S(2)}) collective-permute-start(bf16[1024,64]{1,0:T(8,128)(2,1)} %bitcast.129), channel_id=1, source_target_pairs={{0,4},{2,6},{4,0},{6,2},{1,5},{3,7},{5,1},{7,3},{8,12},{10,14},{12... | collective-permute-start | bytes 393224 | tf_op jit(solution)/shard_map/ppermute | solution.py:875
  573.4 22.5 %collective-permute-start.20 = (bf16[1024,64]{1,0:T(8,128)(2,1)}, bf16[1024,64]{1,0:T(8,128)(2,1)S(1)}, u32[]{:S(2)}, u32[]{:S(2)}) collective-permute-start(bf16[1024,64]{1,0:T(8,128)(2,1)} %bitcast.130), channel_id=1, source_target_pairs={{0,2},{2,4},{4,6},{6,0},{1,3},{3,5},{5,7},{7,1},{8,10},{10,12},{12... | collective-permute-start | bytes 393224 | tf_op jit(solution)/shard_map/ppermute | solution.py:875
  602.6 38.5 %collective-permute-start.19 = (bf16[1024,64]{1,0:T(8,128)(2,1)}, bf16[1024,64]{1,0:T(8,128)(2,1)}, u32[]{:S(2)}, u32[]{:S(2)}) collective-permute-start(bf16[1024,64]{1,0:T(8,128)(2,1)} %bitcast.124), channel_id=1, source_target_pairs={{0,6},{2,0},{4,2},{6,4},{1,7},{3,1},{5,3},{7,5},{8,14},{10,8},{12,... | collective-permute-start | bytes 393224 | tf_op jit(solution)/shard_map/ppermute | solution.py:875
  602.6 39.4 %collective-permute-start.18 = (bf16[1024,64]{1,0:T(8,128)(2,1)}, bf16[1024,64]{1,0:T(8,128)(2,1)}, u32[]{:S(2)}, u32[]{:S(2)}) collective-permute-start(bf16[1024,64]{1,0:T(8,128)(2,1)} %bitcast.125), channel_id=1, source_target_pairs={{0,4},{2,6},{4,0},{6,2},{1,5},{3,7},{5,1},{7,3},{8,12},{10,14},{12... | collective-permute-start | bytes 393224 | tf_op jit(solution)/shard_map/ppermute | solution.py:875
  605.5 37.1 %collective-permute-start.17 = (bf16[1024,64]{1,0:T(8,128)(2,1)}, bf16[1024,64]{1,0:T(8,128)(2,1)}, u32[]{:S(2)}, u32[]{:S(2)}) collective-permute-start(bf16[1024,64]{1,0:T(8,128)(2,1)} %bitcast.126), channel_id=1, source_target_pairs={{0,2},{2,4},{4,6},{6,0},{1,3},{3,5},{5,7},{7,1},{8,10},{10,12},{12... | collective-permute-start | bytes 393224 | tf_op jit(solution)/shard_map/ppermute | solution.py:875
  640.0 20.8 %collective-permute-start.24 = (bf16[1024,256]{1,0:T(8,128)(2,1)}, bf16[1024,256]{1,0:T(8,128)(2,1)S(1)}, u32[]{:S(2)}, u32[]{:S(2)}) collective-permute-start(bf16[1024,256]{1,0:T(8,128)(2,1)} %dynamic-slice_convert_fusion.5), channel_id=1, source_target_pairs={{0,1},{1,0},{2,3},{3,2},{4,5},{5,4},{6,7},{7,6},{8,9},{9,8},{10,11... | collective-permute-start | bytes 1572872 | tf_op jit(solution)/shard_map/ppermute | solution.py:542
  642.0 17.9 %collective-permute-start.35 = (bf16[512,512]{1,0:T(8,128)(2,1)}, bf16[512,512]{1,0:T(8,128)(2,1)S(1)}, u32[]{:S(2)}, u32[]{:S(2)}) collective-permute-start(bf16[512,512]{1,0:T(8,128)(2,1)} %dynamic-slice_convert_fusion.3), channel_id=1, source_target_pairs={{0,16},{8,24},{16,0},{24,8},{1,17},{9,25},{17,1},{25,9},{2,18},{10... | collective-permute-start | bytes 1572872 | tf_op jit(solution)/shard_map/ppermute | solution.py:545
  642.6 15.5 %collective-permute-start.27 = (f32[2048]{0:T(1024)S(1)}, f32[2048]{0:T(1024)S(1)}, u32[]{:S(2)}, u32[]{:S(2)}) collective-permute-start(f32[2048]{0:T(1024)S(1)} %add.377), channel_id=1, source_target_pairs={{0,1},{1,0},{2,3},{3,2},{4,5},{5,4},{6,7},{7,6},{8,9},{9,8},{10,11... | collective-permute-start | bytes 24584 | tf_op jit(solution)/shard_map/ppermute | solution.py:542
  659.8 29.6 %collective-permute-start.32 = (bf16[1024,512]{1,0:T(8,128)(2,1)S(1)}, bf16[1024,512]{1,0:T(8,128)(2,1)S(1)}, u32[]{:S(2)}, u32[]{:S(2)}) collective-permute-start(bf16[1024,512]{1,0:T(8,128)(2,1)S(1)} %copy-done.18), channel_id=1, source_target_pairs={{0,8},{8,0},{16,24},{24,16},{1,9},{9,1},{17,25},{25,17},{2,10},{10... | collective-permute-start | bytes 3145736 | tf_op jit(solution)/shard_map/ppermute | solution.py:545
  660.0 28.0 %collective-permute-start.40 = (f32[40,2048]{1,0:T(8,128)S(1)}, f32[40,2048]{1,0:T(8,128)S(1)}, u32[]{:S(2)}, u32[]{:S(2)}) collective-permute-start(f32[40,2048]{1,0:T(8,128)S(1)} %add.391), channel_id=1, source_target_pairs={{0,16},{8,24},{16,0},{24,8},{1,17},{9,25},{17,1},{25,9},{2,18},{10... | collective-permute-start | bytes 983048 | tf_op jit(solution)/shard_map/ppermute | solution.py:545
  660.8 20.5 %collective-permute-start.36 = (bf16[512,512]{1,0:T(8,128)(2,1)S(1)}, bf16[512,512]{1,0:T(8,128)(2,1)S(1)}, u32[]{:S(2)}, u32[]{:S(2)}) collective-permute-start(bf16[512,512]{1,0:T(8,128)(2,1)S(1)} %reduce-precision_convert_fusion.1), channel_id=1, source_target_pairs={{0,16},{8,24},{16,0},{24,8},{1,17},{9,25},{17,1},{25,9},{2,18},{10... | collective-permute-start | bytes 1572872 | tf_op jit(solution)/shard_map/ppermute | solution.py:545
  (85 other events, 625.4 us)
Sparse Core Ops, SparseCore 0:
  11.5 49.5 all-gather.3
  62.7 79.5 all-gather.5
  143.9 78.7 all-gather.7
  224.8 75.2 reduce-scatter.4
  302.4 77.6 reduce-scatter.6
  382.2 94.2 reduce-scatter.10
  478.8 94.2 reduce-scatter.8
